TPU v7x, 128 devices: a whole 4x4x4 slice. The times are simulated.
128 devices in a mesh: dp: 32 (over y, x, core), mp: 4 (over z).
Axes of the slice: x: 4, y: 4, z: 4, core: 2. Of those that a mesh axis runs over, the one named last changes fastest.
Arguments:
- feats: bfloat16 [16384, 768], P(('dp', 'mp')), may hold values from -6 to 6
- edge_owner: int32 [262144, 1], P(('dp', 'mp')), may hold values from 0 to 127; in each aligned block of 2048 rows (0 to 2047, 2048 to 4095, ...) at most 32 rows name the same one
- edge_row: int32 [262144], P(('dp', 'mp')), may hold values from 0 to 2047
- counts: int32 [16384], P(('dp', 'mp')), may hold values from 12 to 16
- table: float32 [262144, 128], P(('dp', 'mp')), may hold values from -6 to 6
- moment1: float32 [262144, 128], P(('dp', 'mp')), may hold values from -3 to 3
- moment2: float32 [262144, 128], P(('dp', 'mp')), may hold values from 0.001 to 0.1
- w_self: bfloat16 [768, 1024], replicated, may hold values from -0.21875 to 0.21875
- w_rel: bfloat16 [128, 1024], replicated, may hold values from -0.5 to 0.5
- cotangent: float32 [16384, 1024], P(('dp', 'mp')), may hold values from -6 to 6
- next_owner: int32 [16384, 1], P(('dp', 'mp')), may hold values from 0 to 127; in each aligned block of 128 rows (0 to 127, 128 to 255, ...) at most 2 rows name the same one
- next_row: int32 [16384], P(('dp', 'mp')), may hold values from 0 to 1023
- paper_table: bfloat16 [131072, 768], P(('dp', 'mp')), may hold values from -6 to 6
Outputs:
- new_table: float32 [262144, 128], P(('dp', 'mp'))
- new_moment1: float32 [262144, 128], P(('dp', 'mp'))
- new_moment2: float32 [262144, 128], P(('dp', 'mp'))
- grad_self: float32 [768, 1024], replicated
- grad_rel: float32 [128, 1024], replicated
- next_feats: bfloat16 [16384, 768], P(('dp', 'mp'))
Inputs may be any that keep to these rules, and one draw needn't show every extreme that they name: `edge_owner`: in the author slots of one device at most 32 name one owner, a bound that some block reaches. `next_owner`: in the next seeds of one device at most 2 name one owner, a bound that some block reaches.
All inputs are finite; a program needn't handle non-finite values.
Results may differ from a plain program's by a relative error of at most 0.0049.
Values may be sent and summed in bfloat16 or wider, within the bound.
No kernel may reach another device: no remote copies, remote signals or barrier semaphores. Data moves between devices by JAX's collectives and lax.ppermute only.
A program may use at most 64 MiB of HBM per device.

v0:
```python
import jax
import jax.numpy as jnp
from jax import lax
from jax.sharding import PartitionSpec as P


def place_slots(owner, capacity, count_dev):
    owner_col = owner[:, 0]
    onehot = (owner_col[:, None] == jnp.arange(count_dev, dtype=jnp.int32)[None, :]).astype(
        jnp.int32
    )
    before = jnp.cumsum(onehot, axis=0) - onehot
    slot = jnp.sum(before * onehot, axis=1)
    return owner_col * capacity + slot


def shards(
    feats,
    edge_owner,
    edge_row,
    counts,
    table,
    moment1,
    moment2,
    w_self,
    w_rel,
    cotangent,
    next_owner,
    next_row,
    paper_table,
):
    n_dp = lax.axis_size("dp")
    n_mp = lax.axis_size("mp")
    devs = n_dp * n_mp
    seeds = counts.shape[0]
    slots_per = edge_row.shape[0] // seeds
    emb = table.shape[1]
    width = paper_table.shape[1]
    capacity = max(2, 2 * edge_row.shape[0] // devs)
    fcapacity = max(2, 2 * seeds // devs)
    live = jnp.arange(slots_per, dtype=jnp.int32)[None, :] < counts[:, None]
    count_f = counts.astype(jnp.float32)
    where_to = place_slots(edge_owner, capacity, devs)
    asked = (
        jnp.full((devs * capacity,), -1, jnp.int32)
        .at[where_to]
        .set(jnp.where(live.reshape(-1), edge_row, -1))
    )
    wanted_part = lax.all_to_all(
        asked.reshape(devs, capacity), ("dp", "mp"), split_axis=0, concat_axis=0, tiled=True
    )
    wanted = wanted_part
    answer = lax.all_to_all(
        jnp.take(table, jnp.maximum(wanted_part, 0), axis=0),
        ("dp", "mp"),
        split_axis=0,
        concat_axis=0,
        tiled=True,
    )
    wanted = wanted.reshape(devs * capacity)
    fetched = answer.reshape(devs * capacity, emb)
    edge_vals = jnp.take(fetched, where_to, axis=0).reshape(seeds, slots_per, emb)
    agg = (
        jnp.sum(jnp.where(live[:, :, None], edge_vals, jnp.float32(0.0)), axis=1) / count_f[:, None]
    )
    agg_b = agg.astype(jnp.bfloat16)
    pre = jnp.dot(feats, w_self, preferred_element_type=jnp.float32) + jnp.dot(
        agg_b, w_rel, preferred_element_type=jnp.float32
    )
    sig = jax.nn.sigmoid(pre)
    dpre = (cotangent * sig * (1.0 + pre * (1.0 - sig))).astype(jnp.bfloat16)
    part_self = lax.dot_general(
        feats, dpre, (((0,), (0,)), ((), ())), preferred_element_type=jnp.float32
    )
    part_rel = lax.dot_general(
        agg_b, dpre, (((0,), (0,)), ((), ())), preferred_element_type=jnp.float32
    )
    dagg = lax.dot_general(
        dpre, w_rel, (((1,), (1,)), ((), ())), preferred_element_type=jnp.float32
    )
    slot_grad = jnp.where(
        live[:, :, None], (dagg / count_f[:, None])[:, None, :], jnp.float32(0.0)
    ).reshape(seeds * slots_per, emb)
    outgoing = jnp.zeros((devs * capacity, emb), jnp.float32).at[where_to].set(slot_grad)
    arrived = lax.all_to_all(
        outgoing.reshape(devs, capacity, emb).astype(jnp.bfloat16),
        ("dp", "mp"),
        split_axis=0,
        concat_axis=0,
        tiled=True,
    ).astype(jnp.float32)
    arrived = arrived.reshape(devs * capacity, emb)
    valid = wanted >= 0
    safe_rows = jnp.maximum(wanted, 0)
    row_grad = (
        jnp.zeros(table.shape, jnp.float32)
        .at[safe_rows]
        .add(jnp.where(valid[:, None], arrived, jnp.float32(0.0)))
    )
    hits = jnp.zeros((table.shape[0],), jnp.int32).at[safe_rows].add(valid.astype(jnp.int32))
    touched = (hits > 0)[:, None]
    m_new = 0.9 * moment1 + 0.1 * row_grad
    v_new = 0.999 * moment2 + 0.001 * row_grad * row_grad
    update = 0.05 * (m_new / (1.0 - 0.9**10)) / (jnp.sqrt(v_new / (1.0 - 0.999**10)) + 1e-08)
    new_table = jnp.where(touched, table - update, table)
    new_moment1 = jnp.where(touched, m_new, moment1)
    new_moment2 = jnp.where(touched, v_new, moment2)
    grad_self, grad_rel = lax.psum((part_self, part_rel), ("dp", "mp"))
    paper_place = place_slots(next_owner, fcapacity, devs)
    paper_asked = jnp.full((devs * fcapacity,), -1, jnp.int32).at[paper_place].set(next_row)
    paper_rows = lax.all_to_all(
        jnp.take(
            paper_table,
            jnp.maximum(
                lax.all_to_all(
                    paper_asked.reshape(devs, fcapacity),
                    ("dp", "mp"),
                    split_axis=0,
                    concat_axis=0,
                    tiled=True,
                ),
                0,
            ),
            axis=0,
        ),
        ("dp", "mp"),
        split_axis=0,
        concat_axis=0,
        tiled=True,
    )
    next_feats = jnp.take(paper_rows.reshape(devs * fcapacity, width), paper_place, axis=0)
    return (new_table, new_moment1, new_moment2, grad_self, grad_rel, next_feats)


def solution(mesh):
    in_specs = (
        P(("dp", "mp"), None),
        P(("dp", "mp"), None),
        P(("dp", "mp")),
        P(("dp", "mp")),
        P(("dp", "mp"), None),
        P(("dp", "mp"), None),
        P(("dp", "mp"), None),
        P(),
        P(),
        P(("dp", "mp"), None),
        P(("dp", "mp"), None),
        P(("dp", "mp")),
        P(("dp", "mp"), None),
    )
    out_specs = (
        P(("dp", "mp"), None),
        P(("dp", "mp"), None),
        P(("dp", "mp"), None),
        P(),
        P(),
        P(("dp", "mp"), None),
    )
    return jax.shard_map(shards, mesh=mesh, in_specs=in_specs, out_specs=out_specs, check_vma=False)
```

profile of v0, /device:TPU:1, one launch (start us, length us, event | category | flops | bytes accessed | tf_op | source)
XLA Modules:
  0.0 298.8 jit_solution(16578766114047801932)
XLA Ops:
  10.1 8.1 %scatter_custom_fusion = s32[4096]{0:T(1024)S(1)} fusion(s32[2048]{0:T(1024)S(1)} %bitcast.56, s32[2048]{0:T(1024)S(1)} %broadcast_select_fusion.3, s32[]{:T(128)} %constant.52.clone.1), kind=kCustom, calls=%fused_computation.54 | custom fusion | bytes 16388 | tf_op jit(solution)/shard_map/scatter | solution.py:47
  18.9 11.5 %all-to-all-start = ((s32[128,1,32]{2,1,0:T(1,128)}), s32[128,1,32]{2,1,0:T(1,128)S(1)}, u32[]{:S(2)}, u32[]{:S(2)}) async-start(s32[128,1,32]{2,1,0:T(1,128)} %bitcast.7), calls=%async_computation | async-start | bytes 131072 | tf_op jit(solution)/shard_map/all_to_all | solution.py:49
  32.7 7.2 %all-to-all-done = s32[128,1,32]{2,1,0:T(1,128)S(1)} async-done(((s32[128,1,32]{2,1,0:T(1,128)}), s32[128,1,32]{2,1,0:T(1,128)S(1)}, u32[]{:S(2)}, u32[]{:S(2)}) %all-to-all-start) | async-done | bytes 16416 | tf_op jit(solution)/shard_map/all_to_all | solution.py:49
  39.9 4.3 %all-to-all-start.3 = ((s32[128,1,2]{2,1,0:T(1,128)}), s32[128,1,2]{2,1,0:T(1,128)S(1)}, u32[]{:S(2)}, u32[]{:S(2)}) async-start(s32[128,1,2]{2,1,0:T(1,128)} %bitcast.20), calls=%async_computation.3 | async-start | bytes 131072 | tf_op jit(solution)/shard_map/all_to_all | solution.py:115
  44.7 14.2 %gather_fusion = f32[4096,128]{1,0:T(8,128)} fusion(f32[2048,128]{1,0:T(8,128)S(1)} %copy-done.1, s32[4096]{0:T(1024)S(1)} %broadcast_clamp_fusion), kind=kCustom, calls=%fused_computation | custom fusion | bytes 4210688 | tf_op jit(solution)/shard_map/jit(_take)/gather | solution.py:54
  58.9 4.2 %broadcast_select_fusion = f32[128,32,128]{2,1,0:T(8,128)} fusion(f32[128,32,128]{2,1,0:T(8,128)} %bitcast.51, pred[128,32]{1,0:T(8,128)(4,1)S(1)} %copy.36), kind=kLoop, calls=%fused_computation.23 | loop fusion | flops 524288 | bytes 4198400 | tf_op jit(solution)/shard_map/jit(_take)/select_n | solution.py:54
  63.1 10.2 %all-to-all-start.1 = ((f32[128,32,128]{2,1,0:T(8,128)}), f32[128,32,128]{2,1,0:T(8,128)}, u32[]{:S(2)}, u32[]{:S(2)}) async-start(f32[128,32,128]{2,1,0:T(8,128)} %broadcast_select_fusion), calls=%async_computation.1 | async-start | bytes 4194304 | tf_op jit(solution)/shard_map/all_to_all | solution.py:53
  74.0 2.6 fusion.22
  78.6 1.2 broadcast_select_fusion.1
  79.9 23.7 %all-to-all-done.1 = f32[128,32,128]{2,1,0:T(8,128)} async-done(((f32[128,32,128]{2,1,0:T(8,128)}), f32[128,32,128]{2,1,0:T(8,128)}, u32[]{:S(2)}, u32[]{:S(2)}) %all-to-all-start.1) | async-done | bytes 2097184 | tf_op jit(solution)/shard_map/all_to_all | solution.py:53
  103.5 3.7 %all-to-all-start.4 = ((bf16[128,2,768]{2,1,0:T(2,128)(2,1)}), bf16[128,2,768]{2,1,0:T(2,128)(2,1)S(1)}, u32[]{:S(2)}, u32[]{:S(2)}) async-start(bf16[128,2,768]{2,1,0:T(2,128)(2,1)} %broadcast_select_fusion.1), calls=%async_computation.4 | async-start | bytes 786432 | tf_op jit(solution)/shard_map/all_to_all | solution.py:111
  107.5 9.2 %gather_fusion.1 = f32[2048,128]{1,0:T(8,128)} fusion(f32[4096,128]{1,0:T(8,128)} %bitcast.10, s32[2048]{0:T(1024)S(1)} %broadcast_clamp_fusion.1), kind=kCustom, calls=%fused_computation.1 | custom fusion | bytes 2105344 | tf_op jit(solution)/shard_map/jit(_take)/gather | solution.py:62
  116.8 2.7 select_reduce_fusion
  119.4 1.7 multiply_convert_fusion
  121.1 2.3 convolution_bitcast_fusion
  125.7 1.3 bitcast_select_fusion
  127.0 7.4 %scatter_custom_fusion.2 = f32[4096,128]{1,0:T(8,128)} fusion(s32[2048]{0:T(1024)S(1)} %bitcast.58, f32[2048,128]{1,0:T(8,128)} %bitcast_select_fusion, f32[]{:T(128)} %constant.57.clone.1), kind=kCustom, calls=%fused_computation.25 | custom fusion | bytes 2097664 | tf_op jit(solution)/shard_map/scatter | solution.py:84
  134.5 2.7 convert_element_type.35
  137.2 10.3 %all-to-all-start.2 = ((bf16[128,32,128]{2,1,0:T(8,128)(2,1)}), bf16[128,32,128]{2,1,0:T(8,128)(2,1)}, u32[]{:S(2)}, u32[]{:S(2)}) async-start(bf16[128,32,128]{2,1,0:T(8,128)(2,1)} %bitcast.52), calls=%async_computation.2 | async-start | bytes 2097152 | tf_op jit(solution)/shard_map/all_to_all | solution.py:85
  147.8 22.4 %scatter_custom_fusion.1 = s32[2048]{0:T(1024)S(1)} fusion(s32[4096]{0:T(1024)S(1)} %reshape.217, s32[4096]{0:T(1024)S(1)} %convert_element_type.31, s32[]{:T(128)} %constant.45.clone.1), kind=kCustom, calls=%fused_computation.61 | custom fusion | flops 4096 | bytes 8196 | tf_op jit(solution)/shard_map/scatter-add | solution.py:100
  172.0 26.0 %scatter_custom_fusion.3 = f32[2048,128]{1,0:T(8,128)} fusion(s32[4096]{0:T(1024)S(1)} %reshape.217, bf16[4096,128]{1,0:T(8,128)(2,1)} %bitcast.23, f32[]{:T(128)} %constant.57.clone.1, pred[4096]{0:T(1024)(128)(4,1)S(1)} %ge.41), kind=kCustom, calls=%fused_computation.10 | custom fusion | flops 1572864 | bytes 2102272 | tf_op jit(solution)/shard_map/scatter-add | solution.py:98
  198.0 3.4 %fusion.11 = (f32[2048,128]{1,0:T(8,128)}, f32[2048,128]{1,0:T(8,128)}, f32[2048,128]{1,0:T(8,128)}) fusion(f32[2048,128]{1,0:T(8,128)} %param.19, f32[2048,128]{1,0:T(8,128)} %scatter_custom_fusion.3, pred[2048]{0:T(1024)(128)(4,1)S(1)} %broadcast_compare_fusion.1, f32[2048,128]{1,0:T(8,128)S(1)} %copy-done.1, f32[2048,128]{1,0:T(8,128)} %param.18), kind=kLoop, calls=%fused_computation.33 | loop fusion | flops 3932160 | bytes 7342080 | tf_op jit(solution)/shard_map/jit(_where)/select_n | solution.py:107
  201.4 86.1 %all-reduce.3.cloned.1.call-done = (f32[768,1024]{0,1:T(8,128)}, f32[128,1024]{1,0:T(8,128)}) async-done(((f32[768,1024]{0,1:T(8,128)}, f32[128,1024]{1,0:T(8,128)}), (f32[768,1024]{0,1:T(8,128)}, f32[128,1024]{1,0:T(8,128)})) %all-reduce.3.cloned.1.call-update) | async-done | bytes 3670032 | tf_op jit(solution)/shard_map/psum | solution.py:108
  287.6 3.6 %copy.40 = f32[768,1024]{1,0:T(8,128)} copy(f32[768,1024]{0,1:T(8,128)} %get-tuple-element.30) | data formatting | bytes 6291456
  (73 shorter events, 14.3 us)
Async XLA Ops:
  7.2 69.7 %copy-start = (bf16[1024,768]{1,0:T(8,128)(2,1)S(1)}, bf16[1024,768]{1,0:T(8,128)(2,1)}, u32[]{:S(2)}) copy-start(bf16[1024,768]{1,0:T(8,128)(2,1)} %param.25) | copy-start | bytes 4718596
  8.5 0.7 copy-start.5
  8.6 1.3 copy-start.9
  8.6 1.5 copy-start.6
  8.6 21.8 %copy-start.7 = (s32[128,1]{0,1:T(1,128)S(1)}, s32[128,1]{0,1:T(1,128)}, u32[]{:S(2)}) copy-start(s32[128,1]{0,1:T(1,128)} %param.23) | copy-start | bytes 1540
  8.6 36.0 %copy-start.1 = (f32[2048,128]{1,0:T(8,128)S(1)}, f32[2048,128]{1,0:T(8,128)}, u32[]{:S(2)}) copy-start(f32[2048,128]{1,0:T(8,128)} %param.17) | copy-start | bytes 3145732
  18.9 21.1 %all-to-all-start = ((s32[128,1,32]{2,1,0:T(1,128)}), s32[128,1,32]{2,1,0:T(1,128)S(1)}, u32[]{:S(2)}, u32[]{:S(2)}) async-start(s32[128,1,32]{2,1,0:T(1,128)} %bitcast.7), calls=%async_computation | async-start | bytes 131072 | tf_op jit(solution)/shard_map/all_to_all | solution.py:49
  39.9 23.2 %all-to-all-start.3 = ((s32[128,1,2]{2,1,0:T(1,128)}), s32[128,1,2]{2,1,0:T(1,128)S(1)}, u32[]{:S(2)}, u32[]{:S(2)}) async-start(s32[128,1,2]{2,1,0:T(1,128)} %bitcast.20), calls=%async_computation.3 | async-start | bytes 131072 | tf_op jit(solution)/shard_map/all_to_all | solution.py:115
  63.1 10.9 %copy-start.2 = (bf16[128,768]{1,0:T(8,128)(2,1)S(1)}, bf16[128,768]{1,0:T(8,128)(2,1)}, u32[]{:S(2)}) copy-start(bf16[128,768]{1,0:T(8,128)(2,1)} %param.13) | copy-start | bytes 589828
  63.1 40.4 %all-to-all-start.1 = ((f32[128,32,128]{2,1,0:T(8,128)}), f32[128,32,128]{2,1,0:T(8,128)}, u32[]{:S(2)}, u32[]{:S(2)}) async-start(f32[128,32,128]{2,1,0:T(8,128)} %broadcast_select_fusion), calls=%async_computation.1 | async-start | bytes 4194304 | tf_op jit(solution)/shard_map/all_to_all | solution.py:53
  103.5 33.6 %all-to-all-start.4 = ((bf16[128,2,768]{2,1,0:T(2,128)(2,1)}), bf16[128,2,768]{2,1,0:T(2,128)(2,1)S(1)}, u32[]{:S(2)}, u32[]{:S(2)}) async-start(bf16[128,2,768]{2,1,0:T(2,128)(2,1)} %broadcast_select_fusion.1), calls=%async_computation.4 | async-start | bytes 786432 | tf_op jit(solution)/shard_map/all_to_all | solution.py:111
  107.3 180.3 %all-reduce.3.cloned.1.call-start = ((), (), s32[]{:S(2)}) async-start(), calls=%async_computation.5 | async-start | bytes 7340032 | tf_op jit(solution)/shard_map/psum | solution.py:108
  107.5 11.9 %copy-start.8 = (f32[128]{0:T(128)S(1)}, f32[128]{0:T(128)}, u32[]{:S(2)}) copy-start(f32[128]{0:T(128)} %convert_element_type.32) | copy-start | bytes 1540
  116.8 4.4 %copy-start.3 = (bf16[128,768]{1,0:T(8,128)(2,1)S(1)}, bf16[128,768]{1,0:T(8,128)(2,1)}, u32[]{:S(2)}) copy-start(bf16[128,768]{1,0:T(8,128)(2,1)} %param.13) | copy-start | bytes 589828
  137.2 34.8 %all-to-all-start.2 = ((bf16[128,32,128]{2,1,0:T(8,128)(2,1)}), bf16[128,32,128]{2,1,0:T(8,128)(2,1)}, u32[]{:S(2)}, u32[]{:S(2)}) async-start(bf16[128,32,128]{2,1,0:T(8,128)(2,1)} %bitcast.52), calls=%async_computation.2 | async-start | bytes 2097152 | tf_op jit(solution)/shard_map/all_to_all | solution.py:85
  287.6 3.6 %copy-start.4 = (f32[128,1024]{1,0:T(8,128)S(1)}, f32[128,1024]{1,0:T(8,128)}, u32[]{:S(2)}) copy-start(f32[128,1024]{1,0:T(8,128)} %get-tuple-element.45) | copy-start | bytes 1572868
Sparse Core Ops, SparseCore 0:
  124.7 162.8 all-reduce.2
where the time goes:
time: 300 us; the launch traced here: 299 us
  waiting for transfers between devices  117 us (39%)
  other arithmetic  67.3 us (22%)
  local copies, waits for them, and re-layouts  50.9 us (17%)
  starting transfers between devices  40.3 us (13%)
  between operations  14.4 us (5%)
  matrix products  8.84 us (3%)
    psum x1, waiting for transfers between devices, shards(): grad_self, grad_rel = lax.psum((part_self, part_rel), ('dp', 'mp'))  86.1 us
    scatter-add x1, other arithmetic, shards(): row_grad = jnp.zeros(table.shape, jnp.float32).at[safe_rows].add(jnp.wher...  26 us
    all_to_all x1, waiting for transfers between devices, shards(): lax.all_to_all(jnp.take(table, jnp.maximum(wanted_part, 0), axis=0), ('dp...  23.7 us
    scatter-add x1, other arithmetic, shards(): jnp.zeros((table.shape[0],), jnp.int32).at[safe_rows]  22.4 us
    gather x1, local copies, waits for them, and re-layouts, shards(): jnp.take(table, jnp.maximum(wanted_part, 0), axis=0)  14.2 us
    all_to_all x1, starting transfers between devices, shards(): lax.all_to_all(asked.reshape(devs, capacity), ('dp', 'mp'), split_axis=0,...  11.5 us
    all_to_all x1, starting transfers between devices, shards(): lax.all_to_all(outgoing.reshape(devs, capacity, emb).astype(jnp.bfloat16)...  10.3 us
    all_to_all x1, starting transfers between devices, shards(): lax.all_to_all(jnp.take(table, jnp.maximum(wanted_part, 0), axis=0), ('dp...  10.2 us
  transfers between devices with their start and end apart: 6, of which 3 were waited for; matrix products, arithmetic and copies ran while one was open for 37% of the time, Pallas kernels for 0%

commit v1 on v0

v1 whole, which is shorter than its diff:
```python
import functools

import jax
import jax.numpy as jnp
from jax import lax
from jax.experimental import pallas as pl
from jax.experimental.pallas import tpu as pltpu
from jax.sharding import Mesh, PartitionSpec as P

F32 = jnp.float32
BF16 = jnp.bfloat16
I32 = jnp.int32
LANES = 128
CAP = 32
FCAP = 2
GROUP = LANES // CAP
EMPTY = 4095
VMEM = pl.BlockSpec(memory_space=pltpu.VMEM)
SMEM = pl.BlockSpec(memory_space=pltpu.SMEM)


def iota(shape, dim):
    return lax.broadcasted_iota(I32, shape, dim)


def dot(a, b, contract=((1,), (0,))):
    return lax.dot_general(a, b, (contract, ((), ())), preferred_element_type=F32)


def params():
    return pltpu.CompilerParams(vmem_limit_bytes=48 * 1024 * 1024)


def onehot(mask):
    return jnp.where(mask, F32(1.0), F32(0.0)).astype(BF16)


def place_kernel(
    lane_group, owner, row, counts, next_owner, next_row, asked, seed_of, cnt, paper_pick, seed_scr
):
    devs = LANES
    blocks = owner.shape[0]
    group = lane_group[0]
    sub = iota((devs, LANES), 0)
    lane = iota((devs, LANES), 1)
    seeds_row = LANES // (LANES * blocks // devs)
    count_row = counts[...].astype(F32)
    spread = jnp.where(
        iota((blocks, LANES), 1) // seeds_row == iota((blocks, LANES), 0), count_row, F32(0.0)
    ).astype(BF16)
    slots_per = LANES // seeds_row
    pick = onehot(sub % seeds_row == lane // slots_per)
    cnt_edge = dot(spread, pick)
    k_edge = (iota((blocks, LANES), 1) % slots_per).astype(F32)
    live_owner = jnp.where(k_edge < cnt_edge, owner[...], -1)
    upper = onehot(sub < lane)
    ones = jnp.ones((devs, LANES), BF16)
    scan = jnp.concatenate([upper, ones], axis=1)
    base = jnp.zeros((devs, LANES), F32)
    acc = jnp.zeros((devs, 3 * CAP), F32)
    ksub = iota((CAP, LANES), 0).astype(F32)
    for b in range(blocks):
        hot = sub == live_owner[b : b + 1, :]
        hot_f = jnp.where(hot, F32(1.0), F32(0.0))
        hot_b = hot_f.astype(BF16)
        scanned = dot(hot_b, scan)
        slot = jnp.sum(hot_f * (scanned[:, :LANES] + base), axis=0, keepdims=True)
        base = base + scanned[:, LANES:]
        at = ksub == slot
        r = row[b : b + 1, :]
        seed1 = b * seeds_row + iota((1, LANES), 1) // slots_per + 1
        vals = jnp.concatenate(
            [
                jnp.where(at, (r // LANES).astype(F32), F32(0.0)),
                jnp.where(at, (r % LANES).astype(F32), F32(0.0)),
                jnp.where(at, seed1.astype(F32), F32(0.0)),
            ],
            axis=0,
        ).astype(BF16)
        acc = acc + dot(hot_b, vals, ((1,), (1,)))
    acc_i = acc.astype(I32)
    seeds = acc_i[:, 2 * CAP :]
    wanted = jnp.where(seeds > 0, acc_i[:, :CAP] * LANES + acc_i[:, CAP : 2 * CAP], EMPTY)

    hot = sub == next_owner[...]
    hot_f = jnp.where(hot, F32(1.0), F32(0.0))
    hot_b = hot_f.astype(BF16)
    before = dot(hot_b, upper)
    slot = jnp.sum(hot_f * before, axis=0, keepdims=True)
    nrow = next_row[...]
    vals = []
    for t in range(FCAP):
        paper_pick[t] = jnp.where(slot == t, hot_f, F32(0.0)).astype(BF16)
        at = (slot == t) & (iota((CAP, LANES), 0) == t)
        vals.append(
            (
                jnp.where(at, (nrow // LANES).astype(F32), F32(0.0)),
                jnp.where(at, (nrow % LANES).astype(F32), F32(0.0)),
            )
        )
    hi = functools.reduce(lambda a, b: a + b, [v[0] for v in vals])
    lo = functools.reduce(lambda a, b: a + b, [v[1] for v in vals])
    pacc = dot(hot_b, jnp.concatenate([hi, lo], axis=0).astype(BF16), ((1,), (1,))).astype(I32)
    paper = pacc[:, :CAP] * LANES + pacc[:, CAP:]

    quarter = lane // CAP
    wide_wanted = jnp.concatenate([wanted] * GROUP, axis=1)
    wide_paper = jnp.concatenate([paper] * GROUP, axis=1)
    asked[...] = jnp.where(
        quarter == group,
        wide_wanted,
        jnp.where(quarter == (group + 1) % GROUP, wide_paper, 0),
    )
    seed_scr[...] = jnp.where(quarter == sub % GROUP, jnp.concatenate([seeds] * GROUP, axis=1), 0)
    total = seed_scr[pl.ds(0, devs // GROUP, stride=GROUP), :]
    for i in range(1, GROUP):
        total = total + seed_scr[pl.ds(i, devs // GROUP, stride=GROUP), :]
    seed_of[...] = total
    cnt[...] = jnp.broadcast_to(count_row, (devs, LANES)).T


def place(group, owner, row, counts, next_owner, next_row):
    devs = LANES
    return pl.pallas_call(
        place_kernel,
        out_shape=(
            jax.ShapeDtypeStruct((devs, LANES), I32),
            jax.ShapeDtypeStruct((devs // GROUP, LANES), I32),
            jax.ShapeDtypeStruct((devs, LANES), F32),
            jax.ShapeDtypeStruct((FCAP, devs, LANES), BF16),
        ),
        in_specs=[SMEM, VMEM, VMEM, VMEM, VMEM, VMEM],
        out_specs=(VMEM, VMEM, VMEM, VMEM),
        scratch_shapes=[pltpu.VMEM((devs, LANES), I32)],
        compiler_params=params(),
        name="place",
    )(group, owner, row, counts, next_owner, next_row)


def gather_kernel(got, table, rows, wanted_out, hot_scr, hi_scr):
    devs = LANES
    lines = devs // GROUP
    quarter = iota((lines, LANES), 1) // CAP
    wanted = jnp.zeros((lines, LANES), I32)
    for i in range(GROUP):
        wanted = wanted + jnp.where(
            quarter == i, got[pl.ds(i, lines, stride=GROUP), :], 0
        )
    wanted_out[...] = wanted
    lo = (wanted % 256).T
    hi = (wanted // 256).T
    lane2 = iota((LANES, 256), 1)
    for b in range(lines):
        hot_scr[b * LANES : (b + 1) * LANES, :] = onehot(lo[:, b : b + 1] == lane2)
        hi_scr[b * LANES : (b + 1) * LANES, :] = jnp.broadcast_to(
            hi[:, b : b + 1], (LANES, LANES)
        )
    chunk = 512
    tiles = table.shape[0] // 512
    wide = [
        jnp.concatenate(
            [
                table[q * 512 : q * 512 + 256, :].astype(BF16),
                table[q * 512 + 256 : (q + 1) * 512, :].astype(BF16),
            ],
            axis=1,
        )
        for q in range(tiles)
    ]

    def body(c, carry):
        at = pl.ds(pl.multiple_of(c * chunk, chunk), chunk)
        hot = hot_scr[at, :]
        high = hi_scr[at, :]
        out = jnp.zeros((chunk, LANES), F32)
        for q in range(tiles):
            both = dot(hot, wide[q])
            out = jnp.where(high == 2 * q, both[:, :LANES], out)
            out = jnp.where(high == 2 * q + 1, both[:, LANES:], out)
        rows[at, :] = out.astype(BF16)
        return carry

    lax.fori_loop(0, rows.shape[0] // chunk, body, 0)


def gather(got, table):
    slots = LANES * CAP
    return pl.pallas_call(
        gather_kernel,
        out_shape=(
            jax.ShapeDtypeStruct((slots, LANES), BF16),
            jax.ShapeDtypeStruct((LANES // GROUP, LANES), I32),
        ),
        in_specs=[VMEM, VMEM],
        out_specs=(VMEM, VMEM),
        scratch_shapes=[pltpu.VMEM((slots, 256), BF16), pltpu.VMEM((slots, LANES), I32)],
        compiler_params=params(),
        name="gather_rows",
    )(got, table)


def paper_kernel(got, paper, rows):
    devs = LANES
    sub = iota((devs, LANES), 0)
    lane = iota((devs, LANES), 1)
    first = ((sub % GROUP + 1) % GROUP) * CAP
    for t in range(FCAP):
        asked = jnp.sum(jnp.where(lane == first + t, got[...], 0), axis=1, keepdims=True)
        hot = onehot(asked == iota((devs, paper.shape[0]), 1))
        rows[t] = dot(hot, paper[...]).astype(BF16)


def paper_rows(got, paper):
    return pl.pallas_call(
        paper_kernel,
        out_shape=jax.ShapeDtypeStruct((FCAP, LANES, paper.shape[1]), BF16),
        in_specs=[VMEM, VMEM],
        out_specs=VMEM,
        compiler_params=params(),
        name="gather_papers",
    )(got, paper)


def forward_kernel(
    fetched, seed_of, cnt, pre_self, w_rel, cotangent, agg_out, dpre_out, outgoing, match_scr
):
    devs = LANES
    lines = seed_of.shape[0]
    seed1 = iota((devs, LANES), 0) + 1
    agg = jnp.zeros((devs, LANES), F32)
    for b in range(lines):
        at = slice(b * LANES, (b + 1) * LANES)
        match = onehot(seed1 == seed_of[b : b + 1, :])
        agg = agg + dot(match, fetched[at, :])
    count = cnt[...]
    agg_b = (agg / count).astype(BF16)
    agg_out[...] = agg_b
    pre = pre_self[...] + dot(agg_b, w_rel[...])
    sig = jax.nn.sigmoid(pre)
    dpre = (cotangent[...] * sig * (1.0 + pre * (1.0 - sig))).astype(BF16)
    dpre_out[...] = dpre
    dagg = dot(dpre, w_rel[...], ((1,), (1,)))
    grad = (dagg / count).astype(BF16)
    seeds_t = seed_of[...].T
    lane1 = iota((devs, LANES), 1) + 1
    for b in range(lines):
        at = slice(b * LANES, (b + 1) * LANES)
        match = onehot(seeds_t[:, b : b + 1] == lane1)
        outgoing[at, :] = dot(match, grad).astype(BF16)


def forward(fetched, seed_of, cnt, pre_self, w_rel, cotangent):
    seeds, hidden = cotangent.shape
    return pl.pallas_call(
        forward_kernel,
        out_shape=(
            jax.ShapeDtypeStruct((seeds, LANES), BF16),
            jax.ShapeDtypeStruct((seeds, hidden), BF16),
            jax.ShapeDtypeStruct(fetched.shape, BF16),
        ),
        in_specs=[VMEM] * 6,
        out_specs=(VMEM, VMEM, VMEM),
        scratch_shapes=[pltpu.VMEM((8, LANES), F32)],
        compiler_params=params(),
        name="layer",
    )(fetched, seed_of, cnt, pre_self, w_rel, cotangent)


def weight_kernel(feats0, feats1, agg0, agg1, dpre0, dpre1, out):
    left = jnp.concatenate(
        [
            jnp.concatenate([feats0[...], agg0[...]], axis=1),
            jnp.concatenate([feats1[...], agg1[...]], axis=1),
        ],
        axis=0,
    )
    right = jnp.concatenate([dpre0[...], dpre1[...]], axis=0)
    rows = left.shape[1]
    part = dot(left, right, ((0,), (0,)))
    for cb in range(right.shape[1] // LANES):
        out[cb * rows : (cb + 1) * rows, :] = part[:, cb * LANES : (cb + 1) * LANES].astype(BF16)


def weight_part(feats0, feats1, agg0, agg1, dpre0, dpre1):
    rows = feats0.shape[1] + agg0.shape[1]
    cols = dpre0.shape[1]
    return pl.pallas_call(
        weight_kernel,
        out_shape=jax.ShapeDtypeStruct((rows * cols // LANES, LANES), BF16),
        in_specs=[VMEM] * 6,
        out_specs=VMEM,
        compiler_params=params(),
        name="weight_part",
    )(feats0, feats1, agg0, agg1, dpre0, dpre1)


def spread_kernel(core, mine, other, grad_self, grad_rel):
    first = core[0] == 0
    feats = grad_self.shape[0]
    rows = feats + grad_rel.shape[0]
    blocks = mine.shape[0] // rows
    for cb in range(blocks):
        own = mine[cb * rows : (cb + 1) * rows, :].astype(F32)
        far = other[cb * rows : (cb + 1) * rows, :].astype(F32)
        low = jnp.where(first, own, far)
        high = jnp.where(first, far, own)
        for block, at in ((low, cb), (high, blocks + cb)):
            cols = slice(at * LANES, (at + 1) * LANES)
            grad_self[:, cols] = block[:feats]
            grad_rel[:, cols] = block[feats:]


def spread(core, mine, other, feats, emb, hidden):
    return pl.pallas_call(
        spread_kernel,
        out_shape=(
            jax.ShapeDtypeStruct((feats, hidden), F32),
            jax.ShapeDtypeStruct((emb, hidden), F32),
        ),
        in_specs=[SMEM, VMEM, VMEM],
        out_specs=(VMEM, VMEM),
        compiler_params=params(),
        name="weight_out",
    )(core, mine, other)


def adam_kernel(wanted, arrived, table, m1, m2, new_table, new_m1, new_m2, hot_scr, side_scr):
    step = pl.program_id(0)
    lines = wanted.shape[0]

    @pl.when(step == 0)
    def _():
        lo = wanted[...] % 256
        hi = (wanted[...] // 256).astype(F32).T
        sub = iota((256, LANES), 0)
        for b in range(lines):
            at = slice(b * LANES, (b + 1) * LANES)
            hot_scr[:, at] = onehot(sub == lo[b : b + 1, :])
            side_scr[at, :] = jnp.broadcast_to(hi[:, b : b + 1], (LANES, LANES)).astype(BF16)

    here = side_scr[...] == step.astype(F32).astype(BF16)
    mark = jnp.where(here, BF16(1.0), BF16(0.0))
    right = jnp.concatenate([arrived[...] * mark, mark], axis=1)
    both = dot(hot_scr[...], right)
    grad = both[:, :LANES]
    touched = both[:, LANES:] > 0.0
    m = 0.9 * m1[...] + 0.1 * grad
    v = 0.999 * m2[...] + 0.001 * grad * grad
    update = 0.05 * (m / (1.0 - 0.9**10)) / (jnp.sqrt(v / (1.0 - 0.999**10)) + 1e-08)
    new_table[...] = jnp.where(touched, table[...] - update, table[...])
    new_m1[...] = jnp.where(touched, m, m1[...])
    new_m2[...] = jnp.where(touched, v, m2[...])


def adam(wanted, arrived, table, m1, m2):
    rows = 256
    block = pl.BlockSpec((rows, LANES), lambda i: (i, 0))
    whole = lambda a: pl.BlockSpec(a.shape, lambda i: (0, 0))
    slots = arrived.shape[0]
    return pl.pallas_call(
        adam_kernel,
        grid=(table.shape[0] // rows,),
        out_shape=(jax.ShapeDtypeStruct(table.shape, F32),) * 3,
        in_specs=[whole(wanted), whole(arrived), block, block, block],
        out_specs=(block, block, block),
        scratch_shapes=[pltpu.VMEM((rows, slots), BF16), pltpu.VMEM((slots, LANES), BF16)],
        compiler_params=params(),
        name="adam",
    )(wanted, arrived, table, m1, m2)


def shards(
    feats,
    edge_owner,
    edge_row,
    counts,
    table,
    moment1,
    moment2,
    w_self,
    w_rel,
    cotangent,
    next_owner,
    next_row,
    paper_table,
):
    every = ("chip", "core", "mp")
    peers = ("chip", "mp")
    devs = lax.axis_size(every)
    seeds, width = feats.shape
    hidden = cotangent.shape[1]
    emb = table.shape[1]
    core = lax.axis_index("core")
    group = lax.axis_index("mp").astype(I32).reshape(1)

    def exchange(a, axes):
        return lax.all_to_all(a, axes, split_axis=0, concat_axis=0, tiled=True)

    def swap(a):
        return lax.ppermute(a, "core", [(0, 1), (1, 0)])

    asked, seed_of, cnt, paper_pick = place(
        group,
        edge_owner.reshape(-1, LANES),
        edge_row.reshape(-1, LANES),
        counts.reshape(1, -1),
        next_owner.reshape(1, -1),
        next_row.reshape(1, -1),
    )
    got = exchange(asked.reshape(devs, 1, LANES), every).reshape(devs, LANES)
    rows, wanted = gather(got, table)
    fetched = exchange(rows.reshape(devs, CAP, emb), every).reshape(devs * CAP, emb)

    pre_self = jnp.dot(feats, w_self, preferred_element_type=F32)
    feats_far = swap(feats)
    papers = paper_rows(got, paper_table)
    agg_b, dpre, outgoing = forward(fetched, seed_of, cnt, pre_self, w_rel, cotangent)

    half = hidden // 2
    dpre_here = lax.dynamic_slice_in_dim(dpre, core * half, half, 1)
    dpre_there = lax.dynamic_slice_in_dim(dpre, (1 - core) * half, half, 1)
    part = weight_part(feats, feats_far, agg_b, swap(agg_b), dpre_here, swap(dpre_there))
    n_peers = lax.axis_size(peers)
    parts = exchange(part.reshape(n_peers, -1, LANES), peers)
    mine = jnp.sum(parts.astype(F32), axis=0).astype(BF16)
    arrived = exchange(outgoing.reshape(devs, CAP, emb), every).reshape(devs * CAP, emb)
    full = exchange(jnp.broadcast_to(mine[None], parts.shape), peers).reshape(-1, LANES)
    new_table, new_moment1, new_moment2 = adam(wanted, arrived, table, moment1, moment2)
    grad_self, grad_rel = spread(
        core.astype(I32).reshape(1), full, swap(full), width, emb, hidden
    )

    papers = exchange(jnp.transpose(papers, (1, 0, 2)), every)
    next_feats = functools.reduce(
        lambda a, b: a + b,
        [
            lax.dot_general(
                paper_pick[t], papers[:, t, :], (((0,), (0,)), ((), ())), preferred_element_type=F32
            )
            for t in range(FCAP)
        ],
    ).astype(BF16)
    return (new_table, new_moment1, new_moment2, grad_self, grad_rel, next_feats)


def solution(mesh):
    n_mp = mesh.shape["mp"]
    wide = Mesh(mesh.devices.reshape(-1, 2, n_mp), ("chip", "core", "mp"))
    rows = P(("chip", "core", "mp"), None)
    line = P(("chip", "core", "mp"))
    in_specs = (rows, rows, line, line, rows, rows, rows, P(), P(), rows, rows, line, rows)
    out_specs = (rows, rows, rows, P(), P(), rows)
    return jax.shard_map(shards, mesh=wide, in_specs=in_specs, out_specs=out_specs, check_vma=False)
```

time: 300 us -> 170 us (0.57)
  other arithmetic: 67.3 us -> 1.34 us
  waiting for transfers between devices: 117 us -> 59.3 us
  blocking collectives: 0 us -> 41.3 us
  local copies, waits for them, and re-layouts: 50.9 us -> 13.2 us
  Pallas kernels: 0 us -> 25.6 us
  starting transfers between devices: 40.3 us -> 26 us
  between operations: 14.4 us -> 0.8 us
  matrix products: 8.84 us -> 1.53 us
    psum x1 -> x0, waiting for transfers between devices: 86.1 us -> none  [shards(): grad_self, grad_rel = lax.psum((part_self, part_rel), ('dp', 'mp'))]
    scatter-add x2 -> x0, other arithmetic: 48.4 us -> none  [the longest x1 26 us: shards(): row_grad = jnp.zeros(table.shape, jnp.float32).at[safe_rows].add(jnp.wher...]
    all_to_all x0 -> x2, blocking collectives: none -> 41.3 us  [exchange(): return lax.all_to_all(a, axes, split_axis=0, concat_axis=0, tiled=True)]
    all_to_all x5 -> x4, waiting for transfers between devices: 30.9 us -> 58.2 us  [exchange(): return lax.all_to_all(a, axes, split_axis=0, concat_axis=0, tiled=True)]
    gather x5 -> x0, local copies, waits for them, and re-layouts: 25.6 us -> none  [the longest x1 14.2 us: shards(): jnp.take(table, jnp.maximum(wanted_part, 0), axis=0)]
    pallas_call x0 -> x7, Pallas kernels: none -> 25.6 us  [the longest x1 9.83 us: adam(): pl.pallas_call(adam_kernel, grid=(table.shape[0] // rows,), out_shape=(ja...]
    all_to_all x5 -> x4, starting transfers between devices: 40.1 us -> 22.7 us  [exchange(): return lax.all_to_all(a, axes, split_axis=0, concat_axis=0, tiled=True)]
    scatter x3 -> x0, local copies, waits for them, and re-layouts: 16.6 us -> none  [the longest x1 8.06 us: shards(): asked = jnp.full((devs * capacity,), -1, jnp.int32).at[where_to].set(jnp....]
  transfers between devices with their start and end apart: 6 -> 8, of which waited for: 3 -> 5; matrix products, arithmetic and copies ran while one was open for 37% -> 3% of each run, Pallas kernels for 0% -> 8%
where the time goes in v1:
time: 170 us; the launch traced here: 169 us
  waiting for transfers between devices  59.3 us (35%)
  blocking collectives  41.3 us (24%)
  starting transfers between devices  26 us (15%)
  Pallas kernels  25.6 us (15%)
  local copies, waits for them, and re-layouts  13.2 us (8%)
    all_to_all x4, waiting for transfers between devices, exchange(): return lax.all_to_all(a, axes, split_axis=0, concat_axis=0, tiled=True)  58.2 us
    all_to_all x2, blocking collectives, exchange(): return lax.all_to_all(a, axes, split_axis=0, concat_axis=0, tiled=True)  41.3 us
    all_to_all x4, starting transfers between devices, exchange(): return lax.all_to_all(a, axes, split_axis=0, concat_axis=0, tiled=True)  22.7 us
    unnamed x34, local copies, waits for them, and re-layouts  10.1 us
    pallas_call x1, Pallas kernels, adam(): pl.pallas_call(adam_kernel, grid=(table.shape[0] // rows,), out_shape=(ja...  9.83 us
    pallas_call x1, Pallas kernels, gather(): pl.pallas_call(gather_kernel, out_shape=(jax.ShapeDtypeStruct((slots, LAN...  4.83 us
    pallas_call x1, Pallas kernels, spread(): pl.pallas_call(spread_kernel, out_shape=(jax.ShapeDtypeStruct((feats, hid...  3.58 us
  transfers between devices with their start and end apart: 8, of which 5 were waited for; matrix products, arithmetic and copies ran while one was open for 3% of the time, Pallas kernels for 8%

profile of v1, /device:TPU:1, one launch (start us, length us, event | category | flops | bytes accessed | tf_op | source)
XLA Modules:
  0.0 169.2 jit_solution(5446144163788976397)
XLA Ops:
  4.1 1.7 place.1
  5.8 20.9 %all_to_all.30 = s32[128,1,128]{2,1,0:T(1,128)S(1)} all-to-all(s32[128,1,128]{2,1,0:T(1,128)S(1)} %bitcast.39), channel_id=1, replica_groups=mesh['chip'=16,'core'=2,'mp'=4] {'chip','core','mp'}, dimensions={0} | all-to-all | bytes 131072 | tf_op jit(solution)/shard_map/all_to_all | solution.py:397
  26.8 1.2 copy-done.1
  28.0 4.8 %gather_rows.1 = (bf16[4096,128]{1,0:T(8,128)(2,1)S(1)}, s32[32,128]{1,0:T(8,128)S(1)}) custom-call(s32[128,128]{1,0:T(8,128)S(1)} %bitcast.37, f32[2048,128]{1,0:T(8,128)S(1)} %copy-done.1), custom_call_target="tpu_custom_call" | custom-call | tf_op jit(solution)/shard_map/gather_rows/pallas_call | solution.py:188
  33.8 4.3 %all-to-all-start.1 = ((bf16[128,32,128]{2,1,0:T(8,128)(2,1)}), bf16[128,32,128]{2,1,0:T(8,128)(2,1)S(1)}, u32[]{:S(2)}, u32[]{:S(2)}) async-start(bf16[128,32,128]{2,1,0:T(8,128)(2,1)} %bitcast.36), calls=%async_computation.1 | async-start | bytes 2097152 | tf_op jit(solution)/shard_map/all_to_all | solution.py:397
  38.1 1.1 collective-permute-start
  39.7 17.9 %all-to-all-done.1 = bf16[128,32,128]{2,1,0:T(8,128)(2,1)S(1)} async-done(((bf16[128,32,128]{2,1,0:T(8,128)(2,1)}), bf16[128,32,128]{2,1,0:T(8,128)(2,1)S(1)}, u32[]{:S(2)}, u32[]{:S(2)}) %all-to-all-start.1) | async-done | bytes 1048608 | tf_op jit(solution)/shard_map/all_to_all | solution.py:397
  59.6 2.6 %layer.1 = (bf16[128,128]{1,0:T(8,128)(2,1)S(1)}, bf16[128,1024]{1,0:T(8,128)(2,1)S(1)}, bf16[4096,128]{1,0:T(8,128)(2,1)}) custom-call(bf16[4096,128]{1,0:T(8,128)(2,1)S(1)} %bitcast.32, s32[32,128]{1,0:T(8,128)S(1)} %get-tuple-element.23.seed_of, f32[128,128]{1,0:T(8,128)S(1)} %get-tuple-element.24.cnt, f32[128,1024]{1,0:T(8,128)S(1)} %fusion.7.pre_self, ...), custom_call_target="tpu_custom_call" | custom-call | tf_op jit(solution)/shard_map/layer/pallas_call | solution.py:254
  63.9 2.4 %weight_part.1 = bf16[3584,128]{1,0:T(8,128)(2,1)} custom-call(bf16[128,768]{1,0:T(8,128)(2,1)S(1)} %copy-done.7, bf16[128,768]{1,0:T(8,128)(2,1)} %collective-permute-done.feats1, bf16[128,128]{1,0:T(8,128)(2,1)S(1)} %get-tuple-element.29.agg0, bf16[128,128]{1,0:T(8,128)(2,1)S(1)} %collective-permute-done.1.agg1, ...), custom_call_target="tpu_custom_call" | custom-call | tf_op jit(solution)/shard_map/weight_part/pallas_call | solution.py:287
  66.3 5.5 %all-to-all-start.3 = ((bf16[64,56,128]{2,1,0:T(8,128)(2,1)}), bf16[64,56,128]{2,1,0:T(8,128)(2,1)}, u32[]{:S(2)}, u32[]{:S(2)}) async-start(bf16[64,56,128]{2,1,0:T(8,128)(2,1)} %bitcast.14), calls=%async_computation.3 | async-start | bytes 1835008 | tf_op jit(solution)/shard_map/all_to_all | solution.py:397
  72.5 1.2 copy.22
  73.6 14.8 %all-to-all-done.3 = bf16[64,56,128]{2,1,0:T(8,128)(2,1)} async-done(((bf16[64,56,128]{2,1,0:T(8,128)(2,1)}), bf16[64,56,128]{2,1,0:T(8,128)(2,1)}, u32[]{:S(2)}, u32[]{:S(2)}) %all-to-all-start.3) | async-done | bytes 917536 | tf_op jit(solution)/shard_map/all_to_all | solution.py:397
  88.4 6.0 %all-to-all-start.5 = ((bf16[128,2,768]{2,1,0:T(2,128)(2,1)}), bf16[128,2,768]{2,1,0:T(2,128)(2,1)}, u32[]{:S(2)}, u32[]{:S(2)}) async-start(bf16[128,2,768]{2,1,0:T(2,128)(2,1)} %copy.22), calls=%async_computation.5 | async-start | bytes 786432 | tf_op jit(solution)/shard_map/all_to_all | solution.py:397
  94.4 1.3 reduce_sum.12
  95.7 10.9 %all-to-all-done.5 = bf16[128,2,768]{2,1,0:T(2,128)(2,1)} async-done(((bf16[128,2,768]{2,1,0:T(2,128)(2,1)}), bf16[128,2,768]{2,1,0:T(2,128)(2,1)}, u32[]{:S(2)}, u32[]{:S(2)}) %all-to-all-start.5) | async-done | bytes 393248 | tf_op jit(solution)/shard_map/all_to_all | solution.py:397
  106.8 20.4 %all_to_all.31 = bf16[64,56,128]{2,1,0:T(8,128)(2,1)S(1)} all-to-all(bf16[64,56,128]{2,1,0:T(8,128)(2,1)S(1)} %broadcast_in_dim.2), channel_id=1, replica_groups=mesh['chip'=16,'core'=2,'mp'=4] {'chip','mp'}, dimensions={0} | all-to-all | bytes 1835008 | tf_op jit(solution)/shard_map/all_to_all | solution.py:397
  127.1 7.0 %all-to-all-start.2 = ((bf16[128,32,128]{2,1,0:T(8,128)(2,1)}), bf16[128,32,128]{2,1,0:T(8,128)(2,1)}, u32[]{:S(2)}, u32[]{:S(2)}) async-start(bf16[128,32,128]{2,1,0:T(8,128)(2,1)} %bitcast.11), calls=%async_computation.2 | async-start | bytes 2097152 | tf_op jit(solution)/shard_map/all_to_all | solution.py:397
  134.1 1.5 collective-permute-start.3
  135.7 1.8 %fusion.6 = (bf16[128,1,768]{2,1,0:T(2,128)(2,1)S(1)}, bf16[128,1,768]{2,1,0:T(2,128)(2,1)S(1)}) fusion(bf16[128,2,768]{2,1,0:T(2,128)(2,1)} %all-to-all-done.5), kind=kLoop, calls=%fused_computation.11 | loop fusion | bytes 786432 | tf_op jit(solution)/shard_map/slice | solution.py:438
  138.6 14.7 %all-to-all-done.2 = bf16[128,32,128]{2,1,0:T(8,128)(2,1)} async-done(((bf16[128,32,128]{2,1,0:T(8,128)(2,1)}), bf16[128,32,128]{2,1,0:T(8,128)(2,1)}, u32[]{:S(2)}, u32[]{:S(2)}) %all-to-all-start.2) | async-done | bytes 1048608 | tf_op jit(solution)/shard_map/all_to_all | solution.py:397
  153.3 1.2 copy-done.5
  154.5 1.2 copy-done.6
  155.8 9.8 %adam.1 = (f32[2048,128]{1,0:T(8,128)}, f32[2048,128]{1,0:T(8,128)}, f32[2048,128]{1,0:T(8,128)}) custom-call(s32[32,128]{1,0:T(8,128)S(1)} %get-tuple-element.21.wanted, bf16[4096,128]{1,0:T(8,128)(2,1)} %bitcast.12.arrived, f32[2048,128]{1,0:T(8,128)S(1)} %copy-done.2, f32[2048,128]{1,0:T(8,128)S(1)} %copy-done.5, f32[2048,128]{1,0:T(8,128)S(1)} %copy-done.6), custom_call_target="tpu_custom_call" | custom-call | tf_op jit(solution)/shard_map/adam/pallas_call | solution.py:360
  165.6 3.6 %weight_out.1 = (f32[768,1024]{1,0:T(8,128)}, f32[128,1024]{1,0:T(8,128)}) custom-call(s32[1]{0:T(128)} %bitcast.13.core, bf16[3584,128]{1,0:T(8,128)(2,1)S(1)} %bitcast.34, bf16[3584,128]{1,0:T(8,128)(2,1)} %collective-permute-done.3.other), custom_call_target="tpu_custom_call" | custom-call | tf_op jit(solution)/shard_map/weight_out/pallas_call | solution.py:314
  (43 shorter events, 10.5 us)
Async XLA Ops:
  0.6 38.7 %copy-start = (bf16[768,1024]{1,0:T(8,128)(2,1)S(1)}, bf16[768,1024]{1,0:T(8,128)(2,1)}, u32[]{:S(2)}) copy-start(bf16[768,1024]{1,0:T(8,128)(2,1)} %param.20) | copy-start | bytes 4718596
  0.7 0.8 copy-start.12
  1.5 0.7 copy-start.13
  2.2 0.7 copy-start.14
  2.8 0.7 copy-start.15
  5.8 21.0 %copy-start.10 = (bf16[2,128,128]{2,1,0:T(8,128)(2,1)}, bf16[2,128,128]{2,1,0:T(8,128)(2,1)S(1)}, u32[]{:S(2)}) copy-start(bf16[2,128,128]{2,1,0:T(8,128)(2,1)S(1)} %get-tuple-element.33) | copy-start | bytes 196612
  26.8 1.2 copy-start.1
  28.0 10.1 %copy-start.7 = (bf16[128,768]{1,0:T(8,128)(2,1)S(1)}, bf16[128,768]{1,0:T(8,128)(2,1)}, u32[]{:S(2)}) copy-start(bf16[128,768]{1,0:T(8,128)(2,1)} %feats0.1) | copy-start | bytes 589828
  32.8 1.0 copy-start.4
  33.8 23.7 %all-to-all-start.1 = ((bf16[128,32,128]{2,1,0:T(8,128)(2,1)}), bf16[128,32,128]{2,1,0:T(8,128)(2,1)S(1)}, u32[]{:S(2)}, u32[]{:S(2)}) async-start(bf16[128,32,128]{2,1,0:T(8,128)(2,1)} %bitcast.36), calls=%async_computation.1 | async-start | bytes 2097152 | tf_op jit(solution)/shard_map/all_to_all | solution.py:397
  38.1 24.7 %collective-permute-start = (bf16[128,768]{1,0:T(8,128)(2,1)S(1)}, bf16[128,768]{1,0:T(8,128)(2,1)}, u32[]{:S(2)}, u32[]{:S(2)}) collective-permute-start(bf16[128,768]{1,0:T(8,128)(2,1)S(1)} %copy-done.7), channel_id=1, source_target_pairs={{0,4},{4,0},{1,5},{5,1},{2,6},{6,2},{3,7},{7,3},{8,12},{12,8},{9,1... | collective-permute-start | bytes 589832 | tf_op jit(solution)/shard_map/ppermute | solution.py:400
  57.6 1.0 copy-start.8
  58.6 0.9 copy-start.9
  62.2 1.7 collective-permute-start.2
  62.7 1.2 collective-permute-start.1
  63.9 7.9 %copy-start.3 = (bf16[1024,768]{1,0:T(8,128)(2,1)S(1)}, bf16[1024,768]{1,0:T(8,128)(2,1)}, u32[]{:S(2)}) copy-start(bf16[1024,768]{1,0:T(8,128)(2,1)} %paper.1) | copy-start | bytes 4718596
  66.3 22.1 %all-to-all-start.3 = ((bf16[64,56,128]{2,1,0:T(8,128)(2,1)}), bf16[64,56,128]{2,1,0:T(8,128)(2,1)}, u32[]{:S(2)}, u32[]{:S(2)}) async-start(bf16[64,56,128]{2,1,0:T(8,128)(2,1)} %bitcast.14), calls=%async_computation.3 | async-start | bytes 1835008 | tf_op jit(solution)/shard_map/all_to_all | solution.py:397
  88.4 18.3 %all-to-all-start.5 = ((bf16[128,2,768]{2,1,0:T(2,128)(2,1)}), bf16[128,2,768]{2,1,0:T(2,128)(2,1)}, u32[]{:S(2)}, u32[]{:S(2)}) async-start(bf16[128,2,768]{2,1,0:T(2,128)(2,1)} %copy.22), calls=%async_computation.5 | async-start | bytes 786432 | tf_op jit(solution)/shard_map/all_to_all | solution.py:397
  127.1 26.2 %all-to-all-start.2 = ((bf16[128,32,128]{2,1,0:T(8,128)(2,1)}), bf16[128,32,128]{2,1,0:T(8,128)(2,1)}, u32[]{:S(2)}, u32[]{:S(2)}) async-start(bf16[128,32,128]{2,1,0:T(8,128)(2,1)} %bitcast.11), calls=%async_computation.2 | async-start | bytes 2097152 | tf_op jit(solution)/shard_map/all_to_all | solution.py:397
  134.1 3.4 %copy-start.11 = (bf16[2,128,128]{2,1,0:T(8,128)(2,1)S(1)}, bf16[2,128,128]{2,1,0:T(8,128)(2,1)}, u32[]{:S(2)}) copy-start(bf16[2,128,128]{2,1,0:T(8,128)(2,1)} %copy-done.10) | copy-start | bytes 196612
  134.1 19.2 %copy-start.2 = (f32[2048,128]{1,0:T(8,128)S(1)}, f32[2048,128]{1,0:T(8,128)}, u32[]{:S(2)}) copy-start(f32[2048,128]{1,0:T(8,128)} %table.3) | copy-start | bytes 3145732
  134.1 31.5 %collective-permute-start.3 = (bf16[3584,128]{1,0:T(8,128)(2,1)S(1)}, bf16[3584,128]{1,0:T(8,128)(2,1)}, u32[]{:S(2)}, u32[]{:S(2)}) collective-permute-start(bf16[3584,128]{1,0:T(8,128)(2,1)S(1)} %bitcast.33), channel_id=1, source_target_pairs={{0,4},{4,0},{1,5},{5,1},{2,6},{6,2},{3,7},{7,3},{8,12},{12,8},{9,1... | collective-permute-start | bytes 2752520 | tf_op jit(solution)/shard_map/ppermute | solution.py:400
  153.3 1.2 copy-start.5
  154.5 1.2 copy-start.6
  (1 other events, 0.7 us)

commit v2 on v1

v2 whole, which is shorter than its diff:
```python
import functools

import jax
import jax.numpy as jnp
from jax import lax
from jax.experimental import pallas as pl
from jax.experimental.pallas import tpu as pltpu
from jax.sharding import Mesh, PartitionSpec as P

F32 = jnp.float32
BF16 = jnp.bfloat16
I32 = jnp.int32
LANES = 128
CAP = 32
FCAP = 2
GROUP = LANES // CAP
EMPTY = 4095
SELF_ROWS = 24
WEIGHT_ROWS = 32
PAPER_AT = CAP + WEIGHT_ROWS
PAPER_ROWS = 16
BUNDLE = PAPER_AT + PAPER_ROWS
VMEM = pl.BlockSpec(memory_space=pltpu.VMEM)
SMEM = pl.BlockSpec(memory_space=pltpu.SMEM)


def iota(shape, dim):
    return lax.broadcasted_iota(I32, shape, dim)


def dot(a, b, contract=((1,), (0,))):
    return lax.dot_general(a, b, (contract, ((), ())), preferred_element_type=F32)


def onehot(mask):
    return jnp.where(mask, F32(1.0), F32(0.0)).astype(BF16)

ANY = pl.BlockSpec(memory_space=pl.ANY)


def fetch(pairs, sems):
    copies = [pltpu.make_async_copy(a, b, sems.at[i]) for i, (a, b) in enumerate(pairs)]
    for c in copies:
        c.start()
    return copies


def place_kernel(
    lane_group,
    owner_in,
    row_in,
    counts_in,
    next_owner_in,
    next_row_in,
    asked,
    seed_of,
    cnt,
    paper_pick,
    owner,
    row,
    counts,
    next_owner,
    next_row,
    seed_scr,
    sems,
):
    copies = fetch(
        [
            (owner_in, owner),
            (row_in, row),
            (counts_in, counts),
            (next_owner_in, next_owner),
            (next_row_in, next_row),
        ],
        sems,
    )
    devs = LANES
    blocks = owner.shape[0]
    group = lane_group[0]
    sub = iota((devs, LANES), 0)
    lane = iota((devs, LANES), 1)
    seeds_row = LANES // (LANES * blocks // devs)
    slots_per = LANES // seeds_row
    upper = onehot(sub < lane)
    ones = jnp.ones((devs, LANES), BF16)
    scan = jnp.concatenate([upper, ones], axis=1)
    pick = onehot(sub % seeds_row == lane // slots_per)
    for c in copies:
        c.wait()
    count_row = counts[...].astype(F32)
    spread = jnp.where(
        iota((blocks, LANES), 1) // seeds_row == iota((blocks, LANES), 0), count_row, F32(0.0)
    ).astype(BF16)
    cnt_edge = dot(spread, pick)
    k_edge = (iota((blocks, LANES), 1) % slots_per).astype(F32)
    live_owner = jnp.where(k_edge < cnt_edge, owner[...], -1)
    base = jnp.zeros((devs, LANES), F32)
    acc = jnp.zeros((devs, 3 * CAP), F32)
    ksub = iota((CAP, LANES), 0).astype(F32)
    for b in range(blocks):
        hot = sub == live_owner[b : b + 1, :]
        hot_f = jnp.where(hot, F32(1.0), F32(0.0))
        hot_b = hot_f.astype(BF16)
        scanned = dot(hot_b, scan)
        slot = jnp.sum(hot_f * (scanned[:, :LANES] + base), axis=0, keepdims=True)
        base = base + scanned[:, LANES:]
        at = ksub == slot
        r = row[b : b + 1, :]
        seed1 = b * seeds_row + iota((1, LANES), 1) // slots_per + 1
        vals = jnp.concatenate(
            [
                jnp.where(at, (r // LANES).astype(F32), F32(0.0)),
                jnp.where(at, (r % LANES).astype(F32), F32(0.0)),
                jnp.where(at, seed1.astype(F32), F32(0.0)),
            ],
            axis=0,
        ).astype(BF16)
        acc = acc + dot(hot_b, vals, ((1,), (1,)))
    acc_i = acc.astype(I32)
    seeds = acc_i[:, 2 * CAP :]
    wanted = jnp.where(seeds > 0, acc_i[:, :CAP] * LANES + acc_i[:, CAP : 2 * CAP], EMPTY)

    hot = sub == next_owner[...]
    hot_f = jnp.where(hot, F32(1.0), F32(0.0))
    hot_b = hot_f.astype(BF16)
    before = dot(hot_b, upper)
    slot = jnp.sum(hot_f * before, axis=0, keepdims=True)
    nrow = next_row[...]
    for t in range(FCAP):
        paper_pick[t] = jnp.where(slot == t, hot_f, F32(0.0)).astype(BF16)
    at = iota((CAP, LANES), 0) == slot.astype(I32)
    vals = jnp.concatenate(
        [
            jnp.where(at, (nrow // LANES).astype(F32), F32(0.0)),
            jnp.where(at, (nrow % LANES).astype(F32), F32(0.0)),
        ],
        axis=0,
    ).astype(BF16)
    pacc = dot(hot_b, vals, ((1,), (1,))).astype(I32)
    paper = pacc[:, :CAP] * LANES + pacc[:, CAP:]

    quarter = lane // CAP
    wide_wanted = jnp.concatenate([wanted] * GROUP, axis=1)
    wide_paper = jnp.concatenate([paper] * GROUP, axis=1)
    asked[...] = jnp.where(
        quarter == group,
        wide_wanted,
        jnp.where(quarter == (group + 1) % GROUP, wide_paper, 0),
    )
    seed_scr[...] = jnp.where(quarter == sub % GROUP, jnp.concatenate([seeds] * GROUP, axis=1), 0)
    total = seed_scr[pl.ds(0, devs // GROUP, stride=GROUP), :]
    for i in range(1, GROUP):
        total = total + seed_scr[pl.ds(i, devs // GROUP, stride=GROUP), :]
    seed_of[...] = total
    cnt[...] = jnp.broadcast_to(count_row, (devs, LANES)).T


def place(group, owner, row, counts, next_owner, next_row):
    devs = LANES
    ins = (owner, row, counts, next_owner, next_row)
    return pl.pallas_call(
        place_kernel,
        out_shape=(
            jax.ShapeDtypeStruct((devs, LANES), I32),
            jax.ShapeDtypeStruct((devs // GROUP, LANES), I32),
            jax.ShapeDtypeStruct((devs, LANES), F32),
            jax.ShapeDtypeStruct((FCAP, devs, LANES), BF16),
        ),
        in_specs=[SMEM] + [ANY] * len(ins),
        out_specs=(VMEM, VMEM, VMEM, VMEM),
        scratch_shapes=[pltpu.VMEM(a.shape, I32) for a in ins]
        + [pltpu.VMEM((devs, LANES), I32), pltpu.SemaphoreType.DMA((len(ins),))],
        name="place",
    )(group, *ins)


def gather_kernel(got, table_in, rows, wanted_out, table, hot_scr, hi_scr, out_scr, sems, out_sems):
    devs = LANES
    lines = devs // GROUP
    part = table.shape[0] // 4
    copies = fetch(
        [
            (table_in.at[pl.ds(i * part, part), :], table.at[pl.ds(i * part, part), :])
            for i in range(4)
        ],
        sems,
    )
    quarter = iota((lines, LANES), 1) // CAP
    wanted = jnp.zeros((lines, LANES), I32)
    for i in range(GROUP):
        wanted = wanted + jnp.where(quarter == i, got[pl.ds(i, lines, stride=GROUP), :], 0)
    wanted_out[...] = wanted
    lo = (wanted % 256).T
    hi = (wanted // 256).T
    lane2 = iota((LANES, 256), 1)
    for b in range(lines):
        hot_scr[b * LANES : (b + 1) * LANES, :] = onehot(lo[:, b : b + 1] == lane2)
        hi_scr[b * LANES : (b + 1) * LANES, :] = jnp.broadcast_to(hi[:, b : b + 1], (LANES, LANES))
    for c in copies:
        c.wait()
    chunk = 512
    tiles = table.shape[0] // 512
    wide = [
        jnp.concatenate(
            [
                table[q * 512 : q * 512 + 256, :].astype(BF16),
                table[q * 512 + 256 : (q + 1) * 512, :].astype(BF16),
            ],
            axis=1,
        )
        for q in range(tiles)
    ]
    outs = []
    for c in range(out_scr.shape[0] // chunk):
        at = pl.ds(c * chunk, chunk)
        hot = hot_scr[at, :]
        high = hi_scr[at, :]
        out = jnp.zeros((chunk, LANES), F32)
        for q in range(tiles):
            both = dot(hot, wide[q])
            out = jnp.where(high == 2 * q, both[:, :LANES], out)
            out = jnp.where(high == 2 * q + 1, both[:, LANES:], out)
        out_scr[at, :] = out.astype(BF16)
        copy = pltpu.make_async_copy(out_scr.at[at, :], rows.at[at, :], out_sems.at[c])
        copy.start()
        outs.append(copy)
    for copy in outs:
        copy.wait()


def gather(got, table):
    slots = LANES * CAP
    return pl.pallas_call(
        gather_kernel,
        out_shape=(
            jax.ShapeDtypeStruct((slots, LANES), BF16),
            jax.ShapeDtypeStruct((LANES // GROUP, LANES), I32),
        ),
        in_specs=[VMEM, ANY],
        out_specs=(ANY, VMEM),
        scratch_shapes=[
            pltpu.VMEM(table.shape, F32),
            pltpu.VMEM((slots, 256), BF16),
            pltpu.VMEM((slots, LANES), I32),
            pltpu.VMEM((slots, LANES), BF16),
            pltpu.SemaphoreType.DMA((4,)),
            pltpu.SemaphoreType.DMA((slots // 512,)),
        ],
        name="gather_rows",
    )(got, table)


def paper_kernel(got, paper, rows):
    devs = LANES
    sub = iota((devs, LANES), 0)
    lane = iota((devs, LANES), 1)
    first = ((sub % GROUP + 1) % GROUP) * CAP
    width = paper.shape[1]
    for t in range(FCAP):
        asked = jnp.sum(jnp.where(lane == first + t, got[...], 0), axis=1, keepdims=True)
        hot = onehot(asked == iota((devs, paper.shape[0]), 1))
        rows[:, t * width : (t + 1) * width] = dot(hot, paper[...]).astype(BF16)


def paper_rows(got, paper):
    return pl.pallas_call(
        paper_kernel,
        out_shape=jax.ShapeDtypeStruct((LANES, FCAP * paper.shape[1]), BF16),
        in_specs=[VMEM, VMEM],
        out_specs=VMEM,
        cost_estimate=pl.CostEstimate(
            flops=2 * FCAP * LANES * paper.shape[0] * paper.shape[1],
            bytes_accessed=4 * paper.size,
            transcendentals=0,
        ),
        name="gather_papers",
    )(got, paper)


def layer_kernel(
    fetched, seed_of, cnt, pre_in, w_in, cot_in, agg_out, dpre_out, grad_out, pre_self, w_rel, cot, sems
):
    copies = fetch([(w_in, w_rel), (pre_in, pre_self), (cot_in, cot)], sems)
    devs = LANES
    lines = seed_of.shape[0]
    seed1 = iota((devs, LANES), 0) + 1
    agg = jnp.zeros((devs, LANES), F32)
    for b in range(0, lines, 2):
        match = jnp.concatenate(
            [onehot(seed1 == seed_of[b : b + 1, :]), onehot(seed1 == seed_of[b + 1 : b + 2, :])],
            axis=1,
        )
        agg = agg + dot(match, fetched[b * LANES : (b + 2) * LANES, :])
    count = cnt[...]
    agg_b = (agg / count).astype(BF16)
    agg_out[...] = agg_b
    for c in copies:
        c.wait()
    pre = pre_self[...] + dot(agg_b, w_rel[...])
    sig = jax.nn.sigmoid(pre)
    dpre = (cot[...] * sig * (1.0 + pre * (1.0 - sig))).astype(BF16)
    dpre_out[...] = dpre
    dagg = dot(dpre, w_rel[...], ((1,), (1,)))
    grad_out[...] = (dagg / count).astype(BF16)


def layer(fetched, seed_of, cnt, pre_self, w_rel, cotangent):
    seeds, hidden = cotangent.shape
    return pl.pallas_call(
        layer_kernel,
        out_shape=(
            jax.ShapeDtypeStruct((seeds, LANES), BF16),
            jax.ShapeDtypeStruct((seeds, hidden), BF16),
            jax.ShapeDtypeStruct((seeds, LANES), BF16),
        ),
        in_specs=[VMEM, VMEM, VMEM, ANY, ANY, ANY],
        out_specs=(VMEM, VMEM, VMEM),
        scratch_shapes=[
            pltpu.VMEM(pre_self.shape, F32),
            pltpu.VMEM(w_rel.shape, BF16),
            pltpu.VMEM(cotangent.shape, F32),
            pltpu.SemaphoreType.DMA((3,)),
        ],
        name="layer",
    )(fetched, seed_of, cnt, pre_self, w_rel, cotangent)


def slots_kernel(seed_of, grad, papers, bundle, out_scr, sems):
    paper_copy = pltpu.make_async_copy(
        papers, bundle.at[:, pl.ds(PAPER_AT, PAPER_ROWS), :], sems.at[0]
    )
    paper_copy.start()
    lines = seed_of.shape[0]
    seeds_t = seed_of[...].T
    lane1 = iota((LANES, LANES), 1) + 1
    copies = []
    per = 8
    for b in range(lines):
        match = onehot(seeds_t[:, b : b + 1] == lane1)
        out_scr[b * GROUP : (b + 1) * GROUP] = (
            dot(match, grad[...]).astype(BF16).reshape(GROUP, CAP, LANES)
        )
        if b % per == per - 1:
            at = pl.ds((b - per + 1) * GROUP, per * GROUP)
            copy = pltpu.make_async_copy(
                out_scr.at[at], bundle.at[at, pl.ds(0, CAP), :], sems.at[1 + b // per]
            )
            copy.start()
            copies.append(copy)
    for c in copies:
        c.wait()
    paper_copy.wait()


def slot_grads(seed_of, grad, papers):
    return pl.pallas_call(
        slots_kernel,
        out_shape=jax.ShapeDtypeStruct((LANES, BUNDLE, LANES), BF16),
        in_specs=[VMEM, VMEM, ANY],
        out_specs=ANY,
        scratch_shapes=[
            pltpu.VMEM((LANES, CAP, LANES), BF16),
            pltpu.SemaphoreType.DMA((5,)),
        ],
        cost_estimate=pl.CostEstimate(
            flops=2 * LANES * CAP * LANES * LANES, bytes_accessed=4 << 20, transcendentals=0
        ),
        name="slot_grads",
    )(seed_of, grad, papers)


def weight_kernel(feats_t, agg0, agg1, dpre0, dpre1, bundle_in, bundle, out_scr, sems):
    del bundle_in
    right = jnp.concatenate([dpre0[...], dpre1[...]], axis=0)
    aggs = jnp.concatenate([agg0[...], agg1[...]], axis=0)
    emb = aggs.shape[1]
    blocks = LANES // (right.shape[1] // LANES)
    per = emb // blocks
    where = iota((2 * emb, emb), 0)
    twice = onehot((where // (2 * per)) * per + where % per == iota((2 * emb, emb), 1))
    aggs_t = dot(twice, aggs, ((1,), (1,))).astype(BF16)
    copies = []
    rows_f = feats_t.shape[0] // blocks
    for cb in range(right.shape[1] // LANES):
        cols = right[:, cb * LANES : (cb + 1) * LANES]
        part_f = dot(feats_t[...], cols).astype(BF16)
        part_a = dot(aggs_t, cols)
        rest = part_a - part_a.astype(BF16).astype(F32)
        part_a = jnp.where(iota(part_a.shape, 0) % (2 * per) < per, part_a, rest).astype(BF16)
        for i in range(blocks):
            out_scr[cb * blocks + i] = jnp.concatenate(
                [
                    part_f[i * rows_f : (i + 1) * rows_f],
                    part_a[i * 2 * per : (i + 1) * 2 * per],
                ],
                axis=0,
            )
        at = pl.ds(cb * blocks, blocks)
        copy = pltpu.make_async_copy(
            out_scr.at[at], bundle.at[at, pl.ds(CAP, WEIGHT_ROWS), :], sems.at[cb]
        )
        copy.start()
        copies.append(copy)
    for c in copies:
        c.wait()


def weight_part(feats_t, agg0, agg1, dpre0, dpre1, bundle):
    return pl.pallas_call(
        weight_kernel,
        out_shape=jax.ShapeDtypeStruct(bundle.shape, BF16),
        in_specs=[VMEM] * 5 + [ANY],
        out_specs=ANY,
        scratch_shapes=[
            pltpu.VMEM((LANES, WEIGHT_ROWS, LANES), BF16),
            pltpu.SemaphoreType.DMA((dpre0.shape[1] // LANES,)),
        ],
        input_output_aliases={5: 0},
        name="weight_part",
    )(feats_t, agg0, agg1, dpre0, dpre1, bundle)


def sum_kernel(bundle, out, parts, out_scr, sems):
    step = LANES // 4
    copies = fetch(
        [
            (
                bundle.at[pl.ds(i * step, step), pl.ds(CAP, WEIGHT_ROWS), :],
                parts.at[pl.ds(i * step, step)],
            )
            for i in range(4)
        ],
        sems,
    )
    half = [jnp.zeros((WEIGHT_ROWS, LANES), F32) for _ in range(2)]
    for i in range(4):
        copies[i].wait()
        for d in range(i * step, (i + 1) * step):
            c = (d // GROUP) % 2
            half[c] = half[c] + parts[d].astype(F32)
    per = (WEIGHT_ROWS - SELF_ROWS) // 2
    rel = [h[SELF_ROWS : SELF_ROWS + per] + h[SELF_ROWS + per :] for h in half]
    mine = jnp.concatenate([half[0][:SELF_ROWS], half[1][:SELF_ROWS], rel[0], rel[1]], axis=0)
    mine = mine.astype(BF16)
    for i in range(out_scr.shape[0]):
        out_scr[i] = mine
    q = out_scr.shape[0] // 4
    copies = fetch(
        [(out_scr.at[pl.ds(i * q, q)], out.at[pl.ds(i * q, q)]) for i in range(4)], sems
    )
    for c in copies:
        c.wait()


def sum_parts(bundle, peers):
    rows = WEIGHT_ROWS + SELF_ROWS
    return pl.pallas_call(
        sum_kernel,
        out_shape=jax.ShapeDtypeStruct((peers, rows, LANES), BF16),
        in_specs=[ANY],
        out_specs=ANY,
        scratch_shapes=[
            pltpu.VMEM((LANES, WEIGHT_ROWS, LANES), BF16),
            pltpu.VMEM((peers, rows, LANES), BF16),
            pltpu.SemaphoreType.DMA((4,)),
        ],
        name="sum_parts",
    )(bundle)


def spread_kernel(core, mine, other, grad_self, grad_rel):
    first = core[0] == 0
    half = pl.program_id(1)
    per = grad_rel.shape[0] // 32
    chips = mine.shape[0] // GROUP
    rel = []
    for chip in range(chips):
        for c in range(2):
            for mp in range(GROUP):
                src = chip * GROUP + mp
                own = mine[src].astype(F32)
                far = other[src].astype(F32)
                got = jnp.where(first, own, far) if c == 0 else jnp.where(first, far, own)
                i = (chip * 2 + c) * GROUP + mp
                grad_self[i * SELF_ROWS : (i + 1) * SELF_ROWS, :] = jnp.where(
                    half == 0, got[:SELF_ROWS], got[SELF_ROWS : 2 * SELF_ROWS]
                )
                at = 2 * SELF_ROWS
                rel.append(jnp.where(half == 0, got[at : at + per], got[at + per : at + 2 * per]))
    grad_rel[...] = jnp.concatenate(rel, axis=0)


def spread(core, mine, other, feats, emb, hidden):
    blocks = hidden // LANES // 2
    peers, rows, _ = mine.shape
    block = pl.BlockSpec((peers // blocks, rows, LANES), lambda c, h: (c, 0, 0))
    return pl.pallas_call(
        spread_kernel,
        grid=(blocks, 2),
        out_shape=(
            jax.ShapeDtypeStruct((feats, hidden), F32),
            jax.ShapeDtypeStruct((emb, hidden), F32),
        ),
        in_specs=[SMEM, block, block],
        out_specs=(
            pl.BlockSpec((feats, LANES), lambda c, h: (0, h * blocks + c)),
            pl.BlockSpec((emb, LANES), lambda c, h: (0, h * blocks + c)),
        ),
        name="weight_out",
    )(core, mine, other)


def adam_kernel(
    wanted, bundle, table, m1, m2, new_table, new_m1, new_m2, arrived, hot_scr, side_scr, sem
):
    step = pl.program_id(0)
    lines = wanted.shape[0]

    @pl.when(step == 0)
    def _():
        copy = pltpu.make_async_copy(bundle.at[:, pl.ds(0, CAP), :], arrived, sem.at[0])
        copy.start()
        lo = wanted[...] % 256
        hi = (wanted[...] // 256).astype(F32).T
        sub = iota((256, LANES), 0)
        for b in range(lines):
            at = slice(b * LANES, (b + 1) * LANES)
            hot_scr[:, at] = onehot(sub == lo[b : b + 1, :])
            side_scr[at, :] = jnp.broadcast_to(hi[:, b : b + 1], (LANES, LANES)).astype(BF16)
        copy.wait()

    here = side_scr[...] == step.astype(F32).astype(BF16)
    mark = jnp.where(here, BF16(1.0), BF16(0.0))
    got = arrived[...].reshape(LANES * CAP, LANES)
    both = dot(hot_scr[...], jnp.concatenate([got * mark, mark], axis=1))
    grad = both[:, :LANES]
    touched = both[:, LANES:] > 0.0
    m = 0.9 * m1[...] + 0.1 * grad
    v = 0.999 * m2[...] + 0.001 * grad * grad
    update = 0.05 * (m / (1.0 - 0.9**10)) / (jnp.sqrt(v / (1.0 - 0.999**10)) + 1e-08)
    new_table[...] = jnp.where(touched, table[...] - update, table[...])
    new_m1[...] = jnp.where(touched, m, m1[...])
    new_m2[...] = jnp.where(touched, v, m2[...])


def adam(wanted, bundle, table, m1, m2):
    rows = 256
    block = pl.BlockSpec((rows, LANES), lambda i: (i, 0))
    slots = LANES * CAP
    return pl.pallas_call(
        adam_kernel,
        grid=(table.shape[0] // rows,),
        out_shape=(jax.ShapeDtypeStruct(table.shape, F32),) * 3,
        in_specs=[pl.BlockSpec(wanted.shape, lambda i: (0, 0)), ANY, block, block, block],
        out_specs=(block, block, block),
        scratch_shapes=[
            pltpu.VMEM((LANES, CAP, LANES), BF16),
            pltpu.VMEM((rows, slots), BF16),
            pltpu.VMEM((slots, LANES), BF16),
            pltpu.SemaphoreType.DMA((1,)),
        ],
        cost_estimate=pl.CostEstimate(
            flops=2 * 2 * slots * LANES * table.shape[0],
            bytes_accessed=7 << 20,
            transcendentals=0,
        ),
        name="adam",
    )(wanted, bundle, table, m1, m2)


def shards(
    feats,
    edge_owner,
    edge_row,
    counts,
    table,
    moment1,
    moment2,
    w_self,
    w_rel,
    cotangent,
    next_owner,
    next_row,
    paper_table,
):
    every = ("chip", "core", "mp")
    peers = ("chip", "mp")
    devs = lax.axis_size(every)
    seeds, width = feats.shape
    hidden = cotangent.shape[1]
    emb = table.shape[1]
    core = lax.axis_index("core")
    group = lax.axis_index("mp").astype(I32).reshape(1)

    def exchange(a, axes):
        return lax.all_to_all(a, axes, split_axis=0, concat_axis=0, tiled=True)

    def swap(a):
        return lax.ppermute(a, "core", [(0, 1), (1, 0)])

    asked, seed_of, cnt, paper_pick = place(
        group,
        edge_owner.reshape(-1, LANES),
        edge_row.reshape(-1, LANES),
        counts.reshape(1, -1),
        next_owner.reshape(1, -1),
        next_row.reshape(1, -1),
    )
    got = exchange(asked.reshape(devs, 1, LANES), every).reshape(devs, LANES)
    rows, wanted = gather(got, table)
    fetched = exchange(rows.reshape(devs, CAP, emb), every).reshape(devs * CAP, emb)

    pre_self = jnp.dot(feats, w_self, preferred_element_type=F32)
    feats_t = jnp.concatenate([feats, swap(feats)], axis=0).T
    papers = paper_rows(got, paper_table).reshape(devs, -1, LANES)
    papers = jnp.pad(papers, ((0, 0), (0, PAPER_ROWS - papers.shape[1]), (0, 0)))
    agg_b, dpre, grad = layer(fetched, seed_of, cnt, pre_self, w_rel, cotangent)

    half = hidden // 2
    dpre_here = lax.dynamic_slice_in_dim(dpre, core * half, half, 1)
    dpre_there = lax.dynamic_slice_in_dim(dpre, (1 - core) * half, half, 1)
    agg_far, dpre_far = swap(agg_b), swap(dpre_there)
    bundle = slot_grads(seed_of, grad, papers)
    bundle = weight_part(feats_t, agg_b, agg_far, dpre_here, dpre_far, bundle)
    bundle = exchange(bundle, every)
    full = exchange(sum_parts(bundle, lax.axis_size(peers)), peers)
    new_table, new_moment1, new_moment2 = adam(wanted, bundle, table, moment1, moment2)
    grad_self, grad_rel = spread(
        core.astype(I32).reshape(1), full, swap(full), width, emb, hidden
    )

    papers = bundle[:, PAPER_AT : PAPER_AT + FCAP * width // LANES, :].reshape(devs, -1)
    next_feats = functools.reduce(
        lambda a, b: a + b,
        [
            lax.dot_general(
                paper_pick[t],
                papers[:, t * width : (t + 1) * width],
                (((0,), (0,)), ((), ())),
                preferred_element_type=F32,
            )
            for t in range(FCAP)
        ],
    ).astype(BF16)
    return (new_table, new_moment1, new_moment2, grad_self, grad_rel, next_feats)


def solution(mesh):
    n_mp = mesh.shape["mp"]
    wide = Mesh(mesh.devices.reshape(-1, 2, n_mp), ("chip", "core", "mp"))
    rows = P(("chip", "core", "mp"), None)
    line = P(("chip", "core", "mp"))
    in_specs = (rows, rows, line, line, rows, rows, rows, P(), P(), rows, rows, line, rows)
    out_specs = (rows, rows, rows, P(), P(), rows)
    return jax.shard_map(shards, mesh=wide, in_specs=in_specs, out_specs=out_specs, check_vma=False)
```

time: 170 us -> 171 us (level)
  waiting for transfers between devices: 59.3 us -> 11 us
  blocking collectives: 41.3 us -> 83.9 us
  Pallas kernels: 25.6 us -> 55.4 us
  starting transfers between devices: 26 us -> 7.81 us
  local copies, waits for them, and re-layouts: 13.2 us -> 7.02 us
    all_to_all x4 -> x1, waiting for transfers between devices: 58.2 us -> 10.9 us  [exchange(): return lax.all_to_all(a, axes, split_axis=0, concat_axis=0, tiled=True)]
    all_to_all x2 -> x3, blocking collectives: 41.3 us -> 83.9 us  [exchange(): return lax.all_to_all(a, axes, split_axis=0, concat_axis=0, tiled=True)]
    pallas_call x4 -> x6, Pallas kernels: 9.27 us -> 35.7 us  [the longest x1 17.8 us: slot_grads(): pl.pallas_call(slots_kernel, out_shape=jax.ShapeDtypeStruct((LANES, BUNDL...]
    all_to_all x4 -> x1, starting transfers between devices: 22.7 us -> 4.26 us  [exchange(): return lax.all_to_all(a, axes, split_axis=0, concat_axis=0, tiled=True)]
    unnamed x34 -> x15, local copies, waits for them, and re-layouts: 10.1 us -> 2.46 us
    transpose x0 -> x1, other arithmetic: none -> 1.81 us  [shards(): feats_t = jnp.concatenate([feats, swap(feats)], axis=0).T]
  transfers between devices with their start and end apart: 8 -> 5, of which waited for: 5 -> 1; matrix products, arithmetic and copies ran while one was open for 3% -> 6% of each run, Pallas kernels for 8% -> 21%
where the time goes in v2:
time: 171 us; the launch traced here: 170 us
  blocking collectives  83.9 us (49%)
  Pallas kernels  55.4 us (32%)
  waiting for transfers between devices  11 us (6%)
  starting transfers between devices  7.81 us (5%)
  local copies, waits for them, and re-layouts  7.02 us (4%)
  matrix products  2.32 us (1%)
  other arithmetic  1.81 us (1%)
    all_to_all x3, blocking collectives, exchange(): return lax.all_to_all(a, axes, split_axis=0, concat_axis=0, tiled=True)  83.9 us
    pallas_call x1, Pallas kernels, slot_grads(): pl.pallas_call(slots_kernel, out_shape=jax.ShapeDtypeStruct((LANES, BUNDL...  17.8 us
    all_to_all x1, waiting for transfers between devices, exchange(): return lax.all_to_all(a, axes, split_axis=0, concat_axis=0, tiled=True)  10.9 us
    pallas_call x1, Pallas kernels, adam(): pl.pallas_call(adam_kernel, grid=(table.shape[0] // rows,), out_shape=(ja...  10.8 us
    pallas_call x1, Pallas kernels, spread(): pl.pallas_call(spread_kernel, grid=(blocks, 2), out_shape=(jax.ShapeDtype...  6.48 us
    pallas_call x1, Pallas kernels, gather(): pl.pallas_call(gather_kernel, out_shape=(jax.ShapeDtypeStruct((slots, LAN...  5.88 us
    all_to_all x1, starting transfers between devices, exchange(): return lax.all_to_all(a, axes, split_axis=0, concat_axis=0, tiled=True)  4.26 us
    pallas_call x1, Pallas kernels, layer(): pl.pallas_call(layer_kernel, out_shape=(jax.ShapeDtypeStruct((seeds, LANE...  3.61 us
  transfers between devices with their start and end apart: 5, of which 1 were waited for; matrix products, arithmetic and copies ran while one was open for 6% of the time, Pallas kernels for 21%

profile of v2, /device:TPU:1, one launch (start us, length us, event | category | flops | bytes accessed | tf_op | source)
XLA Modules:
  0.0 169.9 jit_solution(14492499435820745645)
XLA Ops:
  0.7 3.1 %place.1 = (s32[128,128]{1,0:T(8,128)}, s32[32,128]{1,0:T(8,128)}, f32[128,128]{1,0:T(8,128)}, bf16[2,128,128]{2,1,0:T(8,128)(2,1)}) custom-call(s32[1]{0:T(128)} %bitcast.lane_group, s32[16,128]{1,0:T(8,128)} %bitcast.33, s32[16,128]{1,0:T(8,128)} %bitcast.34, s32[1,128]{1,0:T(1,128)} %bitcast.35, s32[1,128]{1,0:T(1,128)} %bitcast.36, s32[1,128]{1,0:T(1,128)} %bitcast.37), custom_call_target="tpu_custom_call" | custom-call | tf_op jit(solution)/shard_map/place/pallas_call | solution.py:161
  3.7 21.5 %all_to_all.20 = s32[128,1,128]{2,1,0:T(1,128)} all-to-all(s32[128,1,128]{2,1,0:T(1,128)} %bitcast.32), channel_id=1, replica_groups=mesh['chip'=16,'core'=2,'mp'=4] {'chip','core','mp'}, dimensions={0} | all-to-all | bytes 131072 | tf_op jit(solution)/shard_map/all_to_all | solution.py:596
  25.2 5.9 %gather_rows.1 = (bf16[4096,128]{1,0:T(8,128)(2,1)}, s32[32,128]{1,0:T(8,128)}) custom-call(s32[128,128]{1,0:T(8,128)} %bitcast.30, f32[2048,128]{1,0:T(8,128)} %table.1), custom_call_target="tpu_custom_call" | custom-call | tf_op jit(solution)/shard_map/gather_rows/pallas_call | solution.py:233
  31.1 4.3 %all-to-all-start.1 = ((bf16[128,32,128]{2,1,0:T(8,128)(2,1)}), bf16[128,32,128]{2,1,0:T(8,128)(2,1)S(1)}, u32[]{:S(2)}, u32[]{:S(2)}) async-start(bf16[128,32,128]{2,1,0:T(8,128)(2,1)} %bitcast.29), calls=%async_computation.1 | async-start | bytes 2097152 | tf_op jit(solution)/shard_map/all_to_all | solution.py:596
  35.4 0.8 copy.29
  36.2 1.1 collective-permute-start
  37.3 1.2 fusion.8.pre_in
  38.4 2.9 %gather_papers.1 = bf16[128,1536]{1,0:T(8,128)(2,1)} custom-call(s32[128,128]{1,0:T(8,128)} %bitcast.31, bf16[1024,768]{1,0:T(8,128)(2,1)} %paper.1), custom_call_target="tpu_custom_call" | custom-call | flops 402653184 | bytes 3145728 | tf_op jit(solution)/shard_map/gather_papers/pallas_call | solution.py:266
  41.3 1.2 copy.30
  43.0 0.9 pad.4.papers
  43.9 10.9 %all-to-all-done.1 = bf16[128,32,128]{2,1,0:T(8,128)(2,1)S(1)} async-done(((bf16[128,32,128]{2,1,0:T(8,128)(2,1)}), bf16[128,32,128]{2,1,0:T(8,128)(2,1)S(1)}, u32[]{:S(2)}, u32[]{:S(2)}) %all-to-all-start.1) | async-done | bytes 1048608 | tf_op jit(solution)/shard_map/all_to_all | solution.py:596
  54.8 1.0 copy-done.1
  55.8 3.6 %layer.1 = (bf16[128,128]{1,0:T(8,128)(2,1)}, bf16[128,1024]{1,0:T(8,128)(2,1)}, bf16[128,128]{1,0:T(8,128)(2,1)}) custom-call(bf16[4096,128]{1,0:T(8,128)(2,1)} %bitcast.25, s32[32,128]{1,0:T(8,128)} %get-tuple-element.23.seed_of, f32[128,128]{1,0:T(8,128)} %get-tuple-element.24.cnt, f32[128,1024]{1,0:T(8,128)} %fusion.8.pre_in, bf16[128,1024]{1,0:T(8,128)(2,1)} %w_in.1, ...), custom_call_target="tpu_custom_call" | custom-call | tf_op jit(solution)/shard_map/layer/pallas_call | solution.py:309
  59.9 1.6 constant_dynamic-slice_fusion
  61.6 1.8 %maximum_bitcast_fusion.feats_t = bf16[768,256]{1,0:T(8,128)(2,1)} fusion(bf16[128,768]{0,1:T(8,128)(2,1)} %collective-permute-done, bf16[128,768]{0,1:T(8,128)(2,1)} %copy.29), kind=kLoop, calls=%fused_computation.2 | loop fusion | flops 786432 | bytes 786432 | tf_op jit(solution)/shard_map/transpose | solution.py:614
  63.4 17.8 %slot_grads.1.bundle_in = bf16[128,80,128]{2,1,0:T(8,128)(2,1)} custom-call(s32[32,128]{1,0:T(8,128)} %get-tuple-element.23.seed_of, bf16[128,128]{1,0:T(8,128)(2,1)} %get-tuple-element.27.grad, bf16[128,16,128]{2,1,0:T(8,128)(2,1)} %pad.4.papers), custom_call_target="tpu_custom_call" | custom-call | flops 134217728 | bytes 4194304 | tf_op jit(solution)/shard_map/slot_grads/pallas_call | solution.py:356
  81.9 2.7 %weight_part.1 = bf16[128,80,128]{2,1,0:T(8,128)(2,1)} custom-call(bf16[768,256]{1,0:T(8,128)(2,1)} %maximum_bitcast_fusion.feats_t, bf16[128,128]{1,0:T(8,128)(2,1)} %get-tuple-element.25.agg0, bf16[128,128]{1,0:T(8,128)(2,1)} %copy-done.6, bf16[128,512]{1,0:T(8,128)(2,1)} %get-tuple-element.35.dpre0, ...), custom_call_target="tpu_custom_call", output_to_operand_aliasing={{}: (5, {})} | custom-call | tf_op jit(solution)/shard_map/weight_part/pallas_call | solution.py:409
  84.6 41.1 %all_to_all.21.bundle = bf16[128,80,128]{2,1,0:T(8,128)(2,1)} all-to-all(bf16[128,80,128]{2,1,0:T(8,128)(2,1)} %weight_part.1), channel_id=1, replica_groups=mesh['chip'=16,'core'=2,'mp'=4] {'chip','core','mp'}, dimensions={0} | all-to-all | bytes 5242880 | tf_op jit(solution)/shard_map/all_to_all | solution.py:596
  125.7 2.2 %sum_parts.1 = bf16[64,56,128]{2,1,0:T(8,128)(2,1)} custom-call(bf16[128,80,128]{2,1,0:T(8,128)(2,1)} %all_to_all.21.bundle), custom_call_target="tpu_custom_call" | custom-call | tf_op jit(solution)/shard_map/sum_parts/pallas_call | solution.py:457
  128.0 21.3 %all_to_all.22.mine = bf16[64,56,128]{2,1,0:T(8,128)(2,1)S(1)} all-to-all(bf16[64,56,128]{2,1,0:T(8,128)(2,1)} %sum_parts.1), channel_id=1, replica_groups=mesh['chip'=16,'core'=2,'mp'=4] {'chip','mp'}, dimensions={0} | all-to-all | bytes 1835008 | tf_op jit(solution)/shard_map/all_to_all | solution.py:596
  149.2 1.9 %collective-permute-start.3 = (bf16[64,56,128]{2,1,0:T(8,128)(2,1)S(1)}, bf16[64,56,128]{2,1,0:T(8,128)(2,1)}, u32[]{:S(2)}, u32[]{:S(2)}) collective-permute-start(bf16[64,56,128]{2,1,0:T(8,128)(2,1)S(1)} %all_to_all.22.mine), channel_id=1, source_target_pairs={{0,4},{4,0},{1,5},{5,1},{2,6},{6,2},{3,7},{7,3},{8,12},{12,8},{9,1... | collective-permute-start | bytes 2752520 | tf_op jit(solution)/shard_map/ppermute | solution.py:599
  151.7 0.9 fusion
  152.7 10.8 %adam.1 = (f32[2048,128]{1,0:T(8,128)}, f32[2048,128]{1,0:T(8,128)}, f32[2048,128]{1,0:T(8,128)}) custom-call(s32[32,128]{1,0:T(8,128)} %get-tuple-element.21.wanted, bf16[128,80,128]{2,1,0:T(8,128)(2,1)} %all_to_all.21.bundle, f32[2048,128]{1,0:T(8,128)} %table.1, f32[2048,128]{1,0:T(8,128)} %m1.1, f32[2048,128]{1,0:T(8,128)} %m2.1), custom_call_target="tpu_custom_call" | custom-call | flops 4294967296 | bytes 7340032 | tf_op jit(solution)/shard_map/adam/pallas_call | solution.py:550
  163.5 6.5 %weight_out.1 = (f32[768,1024]{1,0:T(8,128)}, f32[128,1024]{1,0:T(8,128)}) custom-call(s32[1]{0:T(128)} %bitcast.13.core, bf16[64,56,128]{2,1,0:T(8,128)(2,1)} %copy-done.2, bf16[64,56,128]{2,1,0:T(8,128)(2,1)} %collective-permute-done.3.other), custom_call_target="tpu_custom_call" | custom-call | tf_op jit(solution)/shard_map/weight_out/pallas_call | solution.py:497
  (24 shorter events, 2.3 us)
Async XLA Ops:
  0.6 36.6 %copy-start = (bf16[768,1024]{1,0:T(8,128)(2,1)S(1)}, bf16[768,1024]{1,0:T(8,128)(2,1)}, u32[]{:S(2)}) copy-start(bf16[768,1024]{1,0:T(8,128)(2,1)} %param.20) | copy-start | bytes 4718596
  25.2 10.2 %copy-start.3 = (bf16[128,768]{1,0:T(8,128)(2,1)S(1)}, bf16[128,768]{1,0:T(8,128)(2,1)}, u32[]{:S(2)}) copy-start(bf16[128,768]{1,0:T(8,128)(2,1)} %param.13) | copy-start | bytes 589828
  31.1 23.7 %all-to-all-start.1 = ((bf16[128,32,128]{2,1,0:T(8,128)(2,1)}), bf16[128,32,128]{2,1,0:T(8,128)(2,1)S(1)}, u32[]{:S(2)}, u32[]{:S(2)}) async-start(bf16[128,32,128]{2,1,0:T(8,128)(2,1)} %bitcast.29), calls=%async_computation.1 | async-start | bytes 2097152 | tf_op jit(solution)/shard_map/all_to_all | solution.py:596
  36.2 25.4 %collective-permute-start = (bf16[128,768]{0,1:T(8,128)(2,1)}, bf16[128,768]{0,1:T(8,128)(2,1)}, u32[]{:S(2)}, u32[]{:S(2)}) collective-permute-start(bf16[128,768]{0,1:T(8,128)(2,1)} %copy.29), channel_id=1, source_target_pairs={{0,4},{4,0},{1,5},{5,1},{2,6},{6,2},{3,7},{7,3},{8,12},{12,8},{9,1... | collective-permute-start | bytes 589832 | tf_op jit(solution)/shard_map/ppermute | solution.py:599
  54.8 1.0 copy-start.1
  59.4 21.9 %collective-permute-start.1 = (bf16[128,128]{1,0:T(8,128)(2,1)}, bf16[128,128]{1,0:T(8,128)(2,1)S(1)}, u32[]{:S(2)}, u32[]{:S(2)}) collective-permute-start(bf16[128,128]{1,0:T(8,128)(2,1)} %get-tuple-element.25.agg0), channel_id=1, source_target_pairs={{0,4},{4,0},{1,5},{5,1},{2,6},{6,2},{3,7},{7,3},{8,12},{12,8},{9,1... | collective-permute-start | bytes 98312 | tf_op jit(solution)/shard_map/ppermute | solution.py:599
  61.5 19.8 %collective-permute-start.2 = (bf16[128,512]{1,0:T(8,128)(2,1)S(1)}, bf16[128,512]{1,0:T(8,128)(2,1)S(1)}, u32[]{:S(2)}, u32[]{:S(2)}) collective-permute-start(bf16[128,512]{1,0:T(8,128)(2,1)S(1)} %get-tuple-element.34), channel_id=1, source_target_pairs={{0,4},{4,0},{1,5},{5,1},{2,6},{6,2},{3,7},{7,3},{8,12},{12,8},{9,1... | collective-permute-start | bytes 393224 | tf_op jit(solution)/shard_map/ppermute | solution.py:599
  81.2 0.6 copy-start.6
  81.3 0.7 copy-start.4
  127.9 23.2 %slice-start = ((bf16[128,80,128]{2,1,0:T(8,128)(2,1)}), bf16[128,12,128]{2,1,0:T(8,128)(2,1)S(1)}, s32[]{:S(2)}) async-start(bf16[128,80,128]{2,1,0:T(8,128)(2,1)} %all_to_all.21.bundle), calls=%async_computation.4 | async-start | bytes 1048576 | tf_op jit(solution)/shard_map/slice | solution.py:632
  127.9 23.6 %copy-start.5 = (bf16[2,128,128]{2,1,0:T(8,128)(2,1)S(1)}, bf16[2,128,128]{2,1,0:T(8,128)(2,1)}, u32[]{:S(2)}) copy-start(bf16[2,128,128]{2,1,0:T(8,128)(2,1)} %get-tuple-element.33) | copy-start | bytes 196612
  149.2 3.4 %copy-start.2 = (bf16[64,56,128]{2,1,0:T(8,128)(2,1)}, bf16[64,56,128]{2,1,0:T(8,128)(2,1)S(1)}, u32[]{:S(2)}) copy-start(bf16[64,56,128]{2,1,0:T(8,128)(2,1)S(1)} %all_to_all.22.mine) | copy-start | bytes 2752516
  149.2 14.2 %collective-permute-start.3 = (bf16[64,56,128]{2,1,0:T(8,128)(2,1)S(1)}, bf16[64,56,128]{2,1,0:T(8,128)(2,1)}, u32[]{:S(2)}, u32[]{:S(2)}) collective-permute-start(bf16[64,56,128]{2,1,0:T(8,128)(2,1)S(1)} %all_to_all.22.mine), channel_id=1, source_target_pairs={{0,4},{4,0},{1,5},{5,1},{2,6},{6,2},{3,7},{7,3},{8,12},{12,8},{9,1... | collective-permute-start | bytes 2752520 | tf_op jit(solution)/shard_map/ppermute | solution.py:599

commit v3 on v2

--- a/solution.py
+++ b/solution.py
@@ -36,6 +36,11 @@
     return jnp.where(mask, F32(1.0), F32(0.0)).astype(BF16)
 
 ANY = pl.BlockSpec(memory_space=pl.ANY)
+HBM = pl.BlockSpec(memory_space=pltpu.HBM)
+
+
+def params():
+    return pltpu.CompilerParams(vmem_limit_bytes=24 * 1024 * 1024)
 
 
 def fetch(pairs, sems):
@@ -166,7 +171,7 @@
             jax.ShapeDtypeStruct((devs, LANES), F32),
             jax.ShapeDtypeStruct((FCAP, devs, LANES), BF16),
         ),
-        in_specs=[SMEM] + [ANY] * len(ins),
+        in_specs=[SMEM] + [HBM] * len(ins),
         out_specs=(VMEM, VMEM, VMEM, VMEM),
         scratch_shapes=[pltpu.VMEM(a.shape, I32) for a in ins]
         + [pltpu.VMEM((devs, LANES), I32), pltpu.SemaphoreType.DMA((len(ins),))],
@@ -236,8 +241,8 @@
             jax.ShapeDtypeStruct((slots, LANES), BF16),
             jax.ShapeDtypeStruct((LANES // GROUP, LANES), I32),
         ),
-        in_specs=[VMEM, ANY],
-        out_specs=(ANY, VMEM),
+        in_specs=[VMEM, HBM],
+        out_specs=(HBM, VMEM),
         scratch_shapes=[
             pltpu.VMEM(table.shape, F32),
             pltpu.VMEM((slots, 256), BF16),
@@ -250,12 +255,14 @@
     )(got, table)
 
 
-def paper_kernel(got, paper, rows):
+def paper_kernel(got, paper_in, rows, paper, sems):
+    copies = fetch([(paper_in, paper)], sems)
     devs = LANES
     sub = iota((devs, LANES), 0)
     lane = iota((devs, LANES), 1)
     first = ((sub % GROUP + 1) % GROUP) * CAP
     width = paper.shape[1]
+    copies[0].wait()
     for t in range(FCAP):
         asked = jnp.sum(jnp.where(lane == first + t, got[...], 0), axis=1, keepdims=True)
         hot = onehot(asked == iota((devs, paper.shape[0]), 1))
@@ -266,8 +273,9 @@
     return pl.pallas_call(
         paper_kernel,
         out_shape=jax.ShapeDtypeStruct((LANES, FCAP * paper.shape[1]), BF16),
-        in_specs=[VMEM, VMEM],
+        in_specs=[VMEM, HBM],
         out_specs=VMEM,
+        scratch_shapes=[pltpu.VMEM(paper.shape, BF16), pltpu.SemaphoreType.DMA((1,))],
         cost_estimate=pl.CostEstimate(
             flops=2 * FCAP * LANES * paper.shape[0] * paper.shape[1],
             bytes_accessed=4 * paper.size,
@@ -277,10 +285,43 @@
     )(got, paper)
 
 
+def prep_kernel(feats, w_self, cot_in, w_in, pre, cot, w_rel, sems):
+    copies = fetch([(cot_in, cot), (w_in, w_rel)], sems)
+    pre[...] = dot(feats[...], w_self[...])
+    for c in copies:
+        c.wait()
+
+
+def prep(feats, w_self, cotangent, w_rel):
+    return pl.pallas_call(
+        prep_kernel,
+        out_shape=(
+            jax.ShapeDtypeStruct(cotangent.shape, F32),
+            jax.ShapeDtypeStruct(cotangent.shape, F32),
+            jax.ShapeDtypeStruct(w_rel.shape, BF16),
+        ),
+        in_specs=[VMEM, VMEM, ANY, ANY],
+        out_specs=(VMEM, VMEM, VMEM),
+        scratch_shapes=[pltpu.SemaphoreType.DMA((2,))],
+        compiler_params=params(),
+        cost_estimate=pl.CostEstimate(
+            flops=2 * feats.size * w_self.shape[1], bytes_accessed=4 << 20, transcendentals=0
+        ),
+        name="prep",
+    )(feats, w_self, cotangent, w_rel)
+
+
 def layer_kernel(
-    fetched, seed_of, cnt, pre_in, w_in, cot_in, agg_out, dpre_out, grad_out, pre_self, w_rel, cot, sems
+    core,
+    fetched,
+    seed_of,
+    cnt,
+    pre_self,
+    w_rel,
+    cot,
+    *rest,
 ):
-    copies = fetch([(w_in, w_rel), (pre_in, pre_self), (cot_in, cot)], sems)
+    agg_out, here_out, there_out, grad_out = rest[-4:]
     devs = LANES
     lines = seed_of.shape[0]
     seed1 = iota((devs, LANES), 0) + 1
@@ -294,35 +335,32 @@
     count = cnt[...]
     agg_b = (agg / count).astype(BF16)
     agg_out[...] = agg_b
-    for c in copies:
-        c.wait()
     pre = pre_self[...] + dot(agg_b, w_rel[...])
     sig = jax.nn.sigmoid(pre)
     dpre = (cot[...] * sig * (1.0 + pre * (1.0 - sig))).astype(BF16)
-    dpre_out[...] = dpre
+    half = dpre.shape[1] // 2
+    first = core[0] == 0
+    here_out[...] = jnp.where(first, dpre[:, :half], dpre[:, half:])
+    there_out[...] = jnp.where(first, dpre[:, half:], dpre[:, :half])
     dagg = dot(dpre, w_rel[...], ((1,), (1,)))
     grad_out[...] = (dagg / count).astype(BF16)
 
 
-def layer(fetched, seed_of, cnt, pre_self, w_rel, cotangent):
+def layer(core, fetched, seed_of, cnt, pre_self, w_rel, cotangent, *ready):
     seeds, hidden = cotangent.shape
     return pl.pallas_call(
         layer_kernel,
         out_shape=(
             jax.ShapeDtypeStruct((seeds, LANES), BF16),
-            jax.ShapeDtypeStruct((seeds, hidden), BF16),
+            jax.ShapeDtypeStruct((seeds, hidden // 2), BF16),
+            jax.ShapeDtypeStruct((seeds, hidden // 2), BF16),
             jax.ShapeDtypeStruct((seeds, LANES), BF16),
         ),
-        in_specs=[VMEM, VMEM, VMEM, ANY, ANY, ANY],
-        out_specs=(VMEM, VMEM, VMEM),
-        scratch_shapes=[
-            pltpu.VMEM(pre_self.shape, F32),
-            pltpu.VMEM(w_rel.shape, BF16),
-            pltpu.VMEM(cotangent.shape, F32),
-            pltpu.SemaphoreType.DMA((3,)),
-        ],
+        in_specs=[SMEM] + [VMEM] * 6 + [ANY] * len(ready),
+        out_specs=(VMEM, VMEM, VMEM, VMEM),
+        compiler_params=params(),
         name="layer",
-    )(fetched, seed_of, cnt, pre_self, w_rel, cotangent)
+    )(core, fetched, seed_of, cnt, pre_self, w_rel, cotangent, *ready)
 
 
 def slots_kernel(seed_of, grad, papers, bundle, out_scr, sems):
@@ -356,8 +394,8 @@
     return pl.pallas_call(
         slots_kernel,
         out_shape=jax.ShapeDtypeStruct((LANES, BUNDLE, LANES), BF16),
-        in_specs=[VMEM, VMEM, ANY],
-        out_specs=ANY,
+        in_specs=[VMEM, VMEM, VMEM],
+        out_specs=HBM,
         scratch_shapes=[
             pltpu.VMEM((LANES, CAP, LANES), BF16),
             pltpu.SemaphoreType.DMA((5,)),
@@ -365,6 +403,7 @@
         cost_estimate=pl.CostEstimate(
             flops=2 * LANES * CAP * LANES * LANES, bytes_accessed=4 << 20, transcendentals=0
         ),
+        compiler_params=params(),
         name="slot_grads",
     )(seed_of, grad, papers)
 
@@ -409,13 +448,14 @@
     return pl.pallas_call(
         weight_kernel,
         out_shape=jax.ShapeDtypeStruct(bundle.shape, BF16),
-        in_specs=[VMEM] * 5 + [ANY],
-        out_specs=ANY,
+        in_specs=[VMEM] * 5 + [HBM],
+        out_specs=HBM,
         scratch_shapes=[
             pltpu.VMEM((LANES, WEIGHT_ROWS, LANES), BF16),
             pltpu.SemaphoreType.DMA((dpre0.shape[1] // LANES,)),
         ],
         input_output_aliases={5: 0},
+        compiler_params=params(),
         name="weight_part",
     )(feats_t, agg0, agg1, dpre0, dpre1, bundle)
 
@@ -458,63 +498,84 @@
         sum_kernel,
         out_shape=jax.ShapeDtypeStruct((peers, rows, LANES), BF16),
         in_specs=[ANY],
-        out_specs=ANY,
+        out_specs=HBM,
         scratch_shapes=[
             pltpu.VMEM((LANES, WEIGHT_ROWS, LANES), BF16),
             pltpu.VMEM((peers, rows, LANES), BF16),
             pltpu.SemaphoreType.DMA((4,)),
         ],
+        compiler_params=params(),
         name="sum_parts",
     )(bundle)
 
 
 def spread_kernel(core, mine, other, grad_self, grad_rel):
     first = core[0] == 0
-    half = pl.program_id(1)
-    per = grad_rel.shape[0] // 32
-    chips = mine.shape[0] // GROUP
-    rel = []
-    for chip in range(chips):
+    columns = mine.shape[0]
+    per = grad_rel.shape[0] // (2 * GROUP)
+    for cb in range(columns):
+        rel = [[], []]
         for c in range(2):
             for mp in range(GROUP):
-                src = chip * GROUP + mp
-                own = mine[src].astype(F32)
-                far = other[src].astype(F32)
+                own = mine[cb, 0, mp].astype(F32)
+                far = other[cb, 0, mp].astype(F32)
                 got = jnp.where(first, own, far) if c == 0 else jnp.where(first, far, own)
-                i = (chip * 2 + c) * GROUP + mp
-                grad_self[i * SELF_ROWS : (i + 1) * SELF_ROWS, :] = jnp.where(
-                    half == 0, got[:SELF_ROWS], got[SELF_ROWS : 2 * SELF_ROWS]
-                )
-                at = 2 * SELF_ROWS
-                rel.append(jnp.where(half == 0, got[at : at + per], got[at + per : at + 2 * per]))
-    grad_rel[...] = jnp.concatenate(rel, axis=0)
+                i = c * GROUP + mp
+                for h in range(2):
+                    cols = slice((h * columns + cb) * LANES, (h * columns + cb + 1) * LANES)
+                    grad_self[i * SELF_ROWS : (i + 1) * SELF_ROWS, cols] = got[
+                        h * SELF_ROWS : (h + 1) * SELF_ROWS
+                    ]
+                    at = 2 * SELF_ROWS + h * per
+                    rel[h].append(got[at : at + per])
+        for h in range(2):
+            cols = slice((h * columns + cb) * LANES, (h * columns + cb + 1) * LANES)
+            grad_rel[:, cols] = jnp.concatenate(rel[h], axis=0)
 
 
 def spread(core, mine, other, feats, emb, hidden):
-    blocks = hidden // LANES // 2
+    columns = hidden // LANES // 2
     peers, rows, _ = mine.shape
-    block = pl.BlockSpec((peers // blocks, rows, LANES), lambda c, h: (c, 0, 0))
+    steps = peers // columns // GROUP
+    shape = (columns, steps, GROUP, rows, LANES)
+    block = pl.BlockSpec((columns, 1, GROUP, rows, LANES), lambda i: (0, i, 0, 0, 0))
     return pl.pallas_call(
         spread_kernel,
-        grid=(blocks, 2),
+        grid=(steps,),
         out_shape=(
             jax.ShapeDtypeStruct((feats, hidden), F32),
             jax.ShapeDtypeStruct((emb, hidden), F32),
         ),
         in_specs=[SMEM, block, block],
         out_specs=(
-            pl.BlockSpec((feats, LANES), lambda c, h: (0, h * blocks + c)),
-            pl.BlockSpec((emb, LANES), lambda c, h: (0, h * blocks + c)),
+            pl.BlockSpec((feats // steps, hidden), lambda i: (i, 0)),
+            pl.BlockSpec((emb // steps, hidden), lambda i: (i, 0)),
         ),
         name="weight_out",
-    )(core, mine, other)
+    )(core, mine.reshape(shape), other.reshape(shape))
+
+
+def after_kernel(*refs):
+    pass
+
+
+def after(a, *ready):
+    return pl.pallas_call(
+        after_kernel,
+        out_shape=jax.ShapeDtypeStruct(a.shape, a.dtype),
+        in_specs=[ANY] * (1 + len(ready)),
+        out_specs=ANY,
+        input_output_aliases={0: 0},
+        name="after",
+    )(a, *ready)
 
 
 def adam_kernel(
-    wanted, bundle, table, m1, m2, new_table, new_m1, new_m2, arrived, hot_scr, side_scr, sem
+    wanted, bundle, table, m1, m2, new_table, new_m1, new_m2, done, arrived, hot_scr, side_scr, sem
 ):
     step = pl.program_id(0)
     lines = wanted.shape[0]
+    done[...] = jnp.zeros_like(done)
 
     @pl.when(step == 0)
     def _():
@@ -550,9 +611,10 @@
     return pl.pallas_call(
         adam_kernel,
         grid=(table.shape[0] // rows,),
-        out_shape=(jax.ShapeDtypeStruct(table.shape, F32),) * 3,
+        out_shape=(jax.ShapeDtypeStruct(table.shape, F32),) * 3
+        + (jax.ShapeDtypeStruct((8, LANES), F32),),
         in_specs=[pl.BlockSpec(wanted.shape, lambda i: (0, 0)), ANY, block, block, block],
-        out_specs=(block, block, block),
+        out_specs=(block, block, block, pl.BlockSpec((8, LANES), lambda i: (0, 0))),
         scratch_shapes=[
             pltpu.VMEM((LANES, CAP, LANES), BF16),
             pltpu.VMEM((rows, slots), BF16),
@@ -589,7 +651,7 @@
     seeds, width = feats.shape
     hidden = cotangent.shape[1]
     emb = table.shape[1]
-    core = lax.axis_index("core")
+    core = lax.axis_index("core").astype(I32).reshape(1)
     group = lax.axis_index("mp").astype(I32).reshape(1)
 
     def exchange(a, axes):
@@ -610,25 +672,20 @@
     rows, wanted = gather(got, table)
     fetched = exchange(rows.reshape(devs, CAP, emb), every).reshape(devs * CAP, emb)
 
-    pre_self = jnp.dot(feats, w_self, preferred_element_type=F32)
+    pre_self, cot, w_rel = prep(feats, w_self, cotangent, w_rel)
     feats_t = jnp.concatenate([feats, swap(feats)], axis=0).T
     papers = paper_rows(got, paper_table).reshape(devs, -1, LANES)
     papers = jnp.pad(papers, ((0, 0), (0, PAPER_ROWS - papers.shape[1]), (0, 0)))
-    agg_b, dpre, grad = layer(fetched, seed_of, cnt, pre_self, w_rel, cotangent)
-
-    half = hidden // 2
-    dpre_here = lax.dynamic_slice_in_dim(dpre, core * half, half, 1)
-    dpre_there = lax.dynamic_slice_in_dim(dpre, (1 - core) * half, half, 1)
+    agg_b, dpre_here, dpre_there, grad = layer(
+        core, fetched, seed_of, cnt, pre_self, w_rel, cot, feats_t, papers
+    )
+
     agg_far, dpre_far = swap(agg_b), swap(dpre_there)
     bundle = slot_grads(seed_of, grad, papers)
     bundle = weight_part(feats_t, agg_b, agg_far, dpre_here, dpre_far, bundle)
     bundle = exchange(bundle, every)
     full = exchange(sum_parts(bundle, lax.axis_size(peers)), peers)
-    new_table, new_moment1, new_moment2 = adam(wanted, bundle, table, moment1, moment2)
-    grad_self, grad_rel = spread(
-        core.astype(I32).reshape(1), full, swap(full), width, emb, hidden
-    )
-
+    new_table, new_moment1, new_moment2, done = adam(wanted, bundle, table, moment1, moment2)
     papers = bundle[:, PAPER_AT : PAPER_AT + FCAP * width // LANES, :].reshape(devs, -1)
     next_feats = functools.reduce(
         lambda a, b: a + b,
@@ -642,6 +699,8 @@
             for t in range(FCAP)
         ],
     ).astype(BF16)
+    full = after(full, done, next_feats)
+    grad_self, grad_rel = spread(core, full, swap(full), width, emb, hidden)
     return (new_table, new_moment1, new_moment2, grad_self, grad_rel, next_feats)
 
 

time: 171 us -> 134 us (0.78)
  blocking collectives: 83.9 us -> 61.3 us
  Pallas kernels: 55.4 us -> 33.9 us
  starting transfers between devices: 7.81 us -> 13.5 us
    all_to_all x3 -> x2, blocking collectives: 83.9 us -> 61.3 us  [exchange(): return lax.all_to_all(a, axes, split_axis=0, concat_axis=0, tiled=True)]
    pallas_call x1, Pallas kernels: 17.8 us -> 1.76 us  [slot_grads(): pl.pallas_call(slots_kernel, out_shape=jax.ShapeDtypeStruct((LANES, BUNDL...]
    all_to_all x1 -> x2, starting transfers between devices: 4.26 us -> 10 us  [exchange(): return lax.all_to_all(a, axes, split_axis=0, concat_axis=0, tiled=True)]
    pallas_call x1, Pallas kernels: 3.61 us -> 0.9 us  [layer(): pl.pallas_call(layer_kernel, out_shape=(jax.ShapeDtypeStruct((seeds, LANE...]
    ppermute x4, waiting for transfers between devices: 0.01 us -> 2.32 us  [swap(): return lax.ppermute(a, 'core', [(0, 1), (1, 0)])]
    unnamed x15 -> x27, local copies, waits for them, and re-layouts: 2.46 us -> 4.44 us
    pallas_call x1 -> x3, Pallas kernels: 6.48 us -> 4.69 us  [the longest x1 4.23 us: spread(): pl.pallas_call(spread_kernel, grid=(steps,), out_shape=(jax.ShapeDtypeStr...]
    all_to_all x1 -> x2, waiting for transfers between devices: 10.9 us -> 10.1 us  [exchange(): return lax.all_to_all(a, axes, split_axis=0, concat_axis=0, tiled=True)]
  transfers between devices with their start and end apart: 5 -> 6, of which waited for: 1 -> 3; matrix products, arithmetic and copies ran while one was open for 6% -> 5% of each run, Pallas kernels for 21% -> 13%
where the time goes in v3:
time: 134 us; the launch traced here: 133 us
  blocking collectives  61.3 us (46%)
  Pallas kernels  33.9 us (25%)
  starting transfers between devices  13.5 us (10%)
  waiting for transfers between devices  12.4 us (9%)
  local copies, waits for them, and re-layouts  8.49 us (6%)
    all_to_all x2, blocking collectives, exchange(): return lax.all_to_all(a, axes, split_axis=0, concat_axis=0, tiled=True)  61.3 us
    pallas_call x1, Pallas kernels, adam(): pl.pallas_call(adam_kernel, grid=(table.shape[0] // rows,), out_shape=(ja...  10.8 us
    all_to_all x2, waiting for transfers between devices, exchange(): return lax.all_to_all(a, axes, split_axis=0, concat_axis=0, tiled=True)  10.1 us
    all_to_all x2, starting transfers between devices, exchange(): return lax.all_to_all(a, axes, split_axis=0, concat_axis=0, tiled=True)  10 us
    pallas_call x1, Pallas kernels, gather(): pl.pallas_call(gather_kernel, out_shape=(jax.ShapeDtypeStruct((slots, LAN...  5.84 us
    unnamed x27, local copies, waits for them, and re-layouts  4.44 us
    pallas_call x1, Pallas kernels, spread(): pl.pallas_call(spread_kernel, grid=(steps,), out_shape=(jax.ShapeDtypeStr...  4.23 us
    pallas_call x1, Pallas kernels, paper_rows(): pl.pallas_call(paper_kernel, out_shape=jax.ShapeDtypeStruct((LANES, FCAP...  3.71 us
  transfers between devices with their start and end apart: 6, of which 3 were waited for; matrix products, arithmetic and copies ran while one was open for 5% of the time, Pallas kernels for 13%

profile of v3, /device:TPU:1, one launch (start us, length us, event | category | flops | bytes accessed | tf_op | source)
XLA Modules:
  0.0 132.7 jit_solution(10773293624170577167)
XLA Ops:
  0.7 3.1 %place.1 = (s32[128,128]{1,0:T(8,128)}, s32[32,128]{1,0:T(8,128)}, f32[128,128]{1,0:T(8,128)}, bf16[2,128,128]{2,1,0:T(8,128)(2,1)}) custom-call(s32[1]{0:T(128)} %bitcast.lane_group, s32[16,128]{1,0:T(8,128)} %bitcast.34, s32[16,128]{1,0:T(8,128)} %bitcast.35, s32[1,128]{1,0:T(1,128)} %bitcast.36, s32[1,128]{1,0:T(1,128)} %bitcast.37, s32[1,128]{1,0:T(1,128)} %bitcast.38), custom_call_target="tpu_custom_call" | custom-call | tf_op jit(solution)/shard_map/place/pallas_call | solution.py:166
  3.8 21.5 %all_to_all.20 = s32[128,1,128]{2,1,0:T(1,128)} all-to-all(s32[128,1,128]{2,1,0:T(1,128)} %bitcast.33), channel_id=1, replica_groups=mesh['chip'=16,'core'=2,'mp'=4] {'chip','core','mp'}, dimensions={0} | all-to-all | bytes 131072 | tf_op jit(solution)/shard_map/all_to_all | solution.py:658
  25.3 5.8 %gather_rows.1 = (bf16[4096,128]{1,0:T(8,128)(2,1)}, s32[32,128]{1,0:T(8,128)}) custom-call(s32[128,128]{1,0:T(8,128)} %bitcast.31, f32[2048,128]{1,0:T(8,128)} %table.1), custom_call_target="tpu_custom_call" | custom-call | tf_op jit(solution)/shard_map/gather_rows/pallas_call | solution.py:238
  31.1 4.4 %all-to-all-start.1 = ((bf16[128,32,128]{2,1,0:T(8,128)(2,1)}), bf16[128,32,128]{2,1,0:T(8,128)(2,1)S(1)}, u32[]{:S(2)}, u32[]{:S(2)}) async-start(bf16[128,32,128]{2,1,0:T(8,128)(2,1)} %bitcast.29), calls=%async_computation.1 | async-start | bytes 2097152 | tf_op jit(solution)/shard_map/all_to_all | solution.py:658
  36.4 1.1 collective-permute-start
  37.4 1.0 copy-done.3
  40.5 3.7 %gather_papers.1 = bf16[128,1536]{1,0:T(8,128)(2,1)} custom-call(s32[128,128]{1,0:T(8,128)} %bitcast.32, bf16[1024,768]{1,0:T(8,128)(2,1)} %paper_in.1), custom_call_target="tpu_custom_call" | custom-call | flops 402653184 | bytes 3145728 | tf_op jit(solution)/shard_map/gather_papers/pallas_call | solution.py:273
  44.3 1.3 copy.31
  45.6 1.2 copy.32
  46.8 1.1 pad.4.rest_1_.papers
  47.9 1.1 maximum_bitcast_fusion.rest_0_.feats_t
  49.0 6.0 %all-to-all-done.1 = bf16[128,32,128]{2,1,0:T(8,128)(2,1)S(1)} async-done(((bf16[128,32,128]{2,1,0:T(8,128)(2,1)}), bf16[128,32,128]{2,1,0:T(8,128)(2,1)S(1)}, u32[]{:S(2)}, u32[]{:S(2)}) %all-to-all-start.1) | async-done | bytes 1048608 | tf_op jit(solution)/shard_map/all_to_all | solution.py:658
  56.6 1.8 %slot_grads.1.bundle_in = bf16[128,80,128]{2,1,0:T(8,128)(2,1)S(1)} custom-call(s32[32,128]{1,0:T(8,128)S(1)} %copy-done.9, bf16[128,128]{1,0:T(8,128)(2,1)S(1)} %get-tuple-element.36.grad, bf16[128,16,128]{2,1,0:T(8,128)(2,1)S(1)} %pad.4.rest_1_.papers), custom_call_target="tpu_custom_call" | custom-call | flops 134217728 | bytes 4194304 | tf_op jit(solution)/shard_map/slot_grads/pallas_call | solution.py:394
  58.4 1.6 %weight_part.1 = bf16[128,80,128]{2,1,0:T(8,128)(2,1)S(1)} custom-call(bf16[768,256]{1,0:T(8,128)(2,1)S(1)} %maximum_bitcast_fusion.rest_0_.feats_t, bf16[128,128]{1,0:T(8,128)(2,1)S(1)} %get-tuple-element.33.agg0, bf16[128,128]{1,0:T(8,128)(2,1)S(1)} %collective-permute-done.1.agg1, ...), custom_call_target="tpu_custom_call", output_to_operand_aliasing={{}: (5, {})} | custom-call | tf_op jit(solution)/shard_map/weight_part/pallas_call | solution.py:448
  60.0 39.8 %all_to_all.21.bundle = bf16[128,80,128]{2,1,0:T(8,128)(2,1)S(1)} all-to-all(bf16[128,80,128]{2,1,0:T(8,128)(2,1)S(1)} %weight_part.1), channel_id=1, replica_groups=mesh['chip'=16,'core'=2,'mp'=4] {'chip','core','mp'}, dimensions={0} | all-to-all | bytes 5242880 | tf_op jit(solution)/shard_map/all_to_all | solution.py:658
  99.9 1.5 %sum_parts.1 = bf16[64,56,128]{2,1,0:T(8,128)(2,1)} custom-call(bf16[128,80,128]{2,1,0:T(8,128)(2,1)S(1)} %all_to_all.21.bundle), custom_call_target="tpu_custom_call" | custom-call | tf_op jit(solution)/shard_map/sum_parts/pallas_call | solution.py:497
  101.4 5.6 %all-to-all-start.3 = ((bf16[64,56,128]{2,1,0:T(8,128)(2,1)}), bf16[64,56,128]{2,1,0:T(8,128)(2,1)}, u32[]{:S(2)}, u32[]{:S(2)}) async-start(bf16[64,56,128]{2,1,0:T(8,128)(2,1)} %sum_parts.1), calls=%async_computation.3 | async-start | bytes 1835008 | tf_op jit(solution)/shard_map/all_to_all | solution.py:658
  107.7 0.9 fusion.refs_2_
  108.6 10.8 %adam.1 = (f32[2048,128]{1,0:T(8,128)}, f32[2048,128]{1,0:T(8,128)}, f32[2048,128]{1,0:T(8,128)}, f32[8,128]{1,0:T(8,128)}) custom-call(s32[32,128]{1,0:T(8,128)} %get-tuple-element.26.wanted, bf16[128,80,128]{2,1,0:T(8,128)(2,1)} %copy-done, f32[2048,128]{1,0:T(8,128)} %table.1, f32[2048,128]{1,0:T(8,128)} %m1.1, f32[2048,128]{1,0:T(8,128)} %m2.1), custom_call_target="tpu_custom_call" | custom-call | flops 4294967296 | bytes 7340032 | tf_op jit(solution)/shard_map/adam/pallas_call | solution.py:611
  119.4 4.1 %all-to-all-done.3.refs_0_ = bf16[64,56,128]{2,1,0:T(8,128)(2,1)} async-done(((bf16[64,56,128]{2,1,0:T(8,128)(2,1)}), bf16[64,56,128]{2,1,0:T(8,128)(2,1)}, u32[]{:S(2)}, u32[]{:S(2)}) %all-to-all-start.3) | async-done | bytes 917536 | tf_op jit(solution)/shard_map/all_to_all | solution.py:658
  123.5 1.7 %collective-permute-start.3 = (bf16[64,56,128]{2,1,0:T(8,128)(2,1)}, bf16[64,56,128]{2,1,0:T(8,128)(2,1)S(1)}, u32[]{:S(2)}, u32[]{:S(2)}) collective-permute-start(bf16[64,56,128]{2,1,0:T(8,128)(2,1)} %after.1), channel_id=1, source_target_pairs={{0,4},{4,0},{1,5},{5,1},{2,6},{6,2},{3,7},{7,3},{8,12},{12,8},{9,1... | collective-permute-start | bytes 2752520 | tf_op jit(solution)/shard_map/ppermute | solution.py:661
  125.2 2.3 %collective-permute-done.3 = bf16[64,56,128]{2,1,0:T(8,128)(2,1)S(1)} collective-permute-done((bf16[64,56,128]{2,1,0:T(8,128)(2,1)}, bf16[64,56,128]{2,1,0:T(8,128)(2,1)S(1)}, u32[]{:S(2)}, u32[]{:S(2)}) %collective-permute-start.3) | collective-permute-done | bytes 917536 | tf_op jit(solution)/shard_map/ppermute | solution.py:661
  127.5 1.0 copy-done.11
  128.4 4.2 %weight_out.1 = (f32[768,1024]{1,0:T(8,128)}, f32[128,1024]{1,0:T(8,128)}) custom-call(s32[1]{0:T(128)} %bitcast.10.core, bf16[4,4,4,56,128]{4,3,2,1,0:T(8,128)(2,1)} %bitcast.17.mine, bf16[4,4,4,56,128]{4,3,2,1,0:T(8,128)(2,1)} %bitcast.30), custom_call_target="tpu_custom_call" | custom-call | tf_op jit(solution)/shard_map/weight_out/pallas_call | solution.py:542
  (36 shorter events, 5.2 us)
Async XLA Ops:
  0.6 34.9 %copy-start.2 = (bf16[128,768]{1,0:T(8,128)(2,1)S(1)}, bf16[128,768]{1,0:T(8,128)(2,1)}, u32[]{:S(2)}) copy-start(bf16[128,768]{1,0:T(8,128)(2,1)} %feats.1) | copy-start | bytes 589828
  0.6 36.8 %copy-start.8 = (bf16[128,1024]{1,0:T(8,128)(2,1)S(1)}, bf16[128,1024]{1,0:T(8,128)(2,1)}, u32[]{:S(2)}) copy-start(bf16[128,1024]{1,0:T(8,128)(2,1)} %w_in.1) | copy-start | bytes 786436
  0.7 36.8 %copy-start.1 = (bf16[768,1024]{1,0:T(8,128)(2,1)S(1)}, bf16[768,1024]{1,0:T(8,128)(2,1)}, u32[]{:S(2)}) copy-start(bf16[768,1024]{1,0:T(8,128)(2,1)} %w_self.1) | copy-start | bytes 4718596
  31.1 23.8 %all-to-all-start.1 = ((bf16[128,32,128]{2,1,0:T(8,128)(2,1)}), bf16[128,32,128]{2,1,0:T(8,128)(2,1)S(1)}, u32[]{:S(2)}, u32[]{:S(2)}) async-start(bf16[128,32,128]{2,1,0:T(8,128)(2,1)} %bitcast.29), calls=%async_computation.1 | async-start | bytes 2097152 | tf_op jit(solution)/shard_map/all_to_all | solution.py:658
  36.4 11.6 %collective-permute-start = (bf16[128,768]{0,1:T(8,128)(2,1)}, bf16[128,768]{0,1:T(8,128)(2,1)}, u32[]{:S(2)}, u32[]{:S(2)}) collective-permute-start(bf16[128,768]{0,1:T(8,128)(2,1)} %copy.30), channel_id=1, source_target_pairs={{0,4},{4,0},{1,5},{5,1},{2,6},{6,2},{3,7},{7,3},{8,12},{12,8},{9,1... | collective-permute-start | bytes 589832 | tf_op jit(solution)/shard_map/ppermute | solution.py:661
  37.4 1.0 copy-start.3
  38.9 0.8 copy-start.4
  39.7 0.8 copy-start.6
  40.5 14.4 %copy-start.9 = (s32[32,128]{1,0:T(8,128)S(1)}, s32[32,128]{1,0:T(8,128)}, u32[]{:S(2)}) copy-start(s32[32,128]{1,0:T(8,128)} %get-tuple-element.28.seed_of) | copy-start | bytes 49156
  40.5 14.4 %copy-start.10 = (f32[128,128]{1,0:T(8,128)S(1)}, f32[128,128]{1,0:T(8,128)}, u32[]{:S(2)}) copy-start(f32[128,128]{1,0:T(8,128)} %get-tuple-element.29.cnt) | copy-start | bytes 196612
  44.2 10.7 %copy-start.5 = (f32[128,1024]{1,0:T(8,128)S(1)}, f32[128,1024]{1,0:T(8,128)}, u32[]{:S(2)}) copy-start(f32[128,1024]{1,0:T(8,128)} %copy-done.4) | copy-start | bytes 1572868
  44.3 10.7 %copy-start.7 = (f32[128,1024]{1,0:T(8,128)S(1)}, f32[128,1024]{1,0:T(8,128)}, u32[]{:S(2)}) copy-start(f32[128,1024]{1,0:T(8,128)} %copy-done.6) | copy-start | bytes 1572868
  55.9 2.5 %collective-permute-start.2 = (bf16[128,512]{1,0:T(8,128)(2,1)S(1)}, bf16[128,512]{1,0:T(8,128)(2,1)S(1)}, u32[]{:S(2)}, u32[]{:S(2)}) collective-permute-start(bf16[128,512]{1,0:T(8,128)(2,1)S(1)} %get-tuple-element.35), channel_id=1, source_target_pairs={{0,4},{4,0},{1,5},{5,1},{2,6},{6,2},{3,7},{7,3},{8,12},{12,8},{9,1... | collective-permute-start | bytes 393224 | tf_op jit(solution)/shard_map/ppermute | solution.py:661
  56.4 2.0 %collective-permute-start.1 = (bf16[128,128]{1,0:T(8,128)(2,1)S(1)}, bf16[128,128]{1,0:T(8,128)(2,1)S(1)}, u32[]{:S(2)}, u32[]{:S(2)}) collective-permute-start(bf16[128,128]{1,0:T(8,128)(2,1)S(1)} %get-tuple-element.33.agg0), channel_id=1, source_target_pairs={{0,4},{4,0},{1,5},{5,1},{2,6},{6,2},{3,7},{7,3},{8,12},{12,8},{9,1... | collective-permute-start | bytes 98312 | tf_op jit(solution)/shard_map/ppermute | solution.py:661
  99.8 7.1 %copy-start = (bf16[128,80,128]{2,1,0:T(8,128)(2,1)}, bf16[128,80,128]{2,1,0:T(8,128)(2,1)S(1)}, u32[]{:S(2)}) copy-start(bf16[128,80,128]{2,1,0:T(8,128)(2,1)S(1)} %all_to_all.21.bundle) | copy-start | bytes 7864324
  101.4 6.1 %copy-start.12 = (bf16[2,128,128]{2,1,0:T(8,128)(2,1)S(1)}, bf16[2,128,128]{2,1,0:T(8,128)(2,1)}, u32[]{:S(2)}) copy-start(bf16[2,128,128]{2,1,0:T(8,128)(2,1)} %get-tuple-element.41) | copy-start | bytes 196612
  101.4 22.1 %all-to-all-start.3 = ((bf16[64,56,128]{2,1,0:T(8,128)(2,1)}), bf16[64,56,128]{2,1,0:T(8,128)(2,1)}, u32[]{:S(2)}, u32[]{:S(2)}) async-start(bf16[64,56,128]{2,1,0:T(8,128)(2,1)} %sum_parts.1), calls=%async_computation.3 | async-start | bytes 1835008 | tf_op jit(solution)/shard_map/all_to_all | solution.py:658
  123.5 4.0 %collective-permute-start.3 = (bf16[64,56,128]{2,1,0:T(8,128)(2,1)}, bf16[64,56,128]{2,1,0:T(8,128)(2,1)S(1)}, u32[]{:S(2)}, u32[]{:S(2)}) collective-permute-start(bf16[64,56,128]{2,1,0:T(8,128)(2,1)} %after.1), channel_id=1, source_target_pairs={{0,4},{4,0},{1,5},{5,1},{2,6},{6,2},{3,7},{7,3},{8,12},{12,8},{9,1... | collective-permute-start | bytes 2752520 | tf_op jit(solution)/shard_map/ppermute | solution.py:661
  127.5 1.0 copy-start.11

commit v4 on v3

v4 whole, which is shorter than its diff:
```python
import functools

import jax
import jax.numpy as jnp
from jax import lax
from jax.experimental import pallas as pl
from jax.experimental.pallas import tpu as pltpu
from jax.sharding import Mesh, PartitionSpec as P

F32 = jnp.float32
BF16 = jnp.bfloat16
I32 = jnp.int32
LANES = 128
CAP = 32
FCAP = 2
GROUP = LANES // CAP
EMPTY = 4095
SELF_ROWS = 24
REL_ROWS = 4
REL_AT = CAP + SELF_ROWS
PAPER_AT = REL_AT + REL_ROWS
PAPER_ROWS = 12
TILE = 256
BUNDLE = PAPER_AT + PAPER_ROWS
VMEM = pl.BlockSpec(memory_space=pltpu.VMEM)
SMEM = pl.BlockSpec(memory_space=pltpu.SMEM)


def iota(shape, dim):
    return lax.broadcasted_iota(I32, shape, dim)


def dot(a, b, contract=((1,), (0,))):
    return lax.dot_general(a, b, (contract, ((), ())), preferred_element_type=F32)


def onehot(mask):
    return jnp.where(mask, F32(1.0), F32(0.0)).astype(BF16)

ANY = pl.BlockSpec(memory_space=pl.ANY)
HBM = pl.BlockSpec(memory_space=pltpu.HBM)


def params():
    return pltpu.CompilerParams(vmem_limit_bytes=24 * 1024 * 1024)


def in_hbm(*arrays):
    return [pltpu.with_memory_space_constraint(a, pltpu.HBM) for a in arrays]


def fetch(pairs, sems):
    copies = [pltpu.make_async_copy(a, b, sems.at[i]) for i, (a, b) in enumerate(pairs)]
    for c in copies:
        c.start()
    return copies


def place_kernel(
    lane_group,
    owner_in,
    row_in,
    counts_in,
    next_owner_in,
    next_row_in,
    table_in,
    asked,
    seed_of,
    cnt,
    paper_pick,
    wide,
    owner,
    row,
    counts,
    next_owner,
    next_row,
    table,
    seed_scr,
    sems,
):
    copies = fetch(
        [
            (owner_in, owner),
            (row_in, row),
            (counts_in, counts),
            (next_owner_in, next_owner),
            (next_row_in, next_row),
            (table_in, table),
        ],
        sems,
    )
    table_copy = copies.pop()
    devs = LANES
    blocks = owner.shape[0]
    group = lane_group[0]
    sub = iota((devs, LANES), 0)
    lane = iota((devs, LANES), 1)
    seeds_row = LANES // (LANES * blocks // devs)
    slots_per = LANES // seeds_row
    upper = onehot(sub < lane)
    ones = jnp.ones((devs, LANES), BF16)
    scan = jnp.concatenate([upper, ones], axis=1)
    pick = onehot(sub % seeds_row == lane // slots_per)
    for c in copies:
        c.wait()
    count_row = counts[...].astype(F32)
    spread = jnp.where(
        iota((blocks, LANES), 1) // seeds_row == iota((blocks, LANES), 0), count_row, F32(0.0)
    ).astype(BF16)
    cnt_edge = dot(spread, pick)
    k_edge = (iota((blocks, LANES), 1) % slots_per).astype(F32)
    live_owner = jnp.where(k_edge < cnt_edge, owner[...], -1)
    base = jnp.zeros((devs, LANES), F32)
    acc = jnp.zeros((devs, 3 * CAP), F32)
    ksub = iota((CAP, LANES), 0).astype(F32)
    for b in range(blocks):
        hot = sub == live_owner[b : b + 1, :]
        hot_f = jnp.where(hot, F32(1.0), F32(0.0))
        hot_b = hot_f.astype(BF16)
        scanned = dot(hot_b, scan)
        slot = jnp.sum(hot_f * (scanned[:, :LANES] + base), axis=0, keepdims=True)
        base = base + scanned[:, LANES:]
        at = ksub == slot
        r = row[b : b + 1, :]
        seed1 = b * seeds_row + iota((1, LANES), 1) // slots_per + 1
        vals = jnp.concatenate(
            [
                jnp.where(at, (r // LANES).astype(F32), F32(0.0)),
                jnp.where(at, (r % LANES).astype(F32), F32(0.0)),
                jnp.where(at, seed1.astype(F32), F32(0.0)),
            ],
            axis=0,
        ).astype(BF16)
        acc = acc + dot(hot_b, vals, ((1,), (1,)))
    acc_i = acc.astype(I32)
    seeds = acc_i[:, 2 * CAP :]
    wanted = jnp.where(seeds > 0, acc_i[:, :CAP] * LANES + acc_i[:, CAP : 2 * CAP], EMPTY)

    hot = sub == next_owner[...]
    hot_f = jnp.where(hot, F32(1.0), F32(0.0))
    hot_b = hot_f.astype(BF16)
    before = dot(hot_b, upper)
    slot = jnp.sum(hot_f * before, axis=0, keepdims=True)
    nrow = next_row[...]
    for t in range(FCAP):
        paper_pick[t] = jnp.where(slot == t, hot_f, F32(0.0)).astype(BF16)
    at = iota((CAP, LANES), 0) == slot.astype(I32)
    vals = jnp.concatenate(
        [
            jnp.where(at, (nrow // LANES).astype(F32), F32(0.0)),
            jnp.where(at, (nrow % LANES).astype(F32), F32(0.0)),
        ],
        axis=0,
    ).astype(BF16)
    pacc = dot(hot_b, vals, ((1,), (1,))).astype(I32)
    paper = pacc[:, :CAP] * LANES + pacc[:, CAP:]

    quarter = lane // CAP
    wide_wanted = jnp.concatenate([wanted] * GROUP, axis=1)
    wide_paper = jnp.concatenate([paper] * GROUP, axis=1)
    asked[...] = jnp.where(
        quarter == group,
        wide_wanted,
        jnp.where(quarter == (group + 1) % GROUP, wide_paper, 0),
    )
    seed_scr[...] = jnp.where(quarter == sub % GROUP, jnp.concatenate([seeds] * GROUP, axis=1), 0)
    total = seed_scr[pl.ds(0, devs // GROUP, stride=GROUP), :]
    for i in range(1, GROUP):
        total = total + seed_scr[pl.ds(i, devs // GROUP, stride=GROUP), :]
    seed_of[...] = total
    cnt[...] = jnp.broadcast_to(count_row, (devs, LANES)).T
    table_copy.wait()
    for q in range(table.shape[0] // TILE):
        wide[:, q * LANES : (q + 1) * LANES] = table[q * TILE : (q + 1) * TILE, :].astype(BF16)


def place(group, owner, row, counts, next_owner, next_row, table):
    devs = LANES
    ins = (owner, row, counts, next_owner, next_row, table)
    return pl.pallas_call(
        place_kernel,
        out_shape=(
            pltpu.HBM((devs, LANES), I32),
            jax.ShapeDtypeStruct((devs // GROUP, LANES), I32),
            jax.ShapeDtypeStruct((devs, LANES), F32),
            jax.ShapeDtypeStruct((FCAP, devs, LANES), BF16),
            pltpu.VMEM((TILE, table.shape[0] // TILE * LANES), BF16),
        ),
        in_specs=[SMEM] + [HBM] * len(ins),
        out_specs=(VMEM, VMEM, VMEM, VMEM, VMEM),
        scratch_shapes=[pltpu.VMEM(a.shape, a.dtype) for a in ins]
        + [pltpu.VMEM((devs, LANES), I32), pltpu.SemaphoreType.DMA((len(ins),))],
        compiler_params=params(),
        name="place",
    )(group, *in_hbm(*ins))


def gather_kernel(got, wide, rows, wanted_out, hot_scr, hi_scr, out_scr, out_sems):
    devs = LANES
    lines = devs // GROUP
    quarter = iota((lines, LANES), 1) // CAP
    wanted = jnp.zeros((lines, LANES), I32)
    for i in range(GROUP):
        wanted = wanted + jnp.where(quarter == i, got[pl.ds(i, lines, stride=GROUP), :], 0)
    wanted_out[...] = wanted
    lo = (wanted % TILE).T
    hi = (wanted // TILE).T
    lanes = iota((LANES, TILE), 1)
    for b in range(lines):
        hot_scr[b * LANES : (b + 1) * LANES, :] = onehot(lo[:, b : b + 1] == lanes)
        hi_scr[b * LANES : (b + 1) * LANES, :] = jnp.broadcast_to(hi[:, b : b + 1], (LANES, LANES))
    chunk = 512
    outs = []
    for c in range(out_scr.shape[0] // chunk):
        at = pl.ds(c * chunk, chunk)
        hot = hot_scr[at, :]
        high = hi_scr[at, :]
        out = jnp.zeros((chunk, LANES), F32)
        for q in range(0, wide.shape[1] // LANES, 2):
            both = dot(hot, wide[:, q * LANES : (q + 2) * LANES])
            out = jnp.where(high == q, both[:, :LANES], out)
            out = jnp.where(high == q + 1, both[:, LANES:], out)
        out_scr[at, :] = out.astype(BF16)
        copy = pltpu.make_async_copy(out_scr.at[at, :], rows.at[at, :], out_sems.at[c])
        copy.start()
        outs.append(copy)
    for copy in outs:
        copy.wait()


def gather(got, wide):
    slots = LANES * CAP
    return pl.pallas_call(
        gather_kernel,
        out_shape=(
            pltpu.HBM((slots, LANES), BF16),
            pltpu.HBM((LANES // GROUP, LANES), I32),
        ),
        in_specs=[VMEM, VMEM],
        out_specs=(HBM, VMEM),
        scratch_shapes=[
            pltpu.VMEM((slots, TILE), BF16),
            pltpu.VMEM((slots, LANES), I32),
            pltpu.VMEM((slots, LANES), BF16),
            pltpu.SemaphoreType.DMA((slots // 512,)),
        ],
        compiler_params=params(),
        name="gather_rows",
    )(got, wide)


def paper_kernel(got, paper, rows, scr):
    devs = LANES
    sub = iota((devs, LANES), 0)
    lane = iota((devs, LANES), 1)
    first = ((sub % GROUP + 1) % GROUP) * CAP
    parts = paper.shape[1] // LANES
    span = REL_ROWS + PAPER_ROWS
    for i in range(REL_ROWS):
        scr[pl.ds(i, devs, stride=span), :] = jnp.zeros((devs, LANES), F32)
    for t in range(FCAP):
        asked = jnp.sum(jnp.where(lane == first + t, got[...], 0), axis=1, keepdims=True)
        hot = onehot(asked == iota((devs, paper.shape[0]), 1))
        found = dot(hot, paper[...])
        for i in range(parts):
            scr[pl.ds(REL_ROWS + t * parts + i, devs, stride=span), :] = found[
                :, i * LANES : (i + 1) * LANES
            ]
    rows[...] = scr[...].astype(BF16).reshape(rows.shape)


def paper_rows(got, paper):
    span = REL_ROWS + PAPER_ROWS
    return pl.pallas_call(
        paper_kernel,
        out_shape=pltpu.HBM((LANES, span, LANES), BF16),
        in_specs=[VMEM, VMEM],
        out_specs=VMEM,
        scratch_shapes=[pltpu.VMEM((LANES * span, LANES), F32)],
        compiler_params=params(),
        cost_estimate=pl.CostEstimate(
            flops=2 * FCAP * LANES * paper.shape[0] * paper.shape[1],
            bytes_accessed=4 * paper.size,
            transcendentals=0,
        ),
        name="gather_papers",
    )(got, paper)


def prep_kernel(feats, w_self, pre):
    pre[...] = dot(feats[...], w_self[...])


def prep(feats, w_self):
    return pl.pallas_call(
        prep_kernel,
        out_shape=pltpu.HBM((feats.shape[0], w_self.shape[1]), F32),
        in_specs=[VMEM, VMEM],
        out_specs=VMEM,
        compiler_params=params(),
        cost_estimate=pl.CostEstimate(
            flops=2 * feats.size * w_self.shape[1], bytes_accessed=4 << 20, transcendentals=0
        ),
        name="prep",
    )(feats, w_self)


def turn_kernel(feats, far, out):
    seeds = feats.shape[0]
    out[:, :seeds] = feats[...].T
    out[:, seeds:] = far[...].T


def turn(feats, far):
    seeds, width = feats.shape
    return pl.pallas_call(
        turn_kernel,
        out_shape=pltpu.HBM((width, 2 * seeds), BF16),
        in_specs=[VMEM, VMEM],
        out_specs=VMEM,
        compiler_params=params(),
        cost_estimate=pl.CostEstimate(flops=0, bytes_accessed=8 * feats.size, transcendentals=0),
        name="turn",
    )(feats, far)


def layer_kernel(
    core,
    fetched,
    seed_of,
    cnt,
    pre_in,
    w_in,
    cot_in,
    *rest,
):
    agg_out, here_out, there_out, grad_out, pre_self, w_rel, cot, sems = rest[-8:]
    copies = fetch([(w_in, w_rel), (pre_in, pre_self), (cot_in, cot)], sems)
    devs = LANES
    lines = seed_of.shape[0]
    seed1 = iota((devs, LANES), 0) + 1
    agg = jnp.zeros((devs, LANES), F32)
    for b in range(0, lines, 2):
        match = jnp.concatenate(
            [onehot(seed1 == seed_of[b : b + 1, :]), onehot(seed1 == seed_of[b + 1 : b + 2, :])],
            axis=1,
        )
        agg = agg + dot(match, fetched[b * LANES : (b + 2) * LANES, :])
    count = cnt[...]
    agg_b = (agg / count).astype(BF16)
    agg_out[...] = agg_b
    for c in copies:
        c.wait()
    pre = pre_self[...] + dot(agg_b, w_rel[...])
    sig = jax.nn.sigmoid(pre)
    dpre = (cot[...] * sig * (1.0 + pre * (1.0 - sig))).astype(BF16)
    half = dpre.shape[1] // 2
    first = core[0] == 0
    here_out[...] = jnp.where(first, dpre[:, :half], dpre[:, half:])
    there_out[...] = jnp.where(first, dpre[:, half:], dpre[:, :half])
    dagg = dot(dpre, w_rel[...], ((1,), (1,)))
    grad_out[...] = (dagg / count).astype(BF16)


def layer(core, fetched, seed_of, cnt, pre_self, w_rel, cotangent, *ready):
    seeds, hidden = cotangent.shape
    return pl.pallas_call(
        layer_kernel,
        out_shape=(
            jax.ShapeDtypeStruct((seeds, LANES), BF16),
            jax.ShapeDtypeStruct((seeds, hidden // 2), BF16),
            jax.ShapeDtypeStruct((seeds, hidden // 2), BF16),
            jax.ShapeDtypeStruct((seeds, LANES), BF16),
        ),
        in_specs=[SMEM] + [VMEM] * 3 + [HBM] * 3 + [ANY] * len(ready),
        out_specs=(VMEM, VMEM, VMEM, VMEM),
        scratch_shapes=[
            pltpu.VMEM(pre_self.shape, F32),
            pltpu.VMEM(w_rel.shape, BF16),
            pltpu.VMEM(cotangent.shape, F32),
            pltpu.SemaphoreType.DMA((3,)),
        ],
        compiler_params=params(),
        name="layer",
    )(core, fetched, seed_of, cnt, *in_hbm(pre_self, w_rel, cotangent, *ready))


def slots_kernel(seed_of, grad, papers_in, feats_in, out, papers, feats, sems):
    copies = fetch([(papers_in, papers), (feats_in, feats)], sems)
    seeds_t = seed_of[...].T
    lane1 = iota((LANES, LANES), 1) + 1
    for b in range(seed_of.shape[0]):
        match = onehot(seeds_t[:, b : b + 1] == lane1)
        out[b * GROUP : (b + 1) * GROUP] = (
            dot(match, grad[...]).astype(BF16).reshape(GROUP, CAP, LANES)
        )
    for c in copies:
        c.wait()


def slot_grads(seed_of, grad, papers, feats_t):
    return pl.pallas_call(
        slots_kernel,
        out_shape=(
            pltpu.VMEM((LANES, CAP, LANES), BF16),
            pltpu.VMEM(papers.shape, BF16),
            pltpu.VMEM(feats_t.shape, BF16),
        ),
        in_specs=[VMEM, VMEM, HBM, HBM],
        out_specs=(VMEM, VMEM, VMEM),
        scratch_shapes=[pltpu.SemaphoreType.DMA((2,))],
        compiler_params=params(),
        cost_estimate=pl.CostEstimate(
            flops=2 * LANES * CAP * LANES * LANES, bytes_accessed=4 << 20, transcendentals=0
        ),
        name="slot_grads",
    )(seed_of, grad, *in_hbm(papers, feats_t))


def weight_kernel(feats_t, agg0, agg1, dpre0, dpre1, slots, papers, bundle):
    right = jnp.concatenate([dpre0[...], dpre1[...]], axis=0)
    aggs = jnp.concatenate([agg0[...], agg1[...]], axis=0)
    emb = aggs.shape[1]
    columns = right.shape[1] // LANES
    blocks = LANES // columns
    span = 2 * REL_ROWS
    where = iota((span * blocks, emb), 0)
    spread_rows = onehot(
        (where // span * REL_ROWS + where % span == iota((span * blocks, emb), 1))
        & (where % span < REL_ROWS)
    )
    aggs_t = dot(spread_rows, aggs, ((1,), (1,))).astype(BF16)
    for cb in range(columns):
        cols = right[:, cb * LANES : (cb + 1) * LANES]
        part_f = dot(feats_t[...], cols).astype(BF16)
        part_a = dot(aggs_t, cols)
        for i in range(blocks):
            d = cb * blocks + i
            bundle[d, :CAP, :] = slots[d]
            bundle[d, CAP:REL_AT, :] = part_f[i * SELF_ROWS : (i + 1) * SELF_ROWS]
            paper = papers[d].astype(F32)
            rel = part_a[i * span : (i + 1) * span] + paper[:span]
            bundle[d, REL_AT : REL_AT + span, :] = rel.astype(BF16)
            bundle[d, REL_AT + span :, :] = paper[span:].astype(BF16)


def weight_part(feats_t, agg0, agg1, dpre0, dpre1, slots, papers):
    return pl.pallas_call(
        weight_kernel,
        out_shape=jax.ShapeDtypeStruct((LANES, BUNDLE, LANES), BF16),
        in_specs=[VMEM] * 7,
        out_specs=VMEM,
        compiler_params=params(),
        name="weight_part",
    )(feats_t, agg0, agg1, dpre0, dpre1, slots, papers)


def sum_kernel(bundle, out, out_scr, sems):
    span = 2 * REL_ROWS
    half = [jnp.zeros((SELF_ROWS + span, LANES), F32) for _ in range(2)]
    for d in range(LANES):
        c = (d // GROUP) % 2
        half[c] = half[c] + bundle[d, CAP : REL_AT + span, :].astype(F32)
    rel = [h[SELF_ROWS : SELF_ROWS + REL_ROWS] for h in half]
    mine = jnp.concatenate([half[0][:SELF_ROWS], half[1][:SELF_ROWS], rel[0], rel[1]], axis=0)
    mine = mine.astype(BF16)
    for i in range(out_scr.shape[0]):
        out_scr[i] = mine
    q = out_scr.shape[0] // 4
    copies = fetch(
        [(out_scr.at[pl.ds(i * q, q)], out.at[pl.ds(i * q, q)]) for i in range(4)], sems
    )
    for c in copies:
        c.wait()


def sum_parts(bundle, peers):
    rows = 2 * (SELF_ROWS + REL_ROWS)
    return pl.pallas_call(
        sum_kernel,
        out_shape=pltpu.HBM((peers, rows, LANES), BF16),
        in_specs=[VMEM],
        out_specs=HBM,
        scratch_shapes=[
            pltpu.VMEM((peers, rows, LANES), BF16),
            pltpu.SemaphoreType.DMA((4,)),
        ],
        compiler_params=params(),
        name="sum_parts",
    )(bundle)


def spread_kernel(side, got, *rest):
    del side
    grad_self, grad_rel = rest[-2:]
    columns = got.shape[0]
    for cb in range(columns):
        rel = [[], []]
        for mp in range(GROUP):
            block = got[cb, 0, mp].astype(F32)
            for h in range(2):
                cols = slice((h * columns + cb) * LANES, (h * columns + cb + 1) * LANES)
                grad_self[mp * SELF_ROWS : (mp + 1) * SELF_ROWS, cols] = block[
                    h * SELF_ROWS : (h + 1) * SELF_ROWS
                ]
                at = 2 * SELF_ROWS + h * REL_ROWS
                rel[h].append(block[at : at + REL_ROWS])
        for h in range(2):
            cols = slice((h * columns + cb) * LANES, (h * columns + cb + 1) * LANES)
            grad_rel[:, cols] = jnp.concatenate(rel[h], axis=0)


def spread(side, got, feats, emb, hidden, others=()):
    columns = hidden // LANES // 2
    peers, rows, _ = got.shape
    steps = peers // columns // GROUP
    at = lambda i, side: (2 * i + side[0], 0)
    return pl.pallas_call(
        spread_kernel,
        grid_spec=pltpu.PrefetchScalarGridSpec(
            num_scalar_prefetch=1,
            grid=(steps,),
            in_specs=[
                pl.BlockSpec((columns, 1, GROUP, rows, LANES), lambda i, side: (0, i, 0, 0, 0))
            ]
            + [ANY] * len(others),
            out_specs=(
                pl.BlockSpec((feats // steps // 2, hidden), at),
                pl.BlockSpec((emb // steps // 2, hidden), at),
            ),
        ),
        out_shape=(
            jax.ShapeDtypeStruct((feats, hidden), F32),
            jax.ShapeDtypeStruct((emb, hidden), F32),
        ),
        input_output_aliases={2 + i: i for i in range(len(others))},
        compiler_params=params(),
        cost_estimate=pl.CostEstimate(
            flops=feats * hidden, bytes_accessed=3 * feats * hidden, transcendentals=0
        ),
        name="weight_out",
    )(side, got.reshape(columns, steps, GROUP, rows, LANES), *others)


def after_kernel(*refs):
    pass


def after(a, *ready):
    return pl.pallas_call(
        after_kernel,
        out_shape=jax.ShapeDtypeStruct(a.shape, a.dtype),
        in_specs=[ANY] * (1 + len(ready)),
        out_specs=ANY,
        input_output_aliases={0: 0},
        compiler_params=params(),
        name="after",
    )(a, *in_hbm(*ready))


def adam_kernel(
    wanted, bundle, table, m1, m2, new_table, new_m1, new_m2, done, arrived, hot_scr, side_scr, sem
):
    step = pl.program_id(0)
    lines = wanted.shape[0]
    done[...] = jnp.zeros_like(done)

    @pl.when(step == 0)
    def _():
        copy = pltpu.make_async_copy(bundle.at[:, pl.ds(0, CAP), :], arrived, sem.at[0])
        copy.start()
        lo = wanted[...] % 256
        hi = (wanted[...] // 256).astype(F32).T
        sub = iota((256, LANES), 0)
        for b in range(lines):
            at = slice(b * LANES, (b + 1) * LANES)
            hot_scr[:, at] = onehot(sub == lo[b : b + 1, :])
            side_scr[at, :] = jnp.broadcast_to(hi[:, b : b + 1], (LANES, LANES)).astype(BF16)
        copy.wait()

    here = side_scr[...] == step.astype(F32).astype(BF16)
    mark = jnp.where(here, BF16(1.0), BF16(0.0))
    got = arrived[...].reshape(LANES * CAP, LANES)
    both = dot(hot_scr[...], jnp.concatenate([got * mark, mark], axis=1))
    grad = both[:, :LANES]
    touched = both[:, LANES:] > 0.0
    m = 0.9 * m1[...] + 0.1 * grad
    v = 0.999 * m2[...] + 0.001 * grad * grad
    update = 0.05 * (m / (1.0 - 0.9**10)) / (jnp.sqrt(v / (1.0 - 0.999**10)) + 1e-08)
    new_table[...] = jnp.where(touched, table[...] - update, table[...])
    new_m1[...] = jnp.where(touched, m, m1[...])
    new_m2[...] = jnp.where(touched, v, m2[...])


def adam(wanted, bundle, table, m1, m2):
    rows = 256
    block = pl.BlockSpec((rows, LANES), lambda i: (i, 0))
    slots = LANES * CAP
    return pl.pallas_call(
        adam_kernel,
        grid=(table.shape[0] // rows,),
        out_shape=(jax.ShapeDtypeStruct(table.shape, F32),) * 3
        + (jax.ShapeDtypeStruct((8, LANES), F32),),
        in_specs=[pl.BlockSpec(wanted.shape, lambda i: (0, 0)), ANY, block, block, block],
        out_specs=(block, block, block, pl.BlockSpec((8, LANES), lambda i: (0, 0))),
        scratch_shapes=[
            pltpu.VMEM((LANES, CAP, LANES), BF16),
            pltpu.VMEM((rows, slots), BF16),
            pltpu.VMEM((slots, LANES), BF16),
            pltpu.SemaphoreType.DMA((1,)),
        ],
        cost_estimate=pl.CostEstimate(
            flops=2 * 2 * slots * LANES * table.shape[0],
            bytes_accessed=7 << 20,
            transcendentals=0,
        ),
        name="adam",
    )(wanted, bundle, table, m1, m2)


def shards(
    feats,
    edge_owner,
    edge_row,
    counts,
    table,
    moment1,
    moment2,
    w_self,
    w_rel,
    cotangent,
    next_owner,
    next_row,
    paper_table,
):
    every = ("chip", "core", "mp")
    peers = ("chip", "mp")
    devs = lax.axis_size(every)
    seeds, width = feats.shape
    hidden = cotangent.shape[1]
    emb = table.shape[1]
    core = lax.axis_index("core").astype(I32).reshape(1)
    group = lax.axis_index("mp").astype(I32).reshape(1)

    def exchange(a, axes):
        return lax.all_to_all(a, axes, split_axis=0, concat_axis=0, tiled=True)

    def swap(a):
        return lax.ppermute(a, "core", [(0, 1), (1, 0)])

    asked, seed_of, cnt, paper_pick, wide = place(
        group,
        edge_owner.reshape(-1, LANES),
        edge_row.reshape(-1, LANES),
        counts.reshape(1, -1),
        next_owner.reshape(1, -1),
        next_row.reshape(1, -1),
        table,
    )
    got = exchange(asked.reshape(devs, 1, LANES), every).reshape(devs, LANES)
    rows, wanted = gather(got, wide)
    fetched = exchange(rows.reshape(devs, CAP, emb), every).reshape(devs * CAP, emb)

    pre_self = prep(feats, w_self)
    feats_t = turn(feats, swap(feats))
    papers = paper_rows(got, paper_table)
    agg_b, dpre_here, dpre_there, grad = layer(
        core, fetched, seed_of, cnt, pre_self, w_rel, cotangent, feats_t, papers
    )

    agg_far, dpre_far = swap(agg_b), swap(dpre_there)
    slots, papers, feats_t = slot_grads(seed_of, grad, papers, feats_t)
    bundle = weight_part(feats_t, agg_b, agg_far, dpre_here, dpre_far, slots, papers)
    bundle = exchange(bundle, every)
    full = exchange(sum_parts(bundle, lax.axis_size(peers)), peers)
    new_table, new_moment1, new_moment2, done = adam(wanted, bundle, table, moment1, moment2)
    papers = bundle[:, PAPER_AT : PAPER_AT + FCAP * width // LANES, :].reshape(devs, -1)
    next_feats = functools.reduce(
        lambda a, b: a + b,
        [
            lax.dot_general(
                paper_pick[t],
                papers[:, t * width : (t + 1) * width],
                (((0,), (0,)), ((), ())),
                preferred_element_type=F32,
            )
            for t in range(FCAP)
        ],
    ).astype(BF16)
    full = after(full, done, next_feats)
    part = spread(core, full, width, emb, hidden)
    grad_self, grad_rel = spread(1 - core, swap(full), width, emb, hidden, part)
    return (new_table, new_moment1, new_moment2, grad_self, grad_rel, next_feats)


def solution(mesh):
    n_mp = mesh.shape["mp"]
    wide = Mesh(mesh.devices.reshape(-1, 2, n_mp), ("chip", "core", "mp"))
    rows = P(("chip", "core", "mp"), None)
    line = P(("chip", "core", "mp"))
    in_specs = (rows, rows, line, line, rows, rows, rows, P(), P(), rows, rows, line, rows)
    out_specs = (rows, rows, rows, P(), P(), rows)
    return jax.shard_map(shards, mesh=wide, in_specs=in_specs, out_specs=out_specs, check_vma=False)
```

time: 134 us -> 123 us (0.918)
  local copies, waits for them, and re-layouts: 8.49 us -> 2.79 us
  waiting for transfers between devices: 12.4 us -> 16.2 us
  Pallas kernels: 33.9 us -> 30.7 us
  blocking collectives: 61.3 us -> 58.3 us
    all_to_all x2, waiting for transfers between devices: 10.1 us -> 15.9 us  [exchange(): return lax.all_to_all(a, axes, split_axis=0, concat_axis=0, tiled=True)]
    pallas_call x8 -> x10, Pallas kernels: 22.2 us -> 17.8 us  [the longest x1 3.89 us: gather(): pl.pallas_call(gather_kernel, out_shape=(pltpu.HBM((slots, LANES), BF16),...]
    unnamed x27 -> x8, local copies, waits for them, and re-layouts: 4.44 us -> 0.41 us
    all_to_all x2, blocking collectives: 61.3 us -> 58.3 us  [exchange(): return lax.all_to_all(a, axes, split_axis=0, concat_axis=0, tiled=True)]
    ppermute x4, waiting for transfers between devices: 2.32 us -> 0.26 us  [swap(): return lax.ppermute(a, 'core', [(0, 1), (1, 0)])]
    slice x2, local copies, waits for them, and re-layouts: 0.42 us -> 2.38 us  [shards(): bundle[:, PAPER_AT:PAPER_AT + FCAP * width // LANES, :].reshape(devs, -1)]
  transfers between devices with their start and end apart: 6 -> 6, of which waited for: 3 -> 3; matrix products, arithmetic and copies ran while one was open for 5% -> 3% of each run, Pallas kernels for 13% -> 14%
where the time goes in v4:
time: 123 us
  blocking collectives  58.3 us (47%)
  Pallas kernels  30.7 us (25%)
  waiting for transfers between devices  16.2 us (13%)
  starting transfers between devices  12.8 us (10%)
  local copies, waits for them, and re-layouts  2.79 us (2%)
    all_to_all x2, blocking collectives, exchange(): return lax.all_to_all(a, axes, split_axis=0, concat_axis=0, tiled=True)  58.3 us
    all_to_all x2, waiting for transfers between devices, exchange(): return lax.all_to_all(a, axes, split_axis=0, concat_axis=0, tiled=True)  15.9 us
    pallas_call x1, Pallas kernels, adam(): pl.pallas_call(adam_kernel, grid=(table.shape[0] // rows,), out_shape=(ja...  10.8 us
    all_to_all x2, starting transfers between devices, exchange(): return lax.all_to_all(a, axes, split_axis=0, concat_axis=0, tiled=True)  9.16 us
    pallas_call x1, Pallas kernels, gather(): pl.pallas_call(gather_kernel, out_shape=(pltpu.HBM((slots, LANES), BF16),...  3.89 us
    pallas_call x2, Pallas kernels, spread(): pl.pallas_call(spread_kernel, grid_spec=pltpu.PrefetchScalarGridSpec(num_...  3.7 us
    ppermute x4, starting transfers between devices, swap(): return lax.ppermute(a, 'core', [(0, 1), (1, 0)])  3.67 us
    pallas_call x1, Pallas kernels, place(): pl.pallas_call(place_kernel, out_shape=(pltpu.HBM((devs, LANES), I32), ja...  3.08 us
  transfers between devices with their start and end apart: 6, of which 3 were waited for; matrix products, arithmetic and copies ran while one was open for 3% of the time, Pallas kernels for 14%

profile of v4, /device:TPU:1, one launch (start us, length us, event | category | flops | bytes accessed | tf_op | source)
XLA Modules:
  0.0 122.7 jit_solution(12096152514293524432)
XLA Ops:
  0.7 3.1 %place.1 = (s32[128,128]{1,0:T(8,128)}, s32[32,128]{1,0:T(8,128)S(1)}, f32[128,128]{1,0:T(8,128)S(1)}, bf16[2,128,128]{2,1,0:T(8,128)(2,1)S(1)}, bf16[256,1024]{1,0:T(8,128)(2,1)S(1)}) custom-call(s32[1]{0:T(128)} %bitcast.lane_group, s32[16,128]{1,0:T(8,128)} %bitcast.31, s32[16,128]{1,0:T(8,128)} %bitcast.32, s32[1,128]{1,0:T(1,128)} %bitcast.33, ...), custom_call_target="tpu_custom_call" | custom-call | tf_op jit(solution)/shard_map/place/pallas_call | solution.py:180
  3.7 21.1 %all_to_all.20 = s32[128,1,128]{2,1,0:T(1,128)S(1)} all-to-all(s32[128,1,128]{2,1,0:T(1,128)} %bitcast.30), channel_id=1, replica_groups=mesh['chip'=16,'core'=2,'mp'=4] {'chip','core','mp'}, dimensions={0} | all-to-all | bytes 131072 | tf_op jit(solution)/shard_map/all_to_all | solution.py:646
  24.8 3.9 %gather_rows.1 = (bf16[4096,128]{1,0:T(8,128)(2,1)}, s32[32,128]{1,0:T(8,128)}) custom-call(s32[128,128]{1,0:T(8,128)S(1)} %bitcast.25, bf16[256,1024]{1,0:T(8,128)(2,1)S(1)} %get-tuple-element.29.wide), custom_call_target="tpu_custom_call" | custom-call | tf_op jit(solution)/shard_map/gather_rows/pallas_call | solution.py:233
  28.7 4.3 %all-to-all-start.1 = ((bf16[128,32,128]{2,1,0:T(8,128)(2,1)}), bf16[128,32,128]{2,1,0:T(8,128)(2,1)S(1)}, u32[]{:S(2)}, u32[]{:S(2)}) async-start(bf16[128,32,128]{2,1,0:T(8,128)(2,1)} %bitcast.29), calls=%async_computation.1 | async-start | bytes 2097152 | tf_op jit(solution)/shard_map/all_to_all | solution.py:646
  33.1 1.1 collective-permute-start
  34.2 1.2 prep.1.pre_in
  35.8 1.7 %gather_papers.1.rest_1_.papers_in = bf16[128,16,128]{2,1,0:T(8,128)(2,1)} custom-call(s32[128,128]{1,0:T(8,128)S(1)} %bitcast.26, bf16[1024,768]{1,0:T(8,128)(2,1)S(1)} %copy-done.2), custom_call_target="tpu_custom_call" | custom-call | flops 402653184 | bytes 3145728 | tf_op jit(solution)/shard_map/gather_papers/pallas_call | solution.py:274
  37.5 0.9 turn.1.rest_0_.feats_in
  38.4 14.0 %all-to-all-done.1 = bf16[128,32,128]{2,1,0:T(8,128)(2,1)S(1)} async-done(((bf16[128,32,128]{2,1,0:T(8,128)(2,1)}), bf16[128,32,128]{2,1,0:T(8,128)(2,1)S(1)}, u32[]{:S(2)}, u32[]{:S(2)}) %all-to-all-start.1) | async-done | bytes 1048608 | tf_op jit(solution)/shard_map/all_to_all | solution.py:646
  52.5 2.1 %layer.1 = (bf16[128,128]{1,0:T(8,128)(2,1)S(1)}, bf16[128,512]{1,0:T(8,128)(2,1)S(1)}, bf16[128,512]{1,0:T(8,128)(2,1)S(1)}, bf16[128,128]{1,0:T(8,128)(2,1)S(1)}) custom-call(s32[1]{0:T(128)} %bitcast.9.core.side, bf16[4096,128]{1,0:T(8,128)(2,1)S(1)} %bitcast.23, s32[32,128]{1,0:T(8,128)S(1)} %get-tuple-element.31.seed_of, ...), custom_call_target="tpu_custom_call" | custom-call | tf_op jit(solution)/shard_map/layer/pallas_call | solution.py:367
  54.6 0.5 collective-permute-start.2
  55.2 1.2 slot_grads.1
  56.4 0.8 weight_part.1
  57.2 37.2 %all_to_all.21.bundle = bf16[128,72,128]{2,1,0:T(8,128)(2,1)S(1)} all-to-all(bf16[128,72,128]{2,1,0:T(8,128)(2,1)S(1)} %weight_part.1), channel_id=1, replica_groups=mesh['chip'=16,'core'=2,'mp'=4] {'chip','core','mp'}, dimensions={0} | all-to-all | bytes 4718592 | tf_op jit(solution)/shard_map/all_to_all | solution.py:646
  94.4 1.3 %sum_parts.1 = bf16[64,56,128]{2,1,0:T(8,128)(2,1)} custom-call(bf16[128,72,128]{2,1,0:T(8,128)(2,1)S(1)} %all_to_all.21.bundle), custom_call_target="tpu_custom_call" | custom-call | tf_op jit(solution)/shard_map/sum_parts/pallas_call | solution.py:479
  95.8 4.8 %all-to-all-start.3 = ((bf16[64,56,128]{2,1,0:T(8,128)(2,1)}), bf16[64,56,128]{2,1,0:T(8,128)(2,1)S(1)}, u32[]{:S(2)}, u32[]{:S(2)}) async-start(bf16[64,56,128]{2,1,0:T(8,128)(2,1)} %sum_parts.1), calls=%async_computation.3 | async-start | bytes 1835008 | tf_op jit(solution)/shard_map/all_to_all | solution.py:646
  100.6 1.0 slice.20
  101.6 1.4 %copy.24 = bf16[128,12,128]{0,2,1:T(8,128)(2,1)S(1)} copy(bf16[128,12,128]{2,1,0:T(8,128)(2,1)} %slice.20) | data formatting | bytes 786432 | tf_op jit(solution)/shard_map/slice | solution.py:677
  103.2 0.9 fusion.refs_2_
  104.1 10.8 %adam.1 = (f32[2048,128]{1,0:T(8,128)}, f32[2048,128]{1,0:T(8,128)}, f32[2048,128]{1,0:T(8,128)}, f32[8,128]{1,0:T(8,128)}) custom-call(s32[32,128]{1,0:T(8,128)} %get-tuple-element.30.wanted, bf16[128,72,128]{2,1,0:T(8,128)(2,1)} %copy-done, f32[2048,128]{1,0:T(8,128)} %table.1, f32[2048,128]{1,0:T(8,128)} %m1.1, f32[2048,128]{1,0:T(8,128)} %m2.1), custom_call_target="tpu_custom_call" | custom-call | flops 4294967296 | bytes 7340032 | tf_op jit(solution)/shard_map/adam/pallas_call | solution.py:599
  114.9 1.9 %all-to-all-done.3.refs_0_ = bf16[64,56,128]{2,1,0:T(8,128)(2,1)S(1)} async-done(((bf16[64,56,128]{2,1,0:T(8,128)(2,1)}), bf16[64,56,128]{2,1,0:T(8,128)(2,1)S(1)}, u32[]{:S(2)}, u32[]{:S(2)}) %all-to-all-start.3) | async-done | bytes 917536 | tf_op jit(solution)/shard_map/all_to_all | solution.py:646
  116.8 1.9 %collective-permute-start.3 = (bf16[64,56,128]{2,1,0:T(8,128)(2,1)S(1)}, bf16[64,56,128]{2,1,0:T(8,128)(2,1)S(1)}, u32[]{:S(2)}, u32[]{:S(2)}) collective-permute-start(bf16[64,56,128]{2,1,0:T(8,128)(2,1)S(1)} %after.1), channel_id=1, source_target_pairs={{0,4},{4,0},{1,5},{5,1},{2,6},{6,2},{3,7},{7,3},{8,12},{12,8},{9,1... | collective-permute-start | bytes 2752520 | tf_op jit(solution)/shard_map/ppermute | solution.py:649
  118.7 1.8 %weight_out.2 = (f32[768,1024]{1,0:T(8,128)}, f32[128,1024]{1,0:T(8,128)}) custom-call(s32[1]{0:T(128)} %bitcast.9.core.side, bf16[4,4,4,56,128]{4,3,2,1,0:T(8,128)(2,1)S(1)} %bitcast.22), custom_call_target="tpu_custom_call" | custom-call | flops 786432 | bytes 2359296 | tf_op jit(solution)/shard_map/weight_out/pallas_call | solution.py:518
  120.8 1.8 %weight_out.3 = (f32[768,1024]{1,0:T(8,128)}, f32[128,1024]{1,0:T(8,128)}) custom-call(s32[1]{0:T(128)S(6)} %sub.3.side, bf16[4,4,4,56,128]{4,3,2,1,0:T(8,128)(2,1)S(1)} %bitcast.24, f32[768,1024]{1,0:T(8,128)} %get-tuple-element.46.rest_0_, f32[128,1024]{1,0:T(8,128)} %get-tuple-element.47.rest_1_), custom_call_target="tpu_custom_call", output_to_operand_aliasing={{0}: (2, {}), {1}: (3, {})} | custom-call | flops 786432 | bytes 2359296 | tf_op jit(solution)/shard_map/weight_out/pallas_call | solution.py:518
  (15 shorter events, 1.0 us)
Async XLA Ops:
  0.6 32.4 %copy-start.3 = (bf16[128,768]{1,0:T(8,128)(2,1)S(1)}, bf16[128,768]{1,0:T(8,128)(2,1)}, u32[]{:S(2)}) copy-start(bf16[128,768]{1,0:T(8,128)(2,1)} %feats.3) | copy-start | bytes 589828
  0.6 33.6 %copy-start.1 = (bf16[768,1024]{1,0:T(8,128)(2,1)S(1)}, bf16[768,1024]{1,0:T(8,128)(2,1)}, u32[]{:S(2)}) copy-start(bf16[768,1024]{1,0:T(8,128)(2,1)} %w_self.1) | copy-start | bytes 4718596
  28.7 23.7 %all-to-all-start.1 = ((bf16[128,32,128]{2,1,0:T(8,128)(2,1)}), bf16[128,32,128]{2,1,0:T(8,128)(2,1)S(1)}, u32[]{:S(2)}, u32[]{:S(2)}) async-start(bf16[128,32,128]{2,1,0:T(8,128)(2,1)} %bitcast.29), calls=%async_computation.1 | async-start | bytes 2097152 | tf_op jit(solution)/shard_map/all_to_all | solution.py:646
  33.1 4.5 %collective-permute-start = (bf16[128,768]{1,0:T(8,128)(2,1)S(1)}, bf16[128,768]{1,0:T(8,128)(2,1)S(1)}, u32[]{:S(2)}, u32[]{:S(2)}) collective-permute-start(bf16[128,768]{1,0:T(8,128)(2,1)S(1)} %copy-done.3), channel_id=1, source_target_pairs={{0,4},{4,0},{1,5},{5,1},{2,6},{6,2},{3,7},{7,3},{8,12},{12,8},{9,1... | collective-permute-start | bytes 589832 | tf_op jit(solution)/shard_map/ppermute | solution.py:649
  34.2 1.6 %copy-start.2 = (bf16[1024,768]{1,0:T(8,128)(2,1)S(1)}, bf16[1024,768]{1,0:T(8,128)(2,1)}, u32[]{:S(2)}) copy-start(bf16[1024,768]{1,0:T(8,128)(2,1)} %paper.1) | copy-start | bytes 4718596
  54.6 1.8 %collective-permute-start.2 = (bf16[128,512]{1,0:T(8,128)(2,1)S(1)}, bf16[128,512]{1,0:T(8,128)(2,1)S(1)}, u32[]{:S(2)}, u32[]{:S(2)}) collective-permute-start(bf16[128,512]{1,0:T(8,128)(2,1)S(1)} %get-tuple-element.38), channel_id=1, source_target_pairs={{0,4},{4,0},{1,5},{5,1},{2,6},{6,2},{3,7},{7,3},{8,12},{12,8},{9,1... | collective-permute-start | bytes 393224 | tf_op jit(solution)/shard_map/ppermute | solution.py:649
  55.1 1.3 %collective-permute-start.1 = (bf16[128,128]{1,0:T(8,128)(2,1)S(1)}, bf16[128,128]{1,0:T(8,128)(2,1)S(1)}, u32[]{:S(2)}, u32[]{:S(2)}) collective-permute-start(bf16[128,128]{1,0:T(8,128)(2,1)S(1)} %get-tuple-element.36.agg0), channel_id=1, source_target_pairs={{0,4},{4,0},{1,5},{5,1},{2,6},{6,2},{3,7},{7,3},{8,12},{12,8},{9,1... | collective-permute-start | bytes 98312 | tf_op jit(solution)/shard_map/ppermute | solution.py:649
  94.4 6.2 %copy-start = (bf16[128,72,128]{2,1,0:T(8,128)(2,1)}, bf16[128,72,128]{2,1,0:T(8,128)(2,1)S(1)}, u32[]{:S(2)}) copy-start(bf16[128,72,128]{2,1,0:T(8,128)(2,1)S(1)} %all_to_all.21.bundle) | copy-start | bytes 7077892
  95.8 21.0 %all-to-all-start.3 = ((bf16[64,56,128]{2,1,0:T(8,128)(2,1)}), bf16[64,56,128]{2,1,0:T(8,128)(2,1)S(1)}, u32[]{:S(2)}, u32[]{:S(2)}) async-start(bf16[64,56,128]{2,1,0:T(8,128)(2,1)} %sum_parts.1), calls=%async_computation.3 | async-start | bytes 1835008 | tf_op jit(solution)/shard_map/all_to_all | solution.py:646
  116.8 4.0 %collective-permute-start.3 = (bf16[64,56,128]{2,1,0:T(8,128)(2,1)S(1)}, bf16[64,56,128]{2,1,0:T(8,128)(2,1)S(1)}, u32[]{:S(2)}, u32[]{:S(2)}) collective-permute-start(bf16[64,56,128]{2,1,0:T(8,128)(2,1)S(1)} %after.1), channel_id=1, source_target_pairs={{0,4},{4,0},{1,5},{5,1},{2,6},{6,2},{3,7},{7,3},{8,12},{12,8},{9,1... | collective-permute-start | bytes 2752520 | tf_op jit(solution)/shard_map/ppermute | solution.py:649

commit v5 on v4

--- a/solution.py
+++ b/solution.py
@@ -180,7 +180,7 @@
     return pl.pallas_call(
         place_kernel,
         out_shape=(
-            pltpu.HBM((devs, LANES), I32),
+            pltpu.VMEM((devs, LANES), I32),
             jax.ShapeDtypeStruct((devs // GROUP, LANES), I32),
             jax.ShapeDtypeStruct((devs, LANES), F32),
             jax.ShapeDtypeStruct((FCAP, devs, LANES), BF16),
@@ -249,7 +249,8 @@
     )(got, wide)
 
 
-def paper_kernel(got, paper, rows, scr):
+def paper_kernel(got, paper_in, rows, paper, scr, sem):
+    copies = fetch([(paper_in, paper)], sem)
     devs = LANES
     sub = iota((devs, LANES), 0)
     lane = iota((devs, LANES), 1)
@@ -258,6 +259,7 @@
     span = REL_ROWS + PAPER_ROWS
     for i in range(REL_ROWS):
         scr[pl.ds(i, devs, stride=span), :] = jnp.zeros((devs, LANES), F32)
+    copies[0].wait()
     for t in range(FCAP):
         asked = jnp.sum(jnp.where(lane == first + t, got[...], 0), axis=1, keepdims=True)
         hot = onehot(asked == iota((devs, paper.shape[0]), 1))
@@ -274,9 +276,13 @@
     return pl.pallas_call(
         paper_kernel,
         out_shape=pltpu.HBM((LANES, span, LANES), BF16),
-        in_specs=[VMEM, VMEM],
+        in_specs=[VMEM, HBM],
         out_specs=VMEM,
-        scratch_shapes=[pltpu.VMEM((LANES * span, LANES), F32)],
+        scratch_shapes=[
+            pltpu.VMEM(paper.shape, BF16),
+            pltpu.VMEM((LANES * span, LANES), F32),
+            pltpu.SemaphoreType.DMA((1,)),
+        ],
         compiler_params=params(),
         cost_estimate=pl.CostEstimate(
             flops=2 * FCAP * LANES * paper.shape[0] * paper.shape[1],
@@ -284,25 +290,34 @@
             transcendentals=0,
         ),
         name="gather_papers",
-    )(got, paper)
-
-
-def prep_kernel(feats, w_self, pre):
+    )(got, *in_hbm(paper))
+
+
+def prep_kernel(feats, w_self_in, cot_in, w_in, pre, cot, w_rel, w_self, sems):
+    copies = fetch([(w_self_in, w_self), (cot_in, cot), (w_in, w_rel)], sems)
+    copies[0].wait()
     pre[...] = dot(feats[...], w_self[...])
-
-
-def prep(feats, w_self):
+    for c in copies[1:]:
+        c.wait()
+
+
+def prep(feats, w_self, cotangent, w_rel):
     return pl.pallas_call(
         prep_kernel,
-        out_shape=pltpu.HBM((feats.shape[0], w_self.shape[1]), F32),
-        in_specs=[VMEM, VMEM],
-        out_specs=VMEM,
+        out_shape=(
+            pltpu.VMEM(cotangent.shape, F32),
+            pltpu.VMEM(cotangent.shape, F32),
+            pltpu.VMEM(w_rel.shape, BF16),
+        ),
+        in_specs=[VMEM, HBM, HBM, HBM],
+        out_specs=(VMEM, VMEM, VMEM),
+        scratch_shapes=[pltpu.VMEM(w_self.shape, BF16), pltpu.SemaphoreType.DMA((3,))],
         compiler_params=params(),
         cost_estimate=pl.CostEstimate(
             flops=2 * feats.size * w_self.shape[1], bytes_accessed=4 << 20, transcendentals=0
         ),
         name="prep",
-    )(feats, w_self)
+    )(feats, *in_hbm(w_self, cotangent, w_rel))
 
 
 def turn_kernel(feats, far, out):
@@ -329,13 +344,12 @@
     fetched,
     seed_of,
     cnt,
-    pre_in,
-    w_in,
-    cot_in,
+    pre_self,
+    cot,
+    w_rel,
     *rest,
 ):
-    agg_out, here_out, there_out, grad_out, pre_self, w_rel, cot, sems = rest[-8:]
-    copies = fetch([(w_in, w_rel), (pre_in, pre_self), (cot_in, cot)], sems)
+    agg_out, here_out, there_out, grad_out = rest[-4:]
     devs = LANES
     lines = seed_of.shape[0]
     seed1 = iota((devs, LANES), 0) + 1
@@ -349,8 +363,6 @@
     count = cnt[...]
     agg_b = (agg / count).astype(BF16)
     agg_out[...] = agg_b
-    for c in copies:
-        c.wait()
     pre = pre_self[...] + dot(agg_b, w_rel[...])
     sig = jax.nn.sigmoid(pre)
     dpre = (cot[...] * sig * (1.0 + pre * (1.0 - sig))).astype(BF16)
@@ -362,7 +374,7 @@
     grad_out[...] = (dagg / count).astype(BF16)
 
 
-def layer(core, fetched, seed_of, cnt, pre_self, w_rel, cotangent, *ready):
+def layer(core, fetched, seed_of, cnt, pre_self, cotangent, w_rel, *ready):
     seeds, hidden = cotangent.shape
     return pl.pallas_call(
         layer_kernel,
@@ -372,17 +384,11 @@
             jax.ShapeDtypeStruct((seeds, hidden // 2), BF16),
             jax.ShapeDtypeStruct((seeds, LANES), BF16),
         ),
-        in_specs=[SMEM] + [VMEM] * 3 + [HBM] * 3 + [ANY] * len(ready),
+        in_specs=[SMEM] + [VMEM] * 6 + [ANY] * len(ready),
         out_specs=(VMEM, VMEM, VMEM, VMEM),
-        scratch_shapes=[
-            pltpu.VMEM(pre_self.shape, F32),
-            pltpu.VMEM(w_rel.shape, BF16),
-            pltpu.VMEM(cotangent.shape, F32),
-            pltpu.SemaphoreType.DMA((3,)),
-        ],
         compiler_params=params(),
         name="layer",
-    )(core, fetched, seed_of, cnt, *in_hbm(pre_self, w_rel, cotangent, *ready))
+    )(core, fetched, seed_of, cnt, pre_self, cotangent, w_rel, *in_hbm(*ready))
 
 
 def slots_kernel(seed_of, grad, papers_in, feats_in, out, papers, feats, sems):
@@ -491,48 +497,55 @@
 
 
 def spread_kernel(side, got, *rest):
-    del side
-    grad_self, grad_rel = rest[-2:]
-    columns = got.shape[0]
-    for cb in range(columns):
-        rel = [[], []]
-        for mp in range(GROUP):
-            block = got[cb, 0, mp].astype(F32)
+    grad_self, grad_rel, self_scr, rel_scr, sems = rest[-5:]
+    columns, steps = got.shape[:2]
+    copies = []
+    rows_self = GROUP * SELF_ROWS
+    rows_rel = GROUP * REL_ROWS
+    for i in range(steps):
+        for cb in range(columns):
+            rel = [[], []]
+            for mp in range(GROUP):
+                block = got[cb, i, mp].astype(F32)
+                for h in range(2):
+                    cols = slice((h * columns + cb) * LANES, (h * columns + cb + 1) * LANES)
+                    self_scr[i, mp * SELF_ROWS : (mp + 1) * SELF_ROWS, cols] = block[
+                        h * SELF_ROWS : (h + 1) * SELF_ROWS
+                    ]
+                    at = 2 * SELF_ROWS + h * REL_ROWS
+                    rel[h].append(block[at : at + REL_ROWS])
             for h in range(2):
                 cols = slice((h * columns + cb) * LANES, (h * columns + cb + 1) * LANES)
-                grad_self[mp * SELF_ROWS : (mp + 1) * SELF_ROWS, cols] = block[
-                    h * SELF_ROWS : (h + 1) * SELF_ROWS
-                ]
-                at = 2 * SELF_ROWS + h * REL_ROWS
-                rel[h].append(block[at : at + REL_ROWS])
-        for h in range(2):
-            cols = slice((h * columns + cb) * LANES, (h * columns + cb + 1) * LANES)
-            grad_rel[:, cols] = jnp.concatenate(rel[h], axis=0)
+                rel_scr[i, :, cols] = jnp.concatenate(rel[h], axis=0)
+        block_at = 2 * i + side[0]
+        copies += fetch(
+            [
+                (self_scr.at[i], grad_self.at[pl.ds(block_at * rows_self, rows_self), :]),
+                (rel_scr.at[i], grad_rel.at[pl.ds(block_at * rows_rel, rows_rel), :]),
+            ],
+            sems.at[i],
+        )
+    for c in copies:
+        c.wait()
 
 
 def spread(side, got, feats, emb, hidden, others=()):
     columns = hidden // LANES // 2
     peers, rows, _ = got.shape
     steps = peers // columns // GROUP
-    at = lambda i, side: (2 * i + side[0], 0)
     return pl.pallas_call(
         spread_kernel,
-        grid_spec=pltpu.PrefetchScalarGridSpec(
-            num_scalar_prefetch=1,
-            grid=(steps,),
-            in_specs=[
-                pl.BlockSpec((columns, 1, GROUP, rows, LANES), lambda i, side: (0, i, 0, 0, 0))
-            ]
-            + [ANY] * len(others),
-            out_specs=(
-                pl.BlockSpec((feats // steps // 2, hidden), at),
-                pl.BlockSpec((emb // steps // 2, hidden), at),
-            ),
-        ),
         out_shape=(
-            jax.ShapeDtypeStruct((feats, hidden), F32),
-            jax.ShapeDtypeStruct((emb, hidden), F32),
-        ),
+            pltpu.HBM((feats, hidden), F32),
+            pltpu.HBM((emb, hidden), F32),
+        ),
+        in_specs=[SMEM, VMEM] + [HBM] * len(others),
+        out_specs=(HBM, HBM),
+        scratch_shapes=[
+            pltpu.VMEM((steps, GROUP * SELF_ROWS, hidden), F32),
+            pltpu.VMEM((steps, GROUP * REL_ROWS, hidden), F32),
+            pltpu.SemaphoreType.DMA((steps, 2)),
+        ],
         input_output_aliases={2 + i: i for i in range(len(others))},
         compiler_params=params(),
         cost_estimate=pl.CostEstimate(
@@ -661,11 +674,11 @@
     rows, wanted = gather(got, wide)
     fetched = exchange(rows.reshape(devs, CAP, emb), every).reshape(devs * CAP, emb)
 
-    pre_self = prep(feats, w_self)
+    pre_self, cot, w_rel = prep(feats, w_self, cotangent, w_rel)
     feats_t = turn(feats, swap(feats))
     papers = paper_rows(got, paper_table)
     agg_b, dpre_here, dpre_there, grad = layer(
-        core, fetched, seed_of, cnt, pre_self, w_rel, cotangent, feats_t, papers
+        core, fetched, seed_of, cnt, pre_self, cot, w_rel, feats_t, papers
     )
 
     agg_far, dpre_far = swap(agg_b), swap(dpre_there)

time: 123 us -> 121 us (0.984)
    all_to_all x2, waiting for transfers between devices: 15.9 us -> 14.2 us  [exchange(): return lax.all_to_all(a, axes, split_axis=0, concat_axis=0, tiled=True)]
    pallas_call x1, Pallas kernels: 1.74 us -> 3.14 us  [paper_rows(): pl.pallas_call(paper_kernel, out_shape=pltpu.HBM((LANES, span, LANES), BF...]
  transfers between devices with their start and end apart: 6 -> 6, of which waited for: 3 -> 3; matrix products, arithmetic and copies ran while one was open for 3% -> 3% of each run, Pallas kernels for 14% -> 16%
where the time goes in v5:
time: 121 us; the launch traced here: 120 us
  blocking collectives  58.1 us (48%)
  Pallas kernels  29.9 us (25%)
  waiting for transfers between devices  15 us (12%)
  starting transfers between devices  12.8 us (11%)
  local copies, waits for them, and re-layouts  2.39 us (2%)
    all_to_all x2, blocking collectives, exchange(): return lax.all_to_all(a, axes, split_axis=0, concat_axis=0, tiled=True)  58.1 us
    all_to_all x2, waiting for transfers between devices, exchange(): return lax.all_to_all(a, axes, split_axis=0, concat_axis=0, tiled=True)  14.2 us
    pallas_call x1, Pallas kernels, adam(): pl.pallas_call(adam_kernel, grid=(table.shape[0] // rows,), out_shape=(ja...  10.8 us
    all_to_all x2, starting transfers between devices, exchange(): return lax.all_to_all(a, axes, split_axis=0, concat_axis=0, tiled=True)  9.15 us
    pallas_call x1, Pallas kernels, gather(): pl.pallas_call(gather_kernel, out_shape=(pltpu.HBM((slots, LANES), BF16),...  3.92 us
    ppermute x4, starting transfers between devices, swap(): return lax.ppermute(a, 'core', [(0, 1), (1, 0)])  3.67 us
    pallas_call x1, Pallas kernels, paper_rows(): pl.pallas_call(paper_kernel, out_shape=pltpu.HBM((LANES, span, LANES), BF...  3.14 us
    pallas_call x2, Pallas kernels, spread(): pl.pallas_call(spread_kernel, out_shape=(pltpu.HBM((feats, hidden), F32),...  2.65 us
  transfers between devices with their start and end apart: 6, of which 3 were waited for; matrix products, arithmetic and copies ran while one was open for 3% of the time, Pallas kernels for 16%

profile of v5, /device:TPU:1, one launch (start us, length us, event | category | flops | bytes accessed | tf_op | source)
XLA Modules:
  0.0 120.4 jit_solution(14602163392221586900)
XLA Ops:
  0.6 2.5 %place.1 = (s32[128,128]{1,0:T(8,128)S(1)}, s32[32,128]{1,0:T(8,128)S(1)}, f32[128,128]{1,0:T(8,128)S(1)}, bf16[2,128,128]{2,1,0:T(8,128)(2,1)S(1)}, bf16[256,1024]{1,0:T(8,128)(2,1)S(1)}) custom-call(s32[1]{0:T(128)} %bitcast.lane_group, s32[16,128]{1,0:T(8,128)} %bitcast.31, s32[16,128]{1,0:T(8,128)} %bitcast.32, s32[1,128]{1,0:T(1,128)} %bitcast.33, ...), custom_call_target="tpu_custom_call" | custom-call | tf_op jit(solution)/shard_map/place/pallas_call | solution.py:180
  3.1 20.9 %all_to_all.20 = s32[128,1,128]{2,1,0:T(1,128)S(1)} all-to-all(s32[128,1,128]{2,1,0:T(1,128)S(1)} %bitcast.27), channel_id=1, replica_groups=mesh['chip'=16,'core'=2,'mp'=4] {'chip','core','mp'}, dimensions={0} | all-to-all | bytes 131072 | tf_op jit(solution)/shard_map/all_to_all | solution.py:659
  24.1 3.9 %gather_rows.1 = (bf16[4096,128]{1,0:T(8,128)(2,1)}, s32[32,128]{1,0:T(8,128)}) custom-call(s32[128,128]{1,0:T(8,128)S(1)} %bitcast.25, bf16[256,1024]{1,0:T(8,128)(2,1)S(1)} %get-tuple-element.32.wide), custom_call_target="tpu_custom_call" | custom-call | tf_op jit(solution)/shard_map/gather_rows/pallas_call | solution.py:233
  28.0 4.3 %all-to-all-start.1 = ((bf16[128,32,128]{2,1,0:T(8,128)(2,1)}), bf16[128,32,128]{2,1,0:T(8,128)(2,1)S(1)}, u32[]{:S(2)}, u32[]{:S(2)}) async-start(bf16[128,32,128]{2,1,0:T(8,128)(2,1)} %bitcast.30), calls=%async_computation.1 | async-start | bytes 2097152 | tf_op jit(solution)/shard_map/all_to_all | solution.py:659
  32.3 1.1 collective-permute-start
  33.5 1.8 %prep.1 = (f32[128,1024]{1,0:T(8,128)S(1)}, f32[128,1024]{1,0:T(8,128)S(1)}, bf16[128,1024]{1,0:T(8,128)(2,1)S(1)}) custom-call(bf16[128,768]{1,0:T(8,128)(2,1)S(1)} %copy-done.1, bf16[768,1024]{1,0:T(8,128)(2,1)} %w_self_in.1, f32[128,1024]{1,0:T(8,128)} %cot_in.1, bf16[128,1024]{1,0:T(8,128)(2,1)} %w_in.1), custom_call_target="tpu_custom_call" | custom-call | flops 201326592 | bytes 4194304 | tf_op jit(solution)/shard_map/prep/pallas_call | solution.py:305
  35.3 3.1 %gather_papers.1.rest_1_.papers_in = bf16[128,16,128]{2,1,0:T(8,128)(2,1)} custom-call(s32[128,128]{1,0:T(8,128)S(1)} %bitcast.26, bf16[1024,768]{1,0:T(8,128)(2,1)} %paper_in.1), custom_call_target="tpu_custom_call" | custom-call | flops 402653184 | bytes 3145728 | tf_op jit(solution)/shard_map/gather_papers/pallas_call | solution.py:276
  38.5 0.9 turn.1.rest_0_.feats_in
  39.4 12.4 %all-to-all-done.1 = bf16[128,32,128]{2,1,0:T(8,128)(2,1)S(1)} async-done(((bf16[128,32,128]{2,1,0:T(8,128)(2,1)}), bf16[128,32,128]{2,1,0:T(8,128)(2,1)S(1)}, u32[]{:S(2)}, u32[]{:S(2)}) %all-to-all-start.1) | async-done | bytes 1048608 | tf_op jit(solution)/shard_map/all_to_all | solution.py:659
  51.8 0.9 layer.1
  53.2 1.2 slot_grads.1
  54.5 0.8 weight_part.1
  55.3 37.2 %all_to_all.21.bundle = bf16[128,72,128]{2,1,0:T(8,128)(2,1)S(1)} all-to-all(bf16[128,72,128]{2,1,0:T(8,128)(2,1)S(1)} %weight_part.1), channel_id=1, replica_groups=mesh['chip'=16,'core'=2,'mp'=4] {'chip','core','mp'}, dimensions={0} | all-to-all | bytes 4718592 | tf_op jit(solution)/shard_map/all_to_all | solution.py:659
  92.5 1.3 %sum_parts.1 = bf16[64,56,128]{2,1,0:T(8,128)(2,1)} custom-call(bf16[128,72,128]{2,1,0:T(8,128)(2,1)S(1)} %all_to_all.21.bundle), custom_call_target="tpu_custom_call" | custom-call | tf_op jit(solution)/shard_map/sum_parts/pallas_call | solution.py:485
  93.8 4.8 %all-to-all-start.3 = ((bf16[64,56,128]{2,1,0:T(8,128)(2,1)}), bf16[64,56,128]{2,1,0:T(8,128)(2,1)S(1)}, u32[]{:S(2)}, u32[]{:S(2)}) async-start(bf16[64,56,128]{2,1,0:T(8,128)(2,1)} %sum_parts.1), calls=%async_computation.3 | async-start | bytes 1835008 | tf_op jit(solution)/shard_map/all_to_all | solution.py:659
  98.7 1.0 slice.20
  99.7 1.4 %copy.24 = bf16[128,12,128]{0,2,1:T(8,128)(2,1)S(1)} copy(bf16[128,12,128]{2,1,0:T(8,128)(2,1)} %slice.20) | data formatting | bytes 786432 | tf_op jit(solution)/shard_map/slice | solution.py:690
  101.3 0.9 fusion.refs_2_
  102.2 10.8 %adam.1 = (f32[2048,128]{1,0:T(8,128)}, f32[2048,128]{1,0:T(8,128)}, f32[2048,128]{1,0:T(8,128)}, f32[8,128]{1,0:T(8,128)}) custom-call(s32[32,128]{1,0:T(8,128)} %get-tuple-element.33.wanted, bf16[128,72,128]{2,1,0:T(8,128)(2,1)} %copy-done, f32[2048,128]{1,0:T(8,128)} %table.1, f32[2048,128]{1,0:T(8,128)} %m1.1, f32[2048,128]{1,0:T(8,128)} %m2.1), custom_call_target="tpu_custom_call" | custom-call | flops 4294967296 | bytes 7340032 | tf_op jit(solution)/shard_map/adam/pallas_call | solution.py:612
  113.0 1.9 %all-to-all-done.3.refs_0_ = bf16[64,56,128]{2,1,0:T(8,128)(2,1)S(1)} async-done(((bf16[64,56,128]{2,1,0:T(8,128)(2,1)}), bf16[64,56,128]{2,1,0:T(8,128)(2,1)S(1)}, u32[]{:S(2)}, u32[]{:S(2)}) %all-to-all-start.3) | async-done | bytes 917536 | tf_op jit(solution)/shard_map/all_to_all | solution.py:659
  114.9 1.9 %collective-permute-start.3 = (bf16[64,56,128]{2,1,0:T(8,128)(2,1)S(1)}, bf16[64,56,128]{2,1,0:T(8,128)(2,1)S(1)}, u32[]{:S(2)}, u32[]{:S(2)}) collective-permute-start(bf16[64,56,128]{2,1,0:T(8,128)(2,1)S(1)} %after.1), channel_id=1, source_target_pairs={{0,4},{4,0},{1,5},{5,1},{2,6},{6,2},{3,7},{7,3},{8,12},{12,8},{9,1... | collective-permute-start | bytes 2752520 | tf_op jit(solution)/shard_map/ppermute | solution.py:662
  116.8 1.3 %weight_out.2 = (f32[768,1024]{1,0:T(8,128)}, f32[128,1024]{1,0:T(8,128)}) custom-call(s32[1]{0:T(128)} %bitcast.9.core.side, bf16[4,4,4,56,128]{4,3,2,1,0:T(8,128)(2,1)S(1)} %bitcast.22), custom_call_target="tpu_custom_call" | custom-call | flops 786432 | bytes 2359296 | tf_op jit(solution)/shard_map/weight_out/pallas_call | solution.py:536
  118.1 0.8 collective-permute-done.3
  118.9 1.3 %weight_out.3 = (f32[768,1024]{1,0:T(8,128)}, f32[128,1024]{1,0:T(8,128)}) custom-call(s32[1]{0:T(128)S(6)} %sub.3.side, bf16[4,4,4,56,128]{4,3,2,1,0:T(8,128)(2,1)S(1)} %bitcast.24, f32[768,1024]{1,0:T(8,128)} %get-tuple-element.52.rest_0_, f32[128,1024]{1,0:T(8,128)} %get-tuple-element.53.rest_1_), custom_call_target="tpu_custom_call", output_to_operand_aliasing={{0}: (2, {}), {1}: (3, {})} | custom-call | flops 786432 | bytes 2359296 | tf_op jit(solution)/shard_map/weight_out/pallas_call | solution.py:536
  (11 shorter events, 0.8 us)
Async XLA Ops:
  0.6 31.7 %copy-start.1 = (bf16[128,768]{1,0:T(8,128)(2,1)S(1)}, bf16[128,768]{1,0:T(8,128)(2,1)}, u32[]{:S(2)}) copy-start(bf16[128,768]{1,0:T(8,128)(2,1)} %feats.3) | copy-start | bytes 589828
  28.0 23.7 %all-to-all-start.1 = ((bf16[128,32,128]{2,1,0:T(8,128)(2,1)}), bf16[128,32,128]{2,1,0:T(8,128)(2,1)S(1)}, u32[]{:S(2)}, u32[]{:S(2)}) async-start(bf16[128,32,128]{2,1,0:T(8,128)(2,1)} %bitcast.30), calls=%async_computation.1 | async-start | bytes 2097152 | tf_op jit(solution)/shard_map/all_to_all | solution.py:659
  32.3 6.1 %collective-permute-start = (bf16[128,768]{1,0:T(8,128)(2,1)S(1)}, bf16[128,768]{1,0:T(8,128)(2,1)S(1)}, u32[]{:S(2)}, u32[]{:S(2)}) collective-permute-start(bf16[128,768]{1,0:T(8,128)(2,1)S(1)} %copy-done.1), channel_id=1, source_target_pairs={{0,4},{4,0},{1,5},{5,1},{2,6},{6,2},{3,7},{7,3},{8,12},{12,8},{9,1... | collective-permute-start | bytes 589832 | tf_op jit(solution)/shard_map/ppermute | solution.py:662
  52.7 1.8 %collective-permute-start.2 = (bf16[128,512]{1,0:T(8,128)(2,1)S(1)}, bf16[128,512]{1,0:T(8,128)(2,1)S(1)}, u32[]{:S(2)}, u32[]{:S(2)}) collective-permute-start(bf16[128,512]{1,0:T(8,128)(2,1)S(1)} %get-tuple-element.44), channel_id=1, source_target_pairs={{0,4},{4,0},{1,5},{5,1},{2,6},{6,2},{3,7},{7,3},{8,12},{12,8},{9,1... | collective-permute-start | bytes 393224 | tf_op jit(solution)/shard_map/ppermute | solution.py:662
  53.1 1.3 %collective-permute-start.1 = (bf16[128,128]{1,0:T(8,128)(2,1)S(1)}, bf16[128,128]{1,0:T(8,128)(2,1)S(1)}, u32[]{:S(2)}, u32[]{:S(2)}) collective-permute-start(bf16[128,128]{1,0:T(8,128)(2,1)S(1)} %get-tuple-element.42.agg0), channel_id=1, source_target_pairs={{0,4},{4,0},{1,5},{5,1},{2,6},{6,2},{3,7},{7,3},{8,12},{12,8},{9,1... | collective-permute-start | bytes 98312 | tf_op jit(solution)/shard_map/ppermute | solution.py:662
  92.5 6.2 %copy-start = (bf16[128,72,128]{2,1,0:T(8,128)(2,1)}, bf16[128,72,128]{2,1,0:T(8,128)(2,1)S(1)}, u32[]{:S(2)}) copy-start(bf16[128,72,128]{2,1,0:T(8,128)(2,1)S(1)} %all_to_all.21.bundle) | copy-start | bytes 7077892
  93.8 21.0 %all-to-all-start.3 = ((bf16[64,56,128]{2,1,0:T(8,128)(2,1)}), bf16[64,56,128]{2,1,0:T(8,128)(2,1)S(1)}, u32[]{:S(2)}, u32[]{:S(2)}) async-start(bf16[64,56,128]{2,1,0:T(8,128)(2,1)} %sum_parts.1), calls=%async_computation.3 | async-start | bytes 1835008 | tf_op jit(solution)/shard_map/all_to_all | solution.py:659
  114.9 4.0 %collective-permute-start.3 = (bf16[64,56,128]{2,1,0:T(8,128)(2,1)S(1)}, bf16[64,56,128]{2,1,0:T(8,128)(2,1)S(1)}, u32[]{:S(2)}, u32[]{:S(2)}) collective-permute-start(bf16[64,56,128]{2,1,0:T(8,128)(2,1)S(1)} %after.1), channel_id=1, source_target_pairs={{0,4},{4,0},{1,5},{5,1},{2,6},{6,2},{3,7},{7,3},{8,12},{12,8},{9,1... | collective-permute-start | bytes 2752520 | tf_op jit(solution)/shard_map/ppermute | solution.py:662

commit v6 on v5

--- a/solution.py
+++ b/solution.py
@@ -111,7 +111,7 @@
     k_edge = (iota((blocks, LANES), 1) % slots_per).astype(F32)
     live_owner = jnp.where(k_edge < cnt_edge, owner[...], -1)
     base = jnp.zeros((devs, LANES), F32)
-    acc = jnp.zeros((devs, 3 * CAP), F32)
+    hots, values = [], []
     ksub = iota((CAP, LANES), 0).astype(F32)
     for b in range(blocks):
         hot = sub == live_owner[b : b + 1, :]
@@ -131,8 +131,10 @@
             ],
             axis=0,
         ).astype(BF16)
-        acc = acc + dot(hot_b, vals, ((1,), (1,)))
-    acc_i = acc.astype(I32)
+        hots.append(hot_b)
+        values.append(vals)
+    values = jnp.concatenate(values, axis=1)
+    acc_i = dot(jnp.concatenate(hots, axis=1), values, ((1,), (1,))).astype(I32)
     seeds = acc_i[:, 2 * CAP :]
     wanted = jnp.where(seeds > 0, acc_i[:, :CAP] * LANES + acc_i[:, CAP : 2 * CAP], EMPTY)
 
@@ -349,7 +351,7 @@
     w_rel,
     *rest,
 ):
-    agg_out, here_out, there_out, grad_out = rest[-4:]
+    here_out, there_out, grad_out = rest[-3:]
     devs = LANES
     lines = seed_of.shape[0]
     seed1 = iota((devs, LANES), 0) + 1
@@ -362,14 +364,15 @@
         agg = agg + dot(match, fetched[b * LANES : (b + 2) * LANES, :])
     count = cnt[...]
     agg_b = (agg / count).astype(BF16)
-    agg_out[...] = agg_b
     pre = pre_self[...] + dot(agg_b, w_rel[...])
     sig = jax.nn.sigmoid(pre)
     dpre = (cot[...] * sig * (1.0 + pre * (1.0 - sig))).astype(BF16)
     half = dpre.shape[1] // 2
     first = core[0] == 0
-    here_out[...] = jnp.where(first, dpre[:, :half], dpre[:, half:])
-    there_out[...] = jnp.where(first, dpre[:, half:], dpre[:, :half])
+    here_out[:, :half] = jnp.where(first, dpre[:, :half], dpre[:, half:])
+    there_out[:, :half] = jnp.where(first, dpre[:, half:], dpre[:, :half])
+    here_out[:, half:] = agg_b
+    there_out[:, half:] = agg_b
     dagg = dot(dpre, w_rel[...], ((1,), (1,)))
     grad_out[...] = (dagg / count).astype(BF16)
 
@@ -379,13 +382,12 @@
     return pl.pallas_call(
         layer_kernel,
         out_shape=(
+            jax.ShapeDtypeStruct((seeds, hidden // 2 + LANES), BF16),
+            jax.ShapeDtypeStruct((seeds, hidden // 2 + LANES), BF16),
             jax.ShapeDtypeStruct((seeds, LANES), BF16),
-            jax.ShapeDtypeStruct((seeds, hidden // 2), BF16),
-            jax.ShapeDtypeStruct((seeds, hidden // 2), BF16),
-            jax.ShapeDtypeStruct((seeds, LANES), BF16),
         ),
         in_specs=[SMEM] + [VMEM] * 6 + [ANY] * len(ready),
-        out_specs=(VMEM, VMEM, VMEM, VMEM),
+        out_specs=(VMEM, VMEM, VMEM),
         compiler_params=params(),
         name="layer",
     )(core, fetched, seed_of, cnt, pre_self, cotangent, w_rel, *in_hbm(*ready))
@@ -423,10 +425,10 @@
     )(seed_of, grad, *in_hbm(papers, feats_t))
 
 
-def weight_kernel(feats_t, agg0, agg1, dpre0, dpre1, slots, papers, bundle):
-    right = jnp.concatenate([dpre0[...], dpre1[...]], axis=0)
-    aggs = jnp.concatenate([agg0[...], agg1[...]], axis=0)
-    emb = aggs.shape[1]
+def weight_kernel(feats_t, here, far, slots, papers, bundle):
+    both = jnp.concatenate([here[...], far[...]], axis=0)
+    emb = LANES
+    right, aggs = both[:, :-emb], both[:, -emb:]
     columns = right.shape[1] // LANES
     blocks = LANES // columns
     span = 2 * REL_ROWS
@@ -450,15 +452,15 @@
             bundle[d, REL_AT + span :, :] = paper[span:].astype(BF16)
 
 
-def weight_part(feats_t, agg0, agg1, dpre0, dpre1, slots, papers):
+def weight_part(feats_t, here, far, slots, papers):
     return pl.pallas_call(
         weight_kernel,
         out_shape=jax.ShapeDtypeStruct((LANES, BUNDLE, LANES), BF16),
-        in_specs=[VMEM] * 7,
+        in_specs=[VMEM] * 5,
         out_specs=VMEM,
         compiler_params=params(),
         name="weight_part",
-    )(feats_t, agg0, agg1, dpre0, dpre1, slots, papers)
+    )(feats_t, here, far, slots, papers)
 
 
 def sum_kernel(bundle, out, out_scr, sems):
@@ -677,13 +679,13 @@
     pre_self, cot, w_rel = prep(feats, w_self, cotangent, w_rel)
     feats_t = turn(feats, swap(feats))
     papers = paper_rows(got, paper_table)
-    agg_b, dpre_here, dpre_there, grad = layer(
+    here, there, grad = layer(
         core, fetched, seed_of, cnt, pre_self, cot, w_rel, feats_t, papers
     )
 
-    agg_far, dpre_far = swap(agg_b), swap(dpre_there)
+    far = swap(there)
     slots, papers, feats_t = slot_grads(seed_of, grad, papers, feats_t)
-    bundle = weight_part(feats_t, agg_b, agg_far, dpre_here, dpre_far, slots, papers)
+    bundle = weight_part(feats_t, here, far, slots, papers)
     bundle = exchange(bundle, every)
     full = exchange(sum_parts(bundle, lax.axis_size(peers)), peers)
     new_table, new_moment1, new_moment2, done = adam(wanted, bundle, table, moment1, moment2)

time: 121 us -> 120 us (level)
    ppermute x4 -> x3, starting transfers between devices: 3.67 us -> 3.56 us  [swap(): return lax.ppermute(a, 'core', [(0, 1), (1, 0)])]
  transfers between devices with their start and end apart: 6 -> 5, of which waited for: 3 -> 3; matrix products, arithmetic and copies ran while one was open for 3% -> 3% of each run, Pallas kernels for 16% -> 16%
where the time goes in v6:
time: 120 us
  blocking collectives  57.9 us (48%)
  Pallas kernels  29.5 us (25%)
  waiting for transfers between devices  15 us (12%)
  starting transfers between devices  12.7 us (11%)
  local copies, waits for them, and re-layouts  2.39 us (2%)
    all_to_all x2, blocking collectives, exchange(): return lax.all_to_all(a, axes, split_axis=0, concat_axis=0, tiled=True)  57.9 us
    all_to_all x2, waiting for transfers between devices, exchange(): return lax.all_to_all(a, axes, split_axis=0, concat_axis=0, tiled=True)  14.2 us
    pallas_call x1, Pallas kernels, adam(): pl.pallas_call(adam_kernel, grid=(table.shape[0] // rows,), out_shape=(ja...  10.8 us
    all_to_all x2, starting transfers between devices, exchange(): return lax.all_to_all(a, axes, split_axis=0, concat_axis=0, tiled=True)  9.15 us
    pallas_call x1, Pallas kernels, gather(): pl.pallas_call(gather_kernel, out_shape=(pltpu.HBM((slots, LANES), BF16),...  3.88 us
    ppermute x3, starting transfers between devices, swap(): return lax.ppermute(a, 'core', [(0, 1), (1, 0)])  3.56 us
    pallas_call x1, Pallas kernels, paper_rows(): pl.pallas_call(paper_kernel, out_shape=pltpu.HBM((LANES, span, LANES), BF...  3.15 us
    pallas_call x2, Pallas kernels, spread(): pl.pallas_call(spread_kernel, out_shape=(pltpu.HBM((feats, hidden), F32),...  2.65 us
  transfers between devices with their start and end apart: 5, of which 3 were waited for; matrix products, arithmetic and copies ran while one was open for 3% of the time, Pallas kernels for 16%

profile of v6, /device:TPU:1, one launch (start us, length us, event | category | flops | bytes accessed | tf_op | source)
XLA Modules:
  0.0 119.7 jit_solution(8533178941159746025)
XLA Ops:
  0.6 2.1 %place.1 = (s32[128,128]{1,0:T(8,128)S(1)}, s32[32,128]{1,0:T(8,128)S(1)}, f32[128,128]{1,0:T(8,128)S(1)}, bf16[2,128,128]{2,1,0:T(8,128)(2,1)S(1)}, bf16[256,1024]{1,0:T(8,128)(2,1)S(1)}) custom-call(s32[1]{0:T(128)} %bitcast.lane_group, s32[16,128]{1,0:T(8,128)} %bitcast.31, s32[16,128]{1,0:T(8,128)} %bitcast.32, s32[1,128]{1,0:T(1,128)} %bitcast.33, ...), custom_call_target="tpu_custom_call" | custom-call | tf_op jit(solution)/shard_map/place/pallas_call | solution.py:182
  2.8 20.9 %all_to_all.20 = s32[128,1,128]{2,1,0:T(1,128)S(1)} all-to-all(s32[128,1,128]{2,1,0:T(1,128)S(1)} %bitcast.27), channel_id=1, replica_groups=mesh['chip'=16,'core'=2,'mp'=4] {'chip','core','mp'}, dimensions={0} | all-to-all | bytes 131072 | tf_op jit(solution)/shard_map/all_to_all | solution.py:661
  23.7 3.9 %gather_rows.1 = (bf16[4096,128]{1,0:T(8,128)(2,1)}, s32[32,128]{1,0:T(8,128)}) custom-call(s32[128,128]{1,0:T(8,128)S(1)} %bitcast.25, bf16[256,1024]{1,0:T(8,128)(2,1)S(1)} %get-tuple-element.31.wide), custom_call_target="tpu_custom_call" | custom-call | tf_op jit(solution)/shard_map/gather_rows/pallas_call | solution.py:235
  27.6 4.3 %all-to-all-start.1 = ((bf16[128,32,128]{2,1,0:T(8,128)(2,1)}), bf16[128,32,128]{2,1,0:T(8,128)(2,1)S(1)}, u32[]{:S(2)}, u32[]{:S(2)}) async-start(bf16[128,32,128]{2,1,0:T(8,128)(2,1)} %bitcast.30), calls=%async_computation.1 | async-start | bytes 2097152 | tf_op jit(solution)/shard_map/all_to_all | solution.py:661
  32.0 1.1 collective-permute-start
  33.1 1.8 %prep.1 = (f32[128,1024]{1,0:T(8,128)S(1)}, f32[128,1024]{1,0:T(8,128)S(1)}, bf16[128,1024]{1,0:T(8,128)(2,1)S(1)}) custom-call(bf16[128,768]{1,0:T(8,128)(2,1)S(1)} %copy-done.1, bf16[768,1024]{1,0:T(8,128)(2,1)} %w_self_in.1, f32[128,1024]{1,0:T(8,128)} %cot_in.1, bf16[128,1024]{1,0:T(8,128)(2,1)} %w_in.1), custom_call_target="tpu_custom_call" | custom-call | flops 201326592 | bytes 4194304 | tf_op jit(solution)/shard_map/prep/pallas_call | solution.py:307
  34.9 3.2 %gather_papers.1.rest_1_.papers_in = bf16[128,16,128]{2,1,0:T(8,128)(2,1)} custom-call(s32[128,128]{1,0:T(8,128)S(1)} %bitcast.26, bf16[1024,768]{1,0:T(8,128)(2,1)} %paper_in.1), custom_call_target="tpu_custom_call" | custom-call | flops 402653184 | bytes 3145728 | tf_op jit(solution)/shard_map/gather_papers/pallas_call | solution.py:278
  38.1 0.9 turn.1.rest_0_.feats_in
  39.0 12.4 %all-to-all-done.1 = bf16[128,32,128]{2,1,0:T(8,128)(2,1)S(1)} async-done(((bf16[128,32,128]{2,1,0:T(8,128)(2,1)}), bf16[128,32,128]{2,1,0:T(8,128)(2,1)S(1)}, u32[]{:S(2)}, u32[]{:S(2)}) %all-to-all-start.1) | async-done | bytes 1048608 | tf_op jit(solution)/shard_map/all_to_all | solution.py:661
  51.4 0.9 layer.1
  52.8 1.2 slot_grads.1
  53.9 0.8 weight_part.1
  54.8 37.0 %all_to_all.21.bundle = bf16[128,72,128]{2,1,0:T(8,128)(2,1)S(1)} all-to-all(bf16[128,72,128]{2,1,0:T(8,128)(2,1)S(1)} %weight_part.1), channel_id=1, replica_groups=mesh['chip'=16,'core'=2,'mp'=4] {'chip','core','mp'}, dimensions={0} | all-to-all | bytes 4718592 | tf_op jit(solution)/shard_map/all_to_all | solution.py:661
  91.8 1.3 %sum_parts.1 = bf16[64,56,128]{2,1,0:T(8,128)(2,1)} custom-call(bf16[128,72,128]{2,1,0:T(8,128)(2,1)S(1)} %all_to_all.21.bundle), custom_call_target="tpu_custom_call" | custom-call | tf_op jit(solution)/shard_map/sum_parts/pallas_call | solution.py:487
  93.1 4.8 %all-to-all-start.3 = ((bf16[64,56,128]{2,1,0:T(8,128)(2,1)}), bf16[64,56,128]{2,1,0:T(8,128)(2,1)S(1)}, u32[]{:S(2)}, u32[]{:S(2)}) async-start(bf16[64,56,128]{2,1,0:T(8,128)(2,1)} %sum_parts.1), calls=%async_computation.3 | async-start | bytes 1835008 | tf_op jit(solution)/shard_map/all_to_all | solution.py:661
  98.0 1.0 slice.20
  99.0 1.4 %copy.24 = bf16[128,12,128]{0,2,1:T(8,128)(2,1)S(1)} copy(bf16[128,12,128]{2,1,0:T(8,128)(2,1)} %slice.20) | data formatting | bytes 786432 | tf_op jit(solution)/shard_map/slice | solution.py:692
  100.6 0.9 fusion.refs_2_
  101.5 10.8 %adam.1 = (f32[2048,128]{1,0:T(8,128)}, f32[2048,128]{1,0:T(8,128)}, f32[2048,128]{1,0:T(8,128)}, f32[8,128]{1,0:T(8,128)}) custom-call(s32[32,128]{1,0:T(8,128)} %get-tuple-element.32.wanted, bf16[128,72,128]{2,1,0:T(8,128)(2,1)} %copy-done, f32[2048,128]{1,0:T(8,128)} %table.1, f32[2048,128]{1,0:T(8,128)} %m1.1, f32[2048,128]{1,0:T(8,128)} %m2.1), custom_call_target="tpu_custom_call" | custom-call | flops 4294967296 | bytes 7340032 | tf_op jit(solution)/shard_map/adam/pallas_call | solution.py:614
  112.3 1.9 %all-to-all-done.3.refs_0_ = bf16[64,56,128]{2,1,0:T(8,128)(2,1)S(1)} async-done(((bf16[64,56,128]{2,1,0:T(8,128)(2,1)}), bf16[64,56,128]{2,1,0:T(8,128)(2,1)S(1)}, u32[]{:S(2)}, u32[]{:S(2)}) %all-to-all-start.3) | async-done | bytes 917536 | tf_op jit(solution)/shard_map/all_to_all | solution.py:661
  114.2 1.9 %collective-permute-start.2 = (bf16[64,56,128]{2,1,0:T(8,128)(2,1)S(1)}, bf16[64,56,128]{2,1,0:T(8,128)(2,1)S(1)}, u32[]{:S(2)}, u32[]{:S(2)}) collective-permute-start(bf16[64,56,128]{2,1,0:T(8,128)(2,1)S(1)} %after.1), channel_id=1, source_target_pairs={{0,4},{4,0},{1,5},{5,1},{2,6},{6,2},{3,7},{7,3},{8,12},{12,8},{9,1... | collective-permute-start | bytes 2752520 | tf_op jit(solution)/shard_map/ppermute | solution.py:664
  116.1 1.3 %weight_out.2 = (f32[768,1024]{1,0:T(8,128)}, f32[128,1024]{1,0:T(8,128)}) custom-call(s32[1]{0:T(128)} %bitcast.9.core.side, bf16[4,4,4,56,128]{4,3,2,1,0:T(8,128)(2,1)S(1)} %bitcast.22), custom_call_target="tpu_custom_call" | custom-call | flops 786432 | bytes 2359296 | tf_op jit(solution)/shard_map/weight_out/pallas_call | solution.py:538
  117.4 0.8 collective-permute-done.2
  118.2 1.3 %weight_out.3 = (f32[768,1024]{1,0:T(8,128)}, f32[128,1024]{1,0:T(8,128)}) custom-call(s32[1]{0:T(128)S(6)} %sub.3.side, bf16[4,4,4,56,128]{4,3,2,1,0:T(8,128)(2,1)S(1)} %bitcast.24, f32[768,1024]{1,0:T(8,128)} %get-tuple-element.50.rest_0_, f32[128,1024]{1,0:T(8,128)} %get-tuple-element.51.rest_1_), custom_call_target="tpu_custom_call", output_to_operand_aliasing={{0}: (2, {}), {1}: (3, {})} | custom-call | flops 786432 | bytes 2359296 | tf_op jit(solution)/shard_map/weight_out/pallas_call | solution.py:538
  (9 shorter events, 0.7 us)
Async XLA Ops:
  0.6 31.3 %copy-start.1 = (bf16[128,768]{1,0:T(8,128)(2,1)S(1)}, bf16[128,768]{1,0:T(8,128)(2,1)}, u32[]{:S(2)}) copy-start(bf16[128,768]{1,0:T(8,128)(2,1)} %feats.3) | copy-start | bytes 589828
  27.6 23.7 %all-to-all-start.1 = ((bf16[128,32,128]{2,1,0:T(8,128)(2,1)}), bf16[128,32,128]{2,1,0:T(8,128)(2,1)S(1)}, u32[]{:S(2)}, u32[]{:S(2)}) async-start(bf16[128,32,128]{2,1,0:T(8,128)(2,1)} %bitcast.30), calls=%async_computation.1 | async-start | bytes 2097152 | tf_op jit(solution)/shard_map/all_to_all | solution.py:661
  32.0 6.1 %collective-permute-start = (bf16[128,768]{1,0:T(8,128)(2,1)S(1)}, bf16[128,768]{1,0:T(8,128)(2,1)S(1)}, u32[]{:S(2)}, u32[]{:S(2)}) collective-permute-start(bf16[128,768]{1,0:T(8,128)(2,1)S(1)} %copy-done.1), channel_id=1, source_target_pairs={{0,4},{4,0},{1,5},{5,1},{2,6},{6,2},{3,7},{7,3},{8,12},{12,8},{9,1... | collective-permute-start | bytes 589832 | tf_op jit(solution)/shard_map/ppermute | solution.py:664
  52.3 1.7 %collective-permute-start.1 = (bf16[128,640]{1,0:T(8,128)(2,1)S(1)}, bf16[128,640]{1,0:T(8,128)(2,1)S(1)}, u32[]{:S(2)}, u32[]{:S(2)}) collective-permute-start(bf16[128,640]{1,0:T(8,128)(2,1)S(1)} %get-tuple-element.42), channel_id=1, source_target_pairs={{0,4},{4,0},{1,5},{5,1},{2,6},{6,2},{3,7},{7,3},{8,12},{12,8},{9,1... | collective-permute-start | bytes 491528 | tf_op jit(solution)/shard_map/ppermute | solution.py:664
  91.8 6.2 %copy-start = (bf16[128,72,128]{2,1,0:T(8,128)(2,1)}, bf16[128,72,128]{2,1,0:T(8,128)(2,1)S(1)}, u32[]{:S(2)}) copy-start(bf16[128,72,128]{2,1,0:T(8,128)(2,1)S(1)} %all_to_all.21.bundle) | copy-start | bytes 7077892
  93.1 21.0 %all-to-all-start.3 = ((bf16[64,56,128]{2,1,0:T(8,128)(2,1)}), bf16[64,56,128]{2,1,0:T(8,128)(2,1)S(1)}, u32[]{:S(2)}, u32[]{:S(2)}) async-start(bf16[64,56,128]{2,1,0:T(8,128)(2,1)} %sum_parts.1), calls=%async_computation.3 | async-start | bytes 1835008 | tf_op jit(solution)/shard_map/all_to_all | solution.py:661
  114.2 4.0 %collective-permute-start.2 = (bf16[64,56,128]{2,1,0:T(8,128)(2,1)S(1)}, bf16[64,56,128]{2,1,0:T(8,128)(2,1)S(1)}, u32[]{:S(2)}, u32[]{:S(2)}) collective-permute-start(bf16[64,56,128]{2,1,0:T(8,128)(2,1)S(1)} %after.1), channel_id=1, source_target_pairs={{0,4},{4,0},{1,5},{5,1},{2,6},{6,2},{3,7},{7,3},{8,12},{12,8},{9,1... | collective-permute-start | bytes 2752520 | tf_op jit(solution)/shard_map/ppermute | solution.py:664

commit v7 on v6

--- a/solution.py
+++ b/solution.py
@@ -205,8 +205,9 @@
     for i in range(GROUP):
         wanted = wanted + jnp.where(quarter == i, got[pl.ds(i, lines, stride=GROUP), :], 0)
     wanted_out[...] = wanted
-    lo = (wanted % TILE).T
-    hi = (wanted // TILE).T
+    wanted_t = wanted.T
+    lo = wanted_t % TILE
+    hi = wanted_t // TILE
     lanes = iota((LANES, TILE), 1)
     for b in range(lines):
         hot_scr[b * LANES : (b + 1) * LANES, :] = onehot(lo[:, b : b + 1] == lanes)
@@ -439,9 +440,12 @@
     )
     aggs_t = dot(spread_rows, aggs, ((1,), (1,))).astype(BF16)
     for cb in range(columns):
-        cols = right[:, cb * LANES : (cb + 1) * LANES]
-        part_f = dot(feats_t[...], cols).astype(BF16)
-        part_a = dot(aggs_t, cols)
+        mine = slice(cb % 2 * LANES, (cb % 2 + 1) * LANES)
+        if cb % 2 == 0:
+            cols = right[:, cb * LANES : (cb + 2) * LANES]
+            both_f = dot(feats_t[...], cols).astype(BF16)
+            both_a = dot(aggs_t, cols)
+        part_f, part_a = both_f[:, mine], both_a[:, mine]
         for i in range(blocks):
             d = cb * blocks + i
             bundle[d, :CAP, :] = slots[d]

time: 120 us -> 120 us (level)
  no operation moved by 1% of the time
where the time goes in v7:
time: 120 us; the launch traced here: 119 us
  blocking collectives  57.9 us (48%)
  Pallas kernels  29.3 us (24%)
  waiting for transfers between devices  15 us (12%)
  starting transfers between devices  12.7 us (11%)
  local copies, waits for them, and re-layouts  2.39 us (2%)
    all_to_all x2, blocking collectives, exchange(): return lax.all_to_all(a, axes, split_axis=0, concat_axis=0, tiled=True)  57.9 us
    all_to_all x2, waiting for transfers between devices, exchange(): return lax.all_to_all(a, axes, split_axis=0, concat_axis=0, tiled=True)  14.2 us
    pallas_call x1, Pallas kernels, adam(): pl.pallas_call(adam_kernel, grid=(table.shape[0] // rows,), out_shape=(ja...  10.8 us
    all_to_all x2, starting transfers between devices, exchange(): return lax.all_to_all(a, axes, split_axis=0, concat_axis=0, tiled=True)  9.16 us
    pallas_call x1, Pallas kernels, gather(): pl.pallas_call(gather_kernel, out_shape=(pltpu.HBM((slots, LANES), BF16),...  3.83 us
    ppermute x3, starting transfers between devices, swap(): return lax.ppermute(a, 'core', [(0, 1), (1, 0)])  3.56 us
    pallas_call x1, Pallas kernels, paper_rows(): pl.pallas_call(paper_kernel, out_shape=pltpu.HBM((LANES, span, LANES), BF...  3.15 us
    pallas_call x2, Pallas kernels, spread(): pl.pallas_call(spread_kernel, out_shape=(pltpu.HBM((feats, hidden), F32),...  2.65 us
  transfers between devices with their start and end apart: 5, of which 3 were waited for; matrix products, arithmetic and copies ran while one was open for 3% of the time, Pallas kernels for 16%

profile of v7, /device:TPU:1, one launch (start us, length us, event | category | flops | bytes accessed | tf_op | source)
XLA Modules:
  0.0 119.4 jit_solution(12385866725016418357)
XLA Ops:
  0.6 2.1 %place.1 = (s32[128,128]{1,0:T(8,128)S(1)}, s32[32,128]{1,0:T(8,128)S(1)}, f32[128,128]{1,0:T(8,128)S(1)}, bf16[2,128,128]{2,1,0:T(8,128)(2,1)S(1)}, bf16[256,1024]{1,0:T(8,128)(2,1)S(1)}) custom-call(s32[1]{0:T(128)} %bitcast.lane_group, s32[16,128]{1,0:T(8,128)} %bitcast.31, s32[16,128]{1,0:T(8,128)} %bitcast.32, s32[1,128]{1,0:T(1,128)} %bitcast.33, ...), custom_call_target="tpu_custom_call" | custom-call | tf_op jit(solution)/shard_map/place/pallas_call | solution.py:182
  2.8 20.9 %all_to_all.20 = s32[128,1,128]{2,1,0:T(1,128)S(1)} all-to-all(s32[128,1,128]{2,1,0:T(1,128)S(1)} %bitcast.27), channel_id=1, replica_groups=mesh['chip'=16,'core'=2,'mp'=4] {'chip','core','mp'}, dimensions={0} | all-to-all | bytes 131072 | tf_op jit(solution)/shard_map/all_to_all | solution.py:665
  23.7 3.8 %gather_rows.1 = (bf16[4096,128]{1,0:T(8,128)(2,1)}, s32[32,128]{1,0:T(8,128)}) custom-call(s32[128,128]{1,0:T(8,128)S(1)} %bitcast.25, bf16[256,1024]{1,0:T(8,128)(2,1)S(1)} %get-tuple-element.31.wide), custom_call_target="tpu_custom_call" | custom-call | tf_op jit(solution)/shard_map/gather_rows/pallas_call | solution.py:236
  27.6 4.3 %all-to-all-start.1 = ((bf16[128,32,128]{2,1,0:T(8,128)(2,1)}), bf16[128,32,128]{2,1,0:T(8,128)(2,1)S(1)}, u32[]{:S(2)}, u32[]{:S(2)}) async-start(bf16[128,32,128]{2,1,0:T(8,128)(2,1)} %bitcast.30), calls=%async_computation.1 | async-start | bytes 2097152 | tf_op jit(solution)/shard_map/all_to_all | solution.py:665
  31.9 1.1 collective-permute-start
  33.1 1.8 %prep.1 = (f32[128,1024]{1,0:T(8,128)S(1)}, f32[128,1024]{1,0:T(8,128)S(1)}, bf16[128,1024]{1,0:T(8,128)(2,1)S(1)}) custom-call(bf16[128,768]{1,0:T(8,128)(2,1)S(1)} %copy-done.1, bf16[768,1024]{1,0:T(8,128)(2,1)} %w_self_in.1, f32[128,1024]{1,0:T(8,128)} %cot_in.1, bf16[128,1024]{1,0:T(8,128)(2,1)} %w_in.1), custom_call_target="tpu_custom_call" | custom-call | flops 201326592 | bytes 4194304 | tf_op jit(solution)/shard_map/prep/pallas_call | solution.py:308
  34.9 3.2 %gather_papers.1.rest_1_.papers_in = bf16[128,16,128]{2,1,0:T(8,128)(2,1)} custom-call(s32[128,128]{1,0:T(8,128)S(1)} %bitcast.26, bf16[1024,768]{1,0:T(8,128)(2,1)} %paper_in.1), custom_call_target="tpu_custom_call" | custom-call | flops 402653184 | bytes 3145728 | tf_op jit(solution)/shard_map/gather_papers/pallas_call | solution.py:279
  38.1 0.9 turn.1.rest_0_.feats_in
  39.0 12.4 %all-to-all-done.1 = bf16[128,32,128]{2,1,0:T(8,128)(2,1)S(1)} async-done(((bf16[128,32,128]{2,1,0:T(8,128)(2,1)}), bf16[128,32,128]{2,1,0:T(8,128)(2,1)S(1)}, u32[]{:S(2)}, u32[]{:S(2)}) %all-to-all-start.1) | async-done | bytes 1048608 | tf_op jit(solution)/shard_map/all_to_all | solution.py:665
  51.3 0.9 layer.1
  52.7 1.2 slot_grads.1
  53.9 0.6 weight_part.1
  54.5 37.0 %all_to_all.21.bundle = bf16[128,72,128]{2,1,0:T(8,128)(2,1)S(1)} all-to-all(bf16[128,72,128]{2,1,0:T(8,128)(2,1)S(1)} %weight_part.1), channel_id=1, replica_groups=mesh['chip'=16,'core'=2,'mp'=4] {'chip','core','mp'}, dimensions={0} | all-to-all | bytes 4718592 | tf_op jit(solution)/shard_map/all_to_all | solution.py:665
  91.5 1.3 %sum_parts.1 = bf16[64,56,128]{2,1,0:T(8,128)(2,1)} custom-call(bf16[128,72,128]{2,1,0:T(8,128)(2,1)S(1)} %all_to_all.21.bundle), custom_call_target="tpu_custom_call" | custom-call | tf_op jit(solution)/shard_map/sum_parts/pallas_call | solution.py:491
  92.8 4.8 %all-to-all-start.3 = ((bf16[64,56,128]{2,1,0:T(8,128)(2,1)}), bf16[64,56,128]{2,1,0:T(8,128)(2,1)S(1)}, u32[]{:S(2)}, u32[]{:S(2)}) async-start(bf16[64,56,128]{2,1,0:T(8,128)(2,1)} %sum_parts.1), calls=%async_computation.3 | async-start | bytes 1835008 | tf_op jit(solution)/shard_map/all_to_all | solution.py:665
  97.7 1.0 slice.20
  98.7 1.4 %copy.24 = bf16[128,12,128]{0,2,1:T(8,128)(2,1)S(1)} copy(bf16[128,12,128]{2,1,0:T(8,128)(2,1)} %slice.20) | data formatting | bytes 786432 | tf_op jit(solution)/shard_map/slice | solution.py:696
  100.3 0.9 fusion.refs_2_
  101.2 10.8 %adam.1 = (f32[2048,128]{1,0:T(8,128)}, f32[2048,128]{1,0:T(8,128)}, f32[2048,128]{1,0:T(8,128)}, f32[8,128]{1,0:T(8,128)}) custom-call(s32[32,128]{1,0:T(8,128)} %get-tuple-element.32.wanted, bf16[128,72,128]{2,1,0:T(8,128)(2,1)} %copy-done, f32[2048,128]{1,0:T(8,128)} %table.1, f32[2048,128]{1,0:T(8,128)} %m1.1, f32[2048,128]{1,0:T(8,128)} %m2.1), custom_call_target="tpu_custom_call" | custom-call | flops 4294967296 | bytes 7340032 | tf_op jit(solution)/shard_map/adam/pallas_call | solution.py:618
  112.0 1.9 %all-to-all-done.3.refs_0_ = bf16[64,56,128]{2,1,0:T(8,128)(2,1)S(1)} async-done(((bf16[64,56,128]{2,1,0:T(8,128)(2,1)}), bf16[64,56,128]{2,1,0:T(8,128)(2,1)S(1)}, u32[]{:S(2)}, u32[]{:S(2)}) %all-to-all-start.3) | async-done | bytes 917536 | tf_op jit(solution)/shard_map/all_to_all | solution.py:665
  113.9 1.9 %collective-permute-start.2 = (bf16[64,56,128]{2,1,0:T(8,128)(2,1)S(1)}, bf16[64,56,128]{2,1,0:T(8,128)(2,1)S(1)}, u32[]{:S(2)}, u32[]{:S(2)}) collective-permute-start(bf16[64,56,128]{2,1,0:T(8,128)(2,1)S(1)} %after.1), channel_id=1, source_target_pairs={{0,4},{4,0},{1,5},{5,1},{2,6},{6,2},{3,7},{7,3},{8,12},{12,8},{9,1... | collective-permute-start | bytes 2752520 | tf_op jit(solution)/shard_map/ppermute | solution.py:668
  115.8 1.3 %weight_out.2 = (f32[768,1024]{1,0:T(8,128)}, f32[128,1024]{1,0:T(8,128)}) custom-call(s32[1]{0:T(128)} %bitcast.9.core.side, bf16[4,4,4,56,128]{4,3,2,1,0:T(8,128)(2,1)S(1)} %bitcast.22), custom_call_target="tpu_custom_call" | custom-call | flops 786432 | bytes 2359296 | tf_op jit(solution)/shard_map/weight_out/pallas_call | solution.py:542
  117.2 0.8 collective-permute-done.2
  117.9 1.3 %weight_out.3 = (f32[768,1024]{1,0:T(8,128)}, f32[128,1024]{1,0:T(8,128)}) custom-call(s32[1]{0:T(128)S(6)} %sub.3.side, bf16[4,4,4,56,128]{4,3,2,1,0:T(8,128)(2,1)S(1)} %bitcast.24, f32[768,1024]{1,0:T(8,128)} %get-tuple-element.50.rest_0_, f32[128,1024]{1,0:T(8,128)} %get-tuple-element.51.rest_1_), custom_call_target="tpu_custom_call", output_to_operand_aliasing={{0}: (2, {}), {1}: (3, {})} | custom-call | flops 786432 | bytes 2359296 | tf_op jit(solution)/shard_map/weight_out/pallas_call | solution.py:542
  (9 shorter events, 0.7 us)
Async XLA Ops:
  0.6 31.3 %copy-start.1 = (bf16[128,768]{1,0:T(8,128)(2,1)S(1)}, bf16[128,768]{1,0:T(8,128)(2,1)}, u32[]{:S(2)}) copy-start(bf16[128,768]{1,0:T(8,128)(2,1)} %feats.3) | copy-start | bytes 589828
  27.6 23.7 %all-to-all-start.1 = ((bf16[128,32,128]{2,1,0:T(8,128)(2,1)}), bf16[128,32,128]{2,1,0:T(8,128)(2,1)S(1)}, u32[]{:S(2)}, u32[]{:S(2)}) async-start(bf16[128,32,128]{2,1,0:T(8,128)(2,1)} %bitcast.30), calls=%async_computation.1 | async-start | bytes 2097152 | tf_op jit(solution)/shard_map/all_to_all | solution.py:665
  31.9 6.1 %collective-permute-start = (bf16[128,768]{1,0:T(8,128)(2,1)S(1)}, bf16[128,768]{1,0:T(8,128)(2,1)S(1)}, u32[]{:S(2)}, u32[]{:S(2)}) collective-permute-start(bf16[128,768]{1,0:T(8,128)(2,1)S(1)} %copy-done.1), channel_id=1, source_target_pairs={{0,4},{4,0},{1,5},{5,1},{2,6},{6,2},{3,7},{7,3},{8,12},{12,8},{9,1... | collective-permute-start | bytes 589832 | tf_op jit(solution)/shard_map/ppermute | solution.py:668
  52.2 1.7 %collective-permute-start.1 = (bf16[128,640]{1,0:T(8,128)(2,1)S(1)}, bf16[128,640]{1,0:T(8,128)(2,1)S(1)}, u32[]{:S(2)}, u32[]{:S(2)}) collective-permute-start(bf16[128,640]{1,0:T(8,128)(2,1)S(1)} %get-tuple-element.42), channel_id=1, source_target_pairs={{0,4},{4,0},{1,5},{5,1},{2,6},{6,2},{3,7},{7,3},{8,12},{12,8},{9,1... | collective-permute-start | bytes 491528 | tf_op jit(solution)/shard_map/ppermute | solution.py:668
  91.5 6.2 %copy-start = (bf16[128,72,128]{2,1,0:T(8,128)(2,1)}, bf16[128,72,128]{2,1,0:T(8,128)(2,1)S(1)}, u32[]{:S(2)}) copy-start(bf16[128,72,128]{2,1,0:T(8,128)(2,1)S(1)} %all_to_all.21.bundle) | copy-start | bytes 7077892
  92.8 21.0 %all-to-all-start.3 = ((bf16[64,56,128]{2,1,0:T(8,128)(2,1)}), bf16[64,56,128]{2,1,0:T(8,128)(2,1)S(1)}, u32[]{:S(2)}, u32[]{:S(2)}) async-start(bf16[64,56,128]{2,1,0:T(8,128)(2,1)} %sum_parts.1), calls=%async_computation.3 | async-start | bytes 1835008 | tf_op jit(solution)/shard_map/all_to_all | solution.py:665
  113.9 4.0 %collective-permute-start.2 = (bf16[64,56,128]{2,1,0:T(8,128)(2,1)S(1)}, bf16[64,56,128]{2,1,0:T(8,128)(2,1)S(1)}, u32[]{:S(2)}, u32[]{:S(2)}) collective-permute-start(bf16[64,56,128]{2,1,0:T(8,128)(2,1)S(1)} %after.1), channel_id=1, source_target_pairs={{0,4},{4,0},{1,5},{5,1},{2,6},{6,2},{3,7},{7,3},{8,12},{12,8},{9,1... | collective-permute-start | bytes 2752520 | tf_op jit(solution)/shard_map/ppermute | solution.py:668

commit v8 on v7

--- a/solution.py
+++ b/solution.py
@@ -597,22 +597,25 @@
             side_scr[at, :] = jnp.broadcast_to(hi[:, b : b + 1], (LANES, LANES)).astype(BF16)
         copy.wait()
 
-    here = side_scr[...] == step.astype(F32).astype(BF16)
-    mark = jnp.where(here, BF16(1.0), BF16(0.0))
     got = arrived[...].reshape(LANES * CAP, LANES)
-    both = dot(hot_scr[...], jnp.concatenate([got * mark, mark], axis=1))
-    grad = both[:, :LANES]
-    touched = both[:, LANES:] > 0.0
-    m = 0.9 * m1[...] + 0.1 * grad
-    v = 0.999 * m2[...] + 0.001 * grad * grad
-    update = 0.05 * (m / (1.0 - 0.9**10)) / (jnp.sqrt(v / (1.0 - 0.999**10)) + 1e-08)
-    new_table[...] = jnp.where(touched, table[...] - update, table[...])
-    new_m1[...] = jnp.where(touched, m, m1[...])
-    new_m2[...] = jnp.where(touched, v, m2[...])
+    parts = table.shape[0] // 256
+    for part in range(parts):
+        at = slice(part * 256, (part + 1) * 256)
+        here = side_scr[...] == (step * parts + part).astype(F32).astype(BF16)
+        mark = jnp.where(here, BF16(1.0), BF16(0.0))
+        both = dot(hot_scr[...], jnp.concatenate([got * mark, mark], axis=1))
+        grad = both[:, :LANES]
+        touched = both[:, LANES:] > 0.0
+        m = 0.9 * m1[at, :] + 0.1 * grad
+        v = 0.999 * m2[at, :] + 0.001 * grad * grad
+        update = 0.05 * (m / (1.0 - 0.9**10)) / (jnp.sqrt(v / (1.0 - 0.999**10)) + 1e-08)
+        new_table[at, :] = jnp.where(touched, table[at, :] - update, table[at, :])
+        new_m1[at, :] = jnp.where(touched, m, m1[at, :])
+        new_m2[at, :] = jnp.where(touched, v, m2[at, :])
 
 
 def adam(wanted, bundle, table, m1, m2):
-    rows = 256
+    rows = 512
     block = pl.BlockSpec((rows, LANES), lambda i: (i, 0))
     slots = LANES * CAP
     return pl.pallas_call(
@@ -624,7 +627,7 @@
         out_specs=(block, block, block, pl.BlockSpec((8, LANES), lambda i: (0, 0))),
         scratch_shapes=[
             pltpu.VMEM((LANES, CAP, LANES), BF16),
-            pltpu.VMEM((rows, slots), BF16),
+            pltpu.VMEM((256, slots), BF16),
             pltpu.VMEM((slots, LANES), BF16),
             pltpu.SemaphoreType.DMA((1,)),
         ],

time: 120 us -> 120 us (level)
  Pallas kernels: 29.3 us -> 27.8 us
  waiting for transfers between devices: 15 us -> 16.5 us
    all_to_all x2, waiting for transfers between devices: 14.2 us -> 15.7 us  [exchange(): return lax.all_to_all(a, axes, split_axis=0, concat_axis=0, tiled=True)]
    pallas_call x1, Pallas kernels: 10.8 us -> 9.27 us  [adam(): pl.pallas_call(adam_kernel, grid=(table.shape[0] // rows,), out_shape=(ja...]
  transfers between devices with their start and end apart: 5 -> 5, of which waited for: 3 -> 3; matrix products, arithmetic and copies ran while one was open for 3% -> 3% of each run, Pallas kernels for 16% -> 15%
where the time goes in v8:
time: 120 us; the launch traced here: 119 us
  blocking collectives  57.9 us (48%)
  Pallas kernels  27.8 us (23%)
  waiting for transfers between devices  16.5 us (14%)
  starting transfers between devices  12.7 us (11%)
  local copies, waits for them, and re-layouts  2.39 us (2%)
    all_to_all x2, blocking collectives, exchange(): return lax.all_to_all(a, axes, split_axis=0, concat_axis=0, tiled=True)  57.9 us
    all_to_all x2, waiting for transfers between devices, exchange(): return lax.all_to_all(a, axes, split_axis=0, concat_axis=0, tiled=True)  15.7 us
    pallas_call x1, Pallas kernels, adam(): pl.pallas_call(adam_kernel, grid=(table.shape[0] // rows,), out_shape=(ja...  9.27 us
    all_to_all x2, starting transfers between devices, exchange(): return lax.all_to_all(a, axes, split_axis=0, concat_axis=0, tiled=True)  9.16 us
    pallas_call x1, Pallas kernels, gather(): pl.pallas_call(gather_kernel, out_shape=(pltpu.HBM((slots, LANES), BF16),...  3.83 us
    ppermute x3, starting transfers between devices, swap(): return lax.ppermute(a, 'core', [(0, 1), (1, 0)])  3.56 us
    pallas_call x1, Pallas kernels, paper_rows(): pl.pallas_call(paper_kernel, out_shape=pltpu.HBM((LANES, span, LANES), BF...  3.15 us
    pallas_call x2, Pallas kernels, spread(): pl.pallas_call(spread_kernel, out_shape=(pltpu.HBM((feats, hidden), F32),...  2.65 us
  transfers between devices with their start and end apart: 5, of which 3 were waited for; matrix products, arithmetic and copies ran while one was open for 3% of the time, Pallas kernels for 15%

profile of v8, /device:TPU:1, one launch (start us, length us, event | category | flops | bytes accessed | tf_op | source)
XLA Modules:
  0.0 119.4 jit_solution(10508886375140366567)
XLA Ops:
  0.6 2.1 %place.1 = (s32[128,128]{1,0:T(8,128)S(1)}, s32[32,128]{1,0:T(8,128)S(1)}, f32[128,128]{1,0:T(8,128)S(1)}, bf16[2,128,128]{2,1,0:T(8,128)(2,1)S(1)}, bf16[256,1024]{1,0:T(8,128)(2,1)S(1)}) custom-call(s32[1]{0:T(128)} %bitcast.lane_group, s32[16,128]{1,0:T(8,128)} %bitcast.31, s32[16,128]{1,0:T(8,128)} %bitcast.32, s32[1,128]{1,0:T(1,128)} %bitcast.33, ...), custom_call_target="tpu_custom_call" | custom-call | tf_op jit(solution)/shard_map/place/pallas_call | solution.py:182
  2.8 20.9 %all_to_all.20 = s32[128,1,128]{2,1,0:T(1,128)S(1)} all-to-all(s32[128,1,128]{2,1,0:T(1,128)S(1)} %bitcast.27), channel_id=1, replica_groups=mesh['chip'=16,'core'=2,'mp'=4] {'chip','core','mp'}, dimensions={0} | all-to-all | bytes 131072 | tf_op jit(solution)/shard_map/all_to_all | solution.py:668
  23.7 3.8 %gather_rows.1 = (bf16[4096,128]{1,0:T(8,128)(2,1)}, s32[32,128]{1,0:T(8,128)}) custom-call(s32[128,128]{1,0:T(8,128)S(1)} %bitcast.25, bf16[256,1024]{1,0:T(8,128)(2,1)S(1)} %get-tuple-element.31.wide), custom_call_target="tpu_custom_call" | custom-call | tf_op jit(solution)/shard_map/gather_rows/pallas_call | solution.py:236
  27.6 4.3 %all-to-all-start.1 = ((bf16[128,32,128]{2,1,0:T(8,128)(2,1)}), bf16[128,32,128]{2,1,0:T(8,128)(2,1)S(1)}, u32[]{:S(2)}, u32[]{:S(2)}) async-start(bf16[128,32,128]{2,1,0:T(8,128)(2,1)} %bitcast.30), calls=%async_computation.1 | async-start | bytes 2097152 | tf_op jit(solution)/shard_map/all_to_all | solution.py:668
  31.9 1.1 collective-permute-start
  33.1 1.8 %prep.1 = (f32[128,1024]{1,0:T(8,128)S(1)}, f32[128,1024]{1,0:T(8,128)S(1)}, bf16[128,1024]{1,0:T(8,128)(2,1)S(1)}) custom-call(bf16[128,768]{1,0:T(8,128)(2,1)S(1)} %copy-done.1, bf16[768,1024]{1,0:T(8,128)(2,1)} %w_self_in.1, f32[128,1024]{1,0:T(8,128)} %cot_in.1, bf16[128,1024]{1,0:T(8,128)(2,1)} %w_in.1), custom_call_target="tpu_custom_call" | custom-call | flops 201326592 | bytes 4194304 | tf_op jit(solution)/shard_map/prep/pallas_call | solution.py:308
  34.9 3.2 %gather_papers.1.rest_1_.papers_in = bf16[128,16,128]{2,1,0:T(8,128)(2,1)} custom-call(s32[128,128]{1,0:T(8,128)S(1)} %bitcast.26, bf16[1024,768]{1,0:T(8,128)(2,1)} %paper_in.1), custom_call_target="tpu_custom_call" | custom-call | flops 402653184 | bytes 3145728 | tf_op jit(solution)/shard_map/gather_papers/pallas_call | solution.py:279
  38.1 0.9 turn.1.rest_0_.feats_in
  39.0 12.4 %all-to-all-done.1 = bf16[128,32,128]{2,1,0:T(8,128)(2,1)S(1)} async-done(((bf16[128,32,128]{2,1,0:T(8,128)(2,1)}), bf16[128,32,128]{2,1,0:T(8,128)(2,1)S(1)}, u32[]{:S(2)}, u32[]{:S(2)}) %all-to-all-start.1) | async-done | bytes 1048608 | tf_op jit(solution)/shard_map/all_to_all | solution.py:668
  51.3 0.9 layer.1
  52.7 1.2 slot_grads.1
  53.9 0.6 weight_part.1
  54.5 37.0 %all_to_all.21.bundle = bf16[128,72,128]{2,1,0:T(8,128)(2,1)S(1)} all-to-all(bf16[128,72,128]{2,1,0:T(8,128)(2,1)S(1)} %weight_part.1), channel_id=1, replica_groups=mesh['chip'=16,'core'=2,'mp'=4] {'chip','core','mp'}, dimensions={0} | all-to-all | bytes 4718592 | tf_op jit(solution)/shard_map/all_to_all | solution.py:668
  91.5 1.3 %sum_parts.1 = bf16[64,56,128]{2,1,0:T(8,128)(2,1)} custom-call(bf16[128,72,128]{2,1,0:T(8,128)(2,1)S(1)} %all_to_all.21.bundle), custom_call_target="tpu_custom_call" | custom-call | tf_op jit(solution)/shard_map/sum_parts/pallas_call | solution.py:491
  92.8 4.8 %all-to-all-start.3 = ((bf16[64,56,128]{2,1,0:T(8,128)(2,1)}), bf16[64,56,128]{2,1,0:T(8,128)(2,1)S(1)}, u32[]{:S(2)}, u32[]{:S(2)}) async-start(bf16[64,56,128]{2,1,0:T(8,128)(2,1)} %sum_parts.1), calls=%async_computation.3 | async-start | bytes 1835008 | tf_op jit(solution)/shard_map/all_to_all | solution.py:668
  97.7 1.0 slice.20
  98.7 1.4 %copy.24 = bf16[128,12,128]{0,2,1:T(8,128)(2,1)S(1)} copy(bf16[128,12,128]{2,1,0:T(8,128)(2,1)} %slice.20) | data formatting | bytes 786432 | tf_op jit(solution)/shard_map/slice | solution.py:699
  100.3 0.9 fusion.refs_2_
  101.2 9.3 %adam.1 = (f32[2048,128]{1,0:T(8,128)}, f32[2048,128]{1,0:T(8,128)}, f32[2048,128]{1,0:T(8,128)}, f32[8,128]{1,0:T(8,128)}) custom-call(s32[32,128]{1,0:T(8,128)} %get-tuple-element.32.wanted, bf16[128,72,128]{2,1,0:T(8,128)(2,1)} %copy-done, f32[2048,128]{1,0:T(8,128)} %table.1, f32[2048,128]{1,0:T(8,128)} %m1.1, f32[2048,128]{1,0:T(8,128)} %m2.1), custom_call_target="tpu_custom_call" | custom-call | flops 4294967296 | bytes 7340032 | tf_op jit(solution)/shard_map/adam/pallas_call | solution.py:621
  110.5 3.4 %all-to-all-done.3.refs_0_ = bf16[64,56,128]{2,1,0:T(8,128)(2,1)S(1)} async-done(((bf16[64,56,128]{2,1,0:T(8,128)(2,1)}), bf16[64,56,128]{2,1,0:T(8,128)(2,1)S(1)}, u32[]{:S(2)}, u32[]{:S(2)}) %all-to-all-start.3) | async-done | bytes 917536 | tf_op jit(solution)/shard_map/all_to_all | solution.py:668
  113.9 1.9 %collective-permute-start.2 = (bf16[64,56,128]{2,1,0:T(8,128)(2,1)S(1)}, bf16[64,56,128]{2,1,0:T(8,128)(2,1)S(1)}, u32[]{:S(2)}, u32[]{:S(2)}) collective-permute-start(bf16[64,56,128]{2,1,0:T(8,128)(2,1)S(1)} %after.1), channel_id=1, source_target_pairs={{0,4},{4,0},{1,5},{5,1},{2,6},{6,2},{3,7},{7,3},{8,12},{12,8},{9,1... | collective-permute-start | bytes 2752520 | tf_op jit(solution)/shard_map/ppermute | solution.py:671
  115.8 1.3 %weight_out.2 = (f32[768,1024]{1,0:T(8,128)}, f32[128,1024]{1,0:T(8,128)}) custom-call(s32[1]{0:T(128)} %bitcast.9.core.side, bf16[4,4,4,56,128]{4,3,2,1,0:T(8,128)(2,1)S(1)} %bitcast.22), custom_call_target="tpu_custom_call" | custom-call | flops 786432 | bytes 2359296 | tf_op jit(solution)/shard_map/weight_out/pallas_call | solution.py:542
  117.2 0.8 collective-permute-done.2
  117.9 1.3 %weight_out.3 = (f32[768,1024]{1,0:T(8,128)}, f32[128,1024]{1,0:T(8,128)}) custom-call(s32[1]{0:T(128)S(6)} %sub.3.side, bf16[4,4,4,56,128]{4,3,2,1,0:T(8,128)(2,1)S(1)} %bitcast.24, f32[768,1024]{1,0:T(8,128)} %get-tuple-element.50.rest_0_, f32[128,1024]{1,0:T(8,128)} %get-tuple-element.51.rest_1_), custom_call_target="tpu_custom_call", output_to_operand_aliasing={{0}: (2, {}), {1}: (3, {})} | custom-call | flops 786432 | bytes 2359296 | tf_op jit(solution)/shard_map/weight_out/pallas_call | solution.py:542
  (9 shorter events, 0.7 us)
Async XLA Ops:
  0.6 31.3 %copy-start.1 = (bf16[128,768]{1,0:T(8,128)(2,1)S(1)}, bf16[128,768]{1,0:T(8,128)(2,1)}, u32[]{:S(2)}) copy-start(bf16[128,768]{1,0:T(8,128)(2,1)} %feats.3) | copy-start | bytes 589828
  27.6 23.7 %all-to-all-start.1 = ((bf16[128,32,128]{2,1,0:T(8,128)(2,1)}), bf16[128,32,128]{2,1,0:T(8,128)(2,1)S(1)}, u32[]{:S(2)}, u32[]{:S(2)}) async-start(bf16[128,32,128]{2,1,0:T(8,128)(2,1)} %bitcast.30), calls=%async_computation.1 | async-start | bytes 2097152 | tf_op jit(solution)/shard_map/all_to_all | solution.py:668
  31.9 6.1 %collective-permute-start = (bf16[128,768]{1,0:T(8,128)(2,1)S(1)}, bf16[128,768]{1,0:T(8,128)(2,1)S(1)}, u32[]{:S(2)}, u32[]{:S(2)}) collective-permute-start(bf16[128,768]{1,0:T(8,128)(2,1)S(1)} %copy-done.1), channel_id=1, source_target_pairs={{0,4},{4,0},{1,5},{5,1},{2,6},{6,2},{3,7},{7,3},{8,12},{12,8},{9,1... | collective-permute-start | bytes 589832 | tf_op jit(solution)/shard_map/ppermute | solution.py:671
  52.2 1.7 %collective-permute-start.1 = (bf16[128,640]{1,0:T(8,128)(2,1)S(1)}, bf16[128,640]{1,0:T(8,128)(2,1)S(1)}, u32[]{:S(2)}, u32[]{:S(2)}) collective-permute-start(bf16[128,640]{1,0:T(8,128)(2,1)S(1)} %get-tuple-element.42), channel_id=1, source_target_pairs={{0,4},{4,0},{1,5},{5,1},{2,6},{6,2},{3,7},{7,3},{8,12},{12,8},{9,1... | collective-permute-start | bytes 491528 | tf_op jit(solution)/shard_map/ppermute | solution.py:671
  91.5 6.2 %copy-start = (bf16[128,72,128]{2,1,0:T(8,128)(2,1)}, bf16[128,72,128]{2,1,0:T(8,128)(2,1)S(1)}, u32[]{:S(2)}) copy-start(bf16[128,72,128]{2,1,0:T(8,128)(2,1)S(1)} %all_to_all.21.bundle) | copy-start | bytes 7077892
  92.8 21.0 %all-to-all-start.3 = ((bf16[64,56,128]{2,1,0:T(8,128)(2,1)}), bf16[64,56,128]{2,1,0:T(8,128)(2,1)S(1)}, u32[]{:S(2)}, u32[]{:S(2)}) async-start(bf16[64,56,128]{2,1,0:T(8,128)(2,1)} %sum_parts.1), calls=%async_computation.3 | async-start | bytes 1835008 | tf_op jit(solution)/shard_map/all_to_all | solution.py:668
  113.9 4.0 %collective-permute-start.2 = (bf16[64,56,128]{2,1,0:T(8,128)(2,1)S(1)}, bf16[64,56,128]{2,1,0:T(8,128)(2,1)S(1)}, u32[]{:S(2)}, u32[]{:S(2)}) collective-permute-start(bf16[64,56,128]{2,1,0:T(8,128)(2,1)S(1)} %after.1), channel_id=1, source_target_pairs={{0,4},{4,0},{1,5},{5,1},{2,6},{6,2},{3,7},{7,3},{8,12},{12,8},{9,1... | collective-permute-start | bytes 2752520 | tf_op jit(solution)/shard_map/ppermute | solution.py:671

commit v9 on v7

--- a/solution.py
+++ b/solution.py
@@ -212,10 +212,11 @@
     for b in range(lines):
         hot_scr[b * LANES : (b + 1) * LANES, :] = onehot(lo[:, b : b + 1] == lanes)
         hi_scr[b * LANES : (b + 1) * LANES, :] = jnp.broadcast_to(hi[:, b : b + 1], (LANES, LANES))
-    chunk = 512
+    quarter_rows = out_scr.shape[0] // 4
+    chunks = [quarter_rows] * 3 + [quarter_rows // 2] + [quarter_rows // 4] * 2
     outs = []
-    for c in range(out_scr.shape[0] // chunk):
-        at = pl.ds(c * chunk, chunk)
+    for c, chunk in enumerate(chunks):
+        at = pl.ds(sum(chunks[:c]), chunk)
         hot = hot_scr[at, :]
         high = hi_scr[at, :]
         out = jnp.zeros((chunk, LANES), F32)
@@ -478,12 +479,8 @@
     mine = mine.astype(BF16)
     for i in range(out_scr.shape[0]):
         out_scr[i] = mine
-    q = out_scr.shape[0] // 4
-    copies = fetch(
-        [(out_scr.at[pl.ds(i * q, q)], out.at[pl.ds(i * q, q)]) for i in range(4)], sems
-    )
-    for c in copies:
-        c.wait()
+    copy = fetch([(out_scr, out)], sems)[0]
+    copy.wait()
 
 
 def sum_parts(bundle, peers):
@@ -495,7 +492,7 @@
         out_specs=HBM,
         scratch_shapes=[
             pltpu.VMEM((peers, rows, LANES), BF16),
-            pltpu.SemaphoreType.DMA((4,)),
+            pltpu.SemaphoreType.DMA((1,)),
         ],
         compiler_params=params(),
         name="sum_parts",

time: 120 us -> 120 us (level)
  no operation moved by 1% of the time
where the time goes in v9:
time: 120 us; the launch traced here: 119 us
  blocking collectives  57.9 us (48%)
  Pallas kernels  29.2 us (24%)
  waiting for transfers between devices  15 us (12%)
  starting transfers between devices  12.7 us (11%)
  local copies, waits for them, and re-layouts  2.39 us (2%)
    all_to_all x2, blocking collectives, exchange(): return lax.all_to_all(a, axes, split_axis=0, concat_axis=0, tiled=True)  57.9 us
    all_to_all x2, waiting for transfers between devices, exchange(): return lax.all_to_all(a, axes, split_axis=0, concat_axis=0, tiled=True)  14.2 us
    pallas_call x1, Pallas kernels, adam(): pl.pallas_call(adam_kernel, grid=(table.shape[0] // rows,), out_shape=(ja...  10.8 us
    all_to_all x2, starting transfers between devices, exchange(): return lax.all_to_all(a, axes, split_axis=0, concat_axis=0, tiled=True)  9.16 us
    pallas_call x1, Pallas kernels, gather(): pl.pallas_call(gather_kernel, out_shape=(pltpu.HBM((slots, LANES), BF16),...  3.8 us
    ppermute x3, starting transfers between devices, swap(): return lax.ppermute(a, 'core', [(0, 1), (1, 0)])  3.56 us
    pallas_call x1, Pallas kernels, paper_rows(): pl.pallas_call(paper_kernel, out_shape=pltpu.HBM((LANES, span, LANES), BF...  3.15 us
    pallas_call x2, Pallas kernels, spread(): pl.pallas_call(spread_kernel, out_shape=(pltpu.HBM((feats, hidden), F32),...  2.65 us
  transfers between devices with their start and end apart: 5, of which 3 were waited for; matrix products, arithmetic and copies ran while one was open for 3% of the time, Pallas kernels for 16%

profile of v9, /device:TPU:1, one launch (start us, length us, event | category | flops | bytes accessed | tf_op | source)
XLA Modules:
  0.0 119.4 jit_solution(2146465703920028056)
XLA Ops:
  0.6 2.1 %place.1 = (s32[128,128]{1,0:T(8,128)S(1)}, s32[32,128]{1,0:T(8,128)S(1)}, f32[128,128]{1,0:T(8,128)S(1)}, bf16[2,128,128]{2,1,0:T(8,128)(2,1)S(1)}, bf16[256,1024]{1,0:T(8,128)(2,1)S(1)}) custom-call(s32[1]{0:T(128)} %bitcast.lane_group, s32[16,128]{1,0:T(8,128)} %bitcast.31, s32[16,128]{1,0:T(8,128)} %bitcast.32, s32[1,128]{1,0:T(1,128)} %bitcast.33, ...), custom_call_target="tpu_custom_call" | custom-call | tf_op jit(solution)/shard_map/place/pallas_call | solution.py:182
  2.8 20.9 %all_to_all.20 = s32[128,1,128]{2,1,0:T(1,128)S(1)} all-to-all(s32[128,1,128]{2,1,0:T(1,128)S(1)} %bitcast.27), channel_id=1, replica_groups=mesh['chip'=16,'core'=2,'mp'=4] {'chip','core','mp'}, dimensions={0} | all-to-all | bytes 131072 | tf_op jit(solution)/shard_map/all_to_all | solution.py:662
  23.7 3.8 %gather_rows.1 = (bf16[4096,128]{1,0:T(8,128)(2,1)}, s32[32,128]{1,0:T(8,128)}) custom-call(s32[128,128]{1,0:T(8,128)S(1)} %bitcast.25, bf16[256,1024]{1,0:T(8,128)(2,1)S(1)} %get-tuple-element.31.wide), custom_call_target="tpu_custom_call" | custom-call | tf_op jit(solution)/shard_map/gather_rows/pallas_call | solution.py:237
  27.5 4.3 %all-to-all-start.1 = ((bf16[128,32,128]{2,1,0:T(8,128)(2,1)}), bf16[128,32,128]{2,1,0:T(8,128)(2,1)S(1)}, u32[]{:S(2)}, u32[]{:S(2)}) async-start(bf16[128,32,128]{2,1,0:T(8,128)(2,1)} %bitcast.30), calls=%async_computation.1 | async-start | bytes 2097152 | tf_op jit(solution)/shard_map/all_to_all | solution.py:662
  31.9 1.1 collective-permute-start
  33.0 1.8 %prep.1 = (f32[128,1024]{1,0:T(8,128)S(1)}, f32[128,1024]{1,0:T(8,128)S(1)}, bf16[128,1024]{1,0:T(8,128)(2,1)S(1)}) custom-call(bf16[128,768]{1,0:T(8,128)(2,1)S(1)} %copy-done.1, bf16[768,1024]{1,0:T(8,128)(2,1)} %w_self_in.1, f32[128,1024]{1,0:T(8,128)} %cot_in.1, bf16[128,1024]{1,0:T(8,128)(2,1)} %w_in.1), custom_call_target="tpu_custom_call" | custom-call | flops 201326592 | bytes 4194304 | tf_op jit(solution)/shard_map/prep/pallas_call | solution.py:309
  34.9 3.2 %gather_papers.1.rest_1_.papers_in = bf16[128,16,128]{2,1,0:T(8,128)(2,1)} custom-call(s32[128,128]{1,0:T(8,128)S(1)} %bitcast.26, bf16[1024,768]{1,0:T(8,128)(2,1)} %paper_in.1), custom_call_target="tpu_custom_call" | custom-call | flops 402653184 | bytes 3145728 | tf_op jit(solution)/shard_map/gather_papers/pallas_call | solution.py:280
  38.0 0.9 turn.1.rest_0_.feats_in
  38.9 12.4 %all-to-all-done.1 = bf16[128,32,128]{2,1,0:T(8,128)(2,1)S(1)} async-done(((bf16[128,32,128]{2,1,0:T(8,128)(2,1)}), bf16[128,32,128]{2,1,0:T(8,128)(2,1)S(1)}, u32[]{:S(2)}, u32[]{:S(2)}) %all-to-all-start.1) | async-done | bytes 1048608 | tf_op jit(solution)/shard_map/all_to_all | solution.py:662
  51.3 0.9 layer.1
  52.7 1.2 slot_grads.1
  53.9 0.6 weight_part.1
  54.5 37.0 %all_to_all.21.bundle = bf16[128,72,128]{2,1,0:T(8,128)(2,1)S(1)} all-to-all(bf16[128,72,128]{2,1,0:T(8,128)(2,1)S(1)} %weight_part.1), channel_id=1, replica_groups=mesh['chip'=16,'core'=2,'mp'=4] {'chip','core','mp'}, dimensions={0} | all-to-all | bytes 4718592 | tf_op jit(solution)/shard_map/all_to_all | solution.py:662
  91.5 1.3 %sum_parts.1 = bf16[64,56,128]{2,1,0:T(8,128)(2,1)} custom-call(bf16[128,72,128]{2,1,0:T(8,128)(2,1)S(1)} %all_to_all.21.bundle), custom_call_target="tpu_custom_call" | custom-call | tf_op jit(solution)/shard_map/sum_parts/pallas_call | solution.py:488
  92.8 4.8 %all-to-all-start.3 = ((bf16[64,56,128]{2,1,0:T(8,128)(2,1)}), bf16[64,56,128]{2,1,0:T(8,128)(2,1)S(1)}, u32[]{:S(2)}, u32[]{:S(2)}) async-start(bf16[64,56,128]{2,1,0:T(8,128)(2,1)} %sum_parts.1), calls=%async_computation.3 | async-start | bytes 1835008 | tf_op jit(solution)/shard_map/all_to_all | solution.py:662
  97.6 1.0 slice.20
  98.6 1.4 %copy.24 = bf16[128,12,128]{0,2,1:T(8,128)(2,1)S(1)} copy(bf16[128,12,128]{2,1,0:T(8,128)(2,1)} %slice.20) | data formatting | bytes 786432 | tf_op jit(solution)/shard_map/slice | solution.py:693
  100.3 0.9 fusion.refs_2_
  101.2 10.8 %adam.1 = (f32[2048,128]{1,0:T(8,128)}, f32[2048,128]{1,0:T(8,128)}, f32[2048,128]{1,0:T(8,128)}, f32[8,128]{1,0:T(8,128)}) custom-call(s32[32,128]{1,0:T(8,128)} %get-tuple-element.32.wanted, bf16[128,72,128]{2,1,0:T(8,128)(2,1)} %copy-done, f32[2048,128]{1,0:T(8,128)} %table.1, f32[2048,128]{1,0:T(8,128)} %m1.1, f32[2048,128]{1,0:T(8,128)} %m2.1), custom_call_target="tpu_custom_call" | custom-call | flops 4294967296 | bytes 7340032 | tf_op jit(solution)/shard_map/adam/pallas_call | solution.py:615
  112.0 1.9 %all-to-all-done.3.refs_0_ = bf16[64,56,128]{2,1,0:T(8,128)(2,1)S(1)} async-done(((bf16[64,56,128]{2,1,0:T(8,128)(2,1)}), bf16[64,56,128]{2,1,0:T(8,128)(2,1)S(1)}, u32[]{:S(2)}, u32[]{:S(2)}) %all-to-all-start.3) | async-done | bytes 917536 | tf_op jit(solution)/shard_map/all_to_all | solution.py:662
  113.8 1.9 %collective-permute-start.2 = (bf16[64,56,128]{2,1,0:T(8,128)(2,1)S(1)}, bf16[64,56,128]{2,1,0:T(8,128)(2,1)S(1)}, u32[]{:S(2)}, u32[]{:S(2)}) collective-permute-start(bf16[64,56,128]{2,1,0:T(8,128)(2,1)S(1)} %after.1), channel_id=1, source_target_pairs={{0,4},{4,0},{1,5},{5,1},{2,6},{6,2},{3,7},{7,3},{8,12},{12,8},{9,1... | collective-permute-start | bytes 2752520 | tf_op jit(solution)/shard_map/ppermute | solution.py:665
  115.8 1.3 %weight_out.2 = (f32[768,1024]{1,0:T(8,128)}, f32[128,1024]{1,0:T(8,128)}) custom-call(s32[1]{0:T(128)} %bitcast.9.core.side, bf16[4,4,4,56,128]{4,3,2,1,0:T(8,128)(2,1)S(1)} %bitcast.22), custom_call_target="tpu_custom_call" | custom-call | flops 786432 | bytes 2359296 | tf_op jit(solution)/shard_map/weight_out/pallas_call | solution.py:539
  117.1 0.8 collective-permute-done.2
  117.9 1.3 %weight_out.3 = (f32[768,1024]{1,0:T(8,128)}, f32[128,1024]{1,0:T(8,128)}) custom-call(s32[1]{0:T(128)S(6)} %sub.3.side, bf16[4,4,4,56,128]{4,3,2,1,0:T(8,128)(2,1)S(1)} %bitcast.24, f32[768,1024]{1,0:T(8,128)} %get-tuple-element.50.rest_0_, f32[128,1024]{1,0:T(8,128)} %get-tuple-element.51.rest_1_), custom_call_target="tpu_custom_call", output_to_operand_aliasing={{0}: (2, {}), {1}: (3, {})} | custom-call | flops 786432 | bytes 2359296 | tf_op jit(solution)/shard_map/weight_out/pallas_call | solution.py:539
  (9 shorter events, 0.7 us)
Async XLA Ops:
  0.6 31.2 %copy-start.1 = (bf16[128,768]{1,0:T(8,128)(2,1)S(1)}, bf16[128,768]{1,0:T(8,128)(2,1)}, u32[]{:S(2)}) copy-start(bf16[128,768]{1,0:T(8,128)(2,1)} %feats.3) | copy-start | bytes 589828
  27.5 23.7 %all-to-all-start.1 = ((bf16[128,32,128]{2,1,0:T(8,128)(2,1)}), bf16[128,32,128]{2,1,0:T(8,128)(2,1)S(1)}, u32[]{:S(2)}, u32[]{:S(2)}) async-start(bf16[128,32,128]{2,1,0:T(8,128)(2,1)} %bitcast.30), calls=%async_computation.1 | async-start | bytes 2097152 | tf_op jit(solution)/shard_map/all_to_all | solution.py:662
  31.9 6.1 %collective-permute-start = (bf16[128,768]{1,0:T(8,128)(2,1)S(1)}, bf16[128,768]{1,0:T(8,128)(2,1)S(1)}, u32[]{:S(2)}, u32[]{:S(2)}) collective-permute-start(bf16[128,768]{1,0:T(8,128)(2,1)S(1)} %copy-done.1), channel_id=1, source_target_pairs={{0,4},{4,0},{1,5},{5,1},{2,6},{6,2},{3,7},{7,3},{8,12},{12,8},{9,1... | collective-permute-start | bytes 589832 | tf_op jit(solution)/shard_map/ppermute | solution.py:665
  52.2 1.7 %collective-permute-start.1 = (bf16[128,640]{1,0:T(8,128)(2,1)S(1)}, bf16[128,640]{1,0:T(8,128)(2,1)S(1)}, u32[]{:S(2)}, u32[]{:S(2)}) collective-permute-start(bf16[128,640]{1,0:T(8,128)(2,1)S(1)} %get-tuple-element.42), channel_id=1, source_target_pairs={{0,4},{4,0},{1,5},{5,1},{2,6},{6,2},{3,7},{7,3},{8,12},{12,8},{9,1... | collective-permute-start | bytes 491528 | tf_op jit(solution)/shard_map/ppermute | solution.py:665
  91.5 6.2 %copy-start = (bf16[128,72,128]{2,1,0:T(8,128)(2,1)}, bf16[128,72,128]{2,1,0:T(8,128)(2,1)S(1)}, u32[]{:S(2)}) copy-start(bf16[128,72,128]{2,1,0:T(8,128)(2,1)S(1)} %all_to_all.21.bundle) | copy-start | bytes 7077892
  92.8 21.0 %all-to-all-start.3 = ((bf16[64,56,128]{2,1,0:T(8,128)(2,1)}), bf16[64,56,128]{2,1,0:T(8,128)(2,1)S(1)}, u32[]{:S(2)}, u32[]{:S(2)}) async-start(bf16[64,56,128]{2,1,0:T(8,128)(2,1)} %sum_parts.1), calls=%async_computation.3 | async-start | bytes 1835008 | tf_op jit(solution)/shard_map/all_to_all | solution.py:662
  113.8 4.0 %collective-permute-start.2 = (bf16[64,56,128]{2,1,0:T(8,128)(2,1)S(1)}, bf16[64,56,128]{2,1,0:T(8,128)(2,1)S(1)}, u32[]{:S(2)}, u32[]{:S(2)}) collective-permute-start(bf16[64,56,128]{2,1,0:T(8,128)(2,1)S(1)} %after.1), channel_id=1, source_target_pairs={{0,4},{4,0},{1,5},{5,1},{2,6},{6,2},{3,7},{7,3},{8,12},{12,8},{9,1... | collective-permute-start | bytes 2752520 | tf_op jit(solution)/shard_map/ppermute | solution.py:665

commit v10 on v8

--- a/solution.py
+++ b/solution.py
@@ -212,10 +212,11 @@
     for b in range(lines):
         hot_scr[b * LANES : (b + 1) * LANES, :] = onehot(lo[:, b : b + 1] == lanes)
         hi_scr[b * LANES : (b + 1) * LANES, :] = jnp.broadcast_to(hi[:, b : b + 1], (LANES, LANES))
-    chunk = 512
+    quarter_rows = out_scr.shape[0] // 4
+    chunks = [quarter_rows] * 3 + [quarter_rows // 2] + [quarter_rows // 4] * 2
     outs = []
-    for c in range(out_scr.shape[0] // chunk):
-        at = pl.ds(c * chunk, chunk)
+    for c, chunk in enumerate(chunks):
+        at = pl.ds(sum(chunks[:c]), chunk)
         hot = hot_scr[at, :]
         high = hi_scr[at, :]
         out = jnp.zeros((chunk, LANES), F32)
@@ -478,12 +479,8 @@
     mine = mine.astype(BF16)
     for i in range(out_scr.shape[0]):
         out_scr[i] = mine
-    q = out_scr.shape[0] // 4
-    copies = fetch(
-        [(out_scr.at[pl.ds(i * q, q)], out.at[pl.ds(i * q, q)]) for i in range(4)], sems
-    )
-    for c in copies:
-        c.wait()
+    copy = fetch([(out_scr, out)], sems)[0]
+    copy.wait()
 
 
 def sum_parts(bundle, peers):
@@ -495,7 +492,7 @@
         out_specs=HBM,
         scratch_shapes=[
             pltpu.VMEM((peers, rows, LANES), BF16),
-            pltpu.SemaphoreType.DMA((4,)),
+            pltpu.SemaphoreType.DMA((1,)),
         ],
         compiler_params=params(),
         name="sum_parts",

time: 120 us -> 120 us (level)
  no operation moved by 1% of the time
where the time goes in v10:
time: 120 us; the launch traced here: 119 us
  blocking collectives  57.9 us (48%)
  Pallas kernels  27.7 us (23%)
  waiting for transfers between devices  16.5 us (14%)
  starting transfers between devices  12.7 us (11%)
  local copies, waits for them, and re-layouts  2.39 us (2%)
    all_to_all x2, blocking collectives, exchange(): return lax.all_to_all(a, axes, split_axis=0, concat_axis=0, tiled=True)  57.9 us
    all_to_all x2, waiting for transfers between devices, exchange(): return lax.all_to_all(a, axes, split_axis=0, concat_axis=0, tiled=True)  15.7 us
    pallas_call x1, Pallas kernels, adam(): pl.pallas_call(adam_kernel, grid=(table.shape[0] // rows,), out_shape=(ja...  9.27 us
    all_to_all x2, starting transfers between devices, exchange(): return lax.all_to_all(a, axes, split_axis=0, concat_axis=0, tiled=True)  9.16 us
    pallas_call x1, Pallas kernels, gather(): pl.pallas_call(gather_kernel, out_shape=(pltpu.HBM((slots, LANES), BF16),...  3.8 us
    ppermute x3, starting transfers between devices, swap(): return lax.ppermute(a, 'core', [(0, 1), (1, 0)])  3.56 us
    pallas_call x1, Pallas kernels, paper_rows(): pl.pallas_call(paper_kernel, out_shape=pltpu.HBM((LANES, span, LANES), BF...  3.15 us
    pallas_call x2, Pallas kernels, spread(): pl.pallas_call(spread_kernel, out_shape=(pltpu.HBM((feats, hidden), F32),...  2.65 us
  transfers between devices with their start and end apart: 5, of which 3 were waited for; matrix products, arithmetic and copies ran while one was open for 3% of the time, Pallas kernels for 15%

profile of v10, /device:TPU:1, one launch (start us, length us, event | category | flops | bytes accessed | tf_op | source)
XLA Modules:
  0.0 119.4 jit_solution(90072366026598683)
XLA Ops:
  0.6 2.1 %place.1 = (s32[128,128]{1,0:T(8,128)S(1)}, s32[32,128]{1,0:T(8,128)S(1)}, f32[128,128]{1,0:T(8,128)S(1)}, bf16[2,128,128]{2,1,0:T(8,128)(2,1)S(1)}, bf16[256,1024]{1,0:T(8,128)(2,1)S(1)}) custom-call(s32[1]{0:T(128)} %bitcast.lane_group, s32[16,128]{1,0:T(8,128)} %bitcast.31, s32[16,128]{1,0:T(8,128)} %bitcast.32, s32[1,128]{1,0:T(1,128)} %bitcast.33, ...), custom_call_target="tpu_custom_call" | custom-call | tf_op jit(solution)/shard_map/place/pallas_call | solution.py:182
  2.8 20.9 %all_to_all.20 = s32[128,1,128]{2,1,0:T(1,128)S(1)} all-to-all(s32[128,1,128]{2,1,0:T(1,128)S(1)} %bitcast.27), channel_id=1, replica_groups=mesh['chip'=16,'core'=2,'mp'=4] {'chip','core','mp'}, dimensions={0} | all-to-all | bytes 131072 | tf_op jit(solution)/shard_map/all_to_all | solution.py:665
  23.7 3.8 %gather_rows.1 = (bf16[4096,128]{1,0:T(8,128)(2,1)}, s32[32,128]{1,0:T(8,128)}) custom-call(s32[128,128]{1,0:T(8,128)S(1)} %bitcast.25, bf16[256,1024]{1,0:T(8,128)(2,1)S(1)} %get-tuple-element.31.wide), custom_call_target="tpu_custom_call" | custom-call | tf_op jit(solution)/shard_map/gather_rows/pallas_call | solution.py:237
  27.5 4.3 %all-to-all-start.1 = ((bf16[128,32,128]{2,1,0:T(8,128)(2,1)}), bf16[128,32,128]{2,1,0:T(8,128)(2,1)S(1)}, u32[]{:S(2)}, u32[]{:S(2)}) async-start(bf16[128,32,128]{2,1,0:T(8,128)(2,1)} %bitcast.30), calls=%async_computation.1 | async-start | bytes 2097152 | tf_op jit(solution)/shard_map/all_to_all | solution.py:665
  31.9 1.1 collective-permute-start
  33.0 1.8 %prep.1 = (f32[128,1024]{1,0:T(8,128)S(1)}, f32[128,1024]{1,0:T(8,128)S(1)}, bf16[128,1024]{1,0:T(8,128)(2,1)S(1)}) custom-call(bf16[128,768]{1,0:T(8,128)(2,1)S(1)} %copy-done.1, bf16[768,1024]{1,0:T(8,128)(2,1)} %w_self_in.1, f32[128,1024]{1,0:T(8,128)} %cot_in.1, bf16[128,1024]{1,0:T(8,128)(2,1)} %w_in.1), custom_call_target="tpu_custom_call" | custom-call | flops 201326592 | bytes 4194304 | tf_op jit(solution)/shard_map/prep/pallas_call | solution.py:309
  34.9 3.2 %gather_papers.1.rest_1_.papers_in = bf16[128,16,128]{2,1,0:T(8,128)(2,1)} custom-call(s32[128,128]{1,0:T(8,128)S(1)} %bitcast.26, bf16[1024,768]{1,0:T(8,128)(2,1)} %paper_in.1), custom_call_target="tpu_custom_call" | custom-call | flops 402653184 | bytes 3145728 | tf_op jit(solution)/shard_map/gather_papers/pallas_call | solution.py:280
  38.0 0.9 turn.1.rest_0_.feats_in
  38.9 12.4 %all-to-all-done.1 = bf16[128,32,128]{2,1,0:T(8,128)(2,1)S(1)} async-done(((bf16[128,32,128]{2,1,0:T(8,128)(2,1)}), bf16[128,32,128]{2,1,0:T(8,128)(2,1)S(1)}, u32[]{:S(2)}, u32[]{:S(2)}) %all-to-all-start.1) | async-done | bytes 1048608 | tf_op jit(solution)/shard_map/all_to_all | solution.py:665
  51.3 0.9 layer.1
  52.7 1.2 slot_grads.1
  53.9 0.6 weight_part.1
  54.5 37.0 %all_to_all.21.bundle = bf16[128,72,128]{2,1,0:T(8,128)(2,1)S(1)} all-to-all(bf16[128,72,128]{2,1,0:T(8,128)(2,1)S(1)} %weight_part.1), channel_id=1, replica_groups=mesh['chip'=16,'core'=2,'mp'=4] {'chip','core','mp'}, dimensions={0} | all-to-all | bytes 4718592 | tf_op jit(solution)/shard_map/all_to_all | solution.py:665
  91.5 1.3 %sum_parts.1 = bf16[64,56,128]{2,1,0:T(8,128)(2,1)} custom-call(bf16[128,72,128]{2,1,0:T(8,128)(2,1)S(1)} %all_to_all.21.bundle), custom_call_target="tpu_custom_call" | custom-call | tf_op jit(solution)/shard_map/sum_parts/pallas_call | solution.py:488
  92.8 4.8 %all-to-all-start.3 = ((bf16[64,56,128]{2,1,0:T(8,128)(2,1)}), bf16[64,56,128]{2,1,0:T(8,128)(2,1)S(1)}, u32[]{:S(2)}, u32[]{:S(2)}) async-start(bf16[64,56,128]{2,1,0:T(8,128)(2,1)} %sum_parts.1), calls=%async_computation.3 | async-start | bytes 1835008 | tf_op jit(solution)/shard_map/all_to_all | solution.py:665
  97.6 1.0 slice.20
  98.6 1.4 %copy.24 = bf16[128,12,128]{0,2,1:T(8,128)(2,1)S(1)} copy(bf16[128,12,128]{2,1,0:T(8,128)(2,1)} %slice.20) | data formatting | bytes 786432 | tf_op jit(solution)/shard_map/slice | solution.py:696
  100.3 0.9 fusion.refs_2_
  101.2 9.3 %adam.1 = (f32[2048,128]{1,0:T(8,128)}, f32[2048,128]{1,0:T(8,128)}, f32[2048,128]{1,0:T(8,128)}, f32[8,128]{1,0:T(8,128)}) custom-call(s32[32,128]{1,0:T(8,128)} %get-tuple-element.32.wanted, bf16[128,72,128]{2,1,0:T(8,128)(2,1)} %copy-done, f32[2048,128]{1,0:T(8,128)} %table.1, f32[2048,128]{1,0:T(8,128)} %m1.1, f32[2048,128]{1,0:T(8,128)} %m2.1), custom_call_target="tpu_custom_call" | custom-call | flops 4294967296 | bytes 7340032 | tf_op jit(solution)/shard_map/adam/pallas_call | solution.py:618
  110.5 3.4 %all-to-all-done.3.refs_0_ = bf16[64,56,128]{2,1,0:T(8,128)(2,1)S(1)} async-done(((bf16[64,56,128]{2,1,0:T(8,128)(2,1)}), bf16[64,56,128]{2,1,0:T(8,128)(2,1)S(1)}, u32[]{:S(2)}, u32[]{:S(2)}) %all-to-all-start.3) | async-done | bytes 917536 | tf_op jit(solution)/shard_map/all_to_all | solution.py:665
  113.8 1.9 %collective-permute-start.2 = (bf16[64,56,128]{2,1,0:T(8,128)(2,1)S(1)}, bf16[64,56,128]{2,1,0:T(8,128)(2,1)S(1)}, u32[]{:S(2)}, u32[]{:S(2)}) collective-permute-start(bf16[64,56,128]{2,1,0:T(8,128)(2,1)S(1)} %after.1), channel_id=1, source_target_pairs={{0,4},{4,0},{1,5},{5,1},{2,6},{6,2},{3,7},{7,3},{8,12},{12,8},{9,1... | collective-permute-start | bytes 2752520 | tf_op jit(solution)/shard_map/ppermute | solution.py:668
  115.8 1.3 %weight_out.2 = (f32[768,1024]{1,0:T(8,128)}, f32[128,1024]{1,0:T(8,128)}) custom-call(s32[1]{0:T(128)} %bitcast.9.core.side, bf16[4,4,4,56,128]{4,3,2,1,0:T(8,128)(2,1)S(1)} %bitcast.22), custom_call_target="tpu_custom_call" | custom-call | flops 786432 | bytes 2359296 | tf_op jit(solution)/shard_map/weight_out/pallas_call | solution.py:539
  117.1 0.8 collective-permute-done.2
  117.9 1.3 %weight_out.3 = (f32[768,1024]{1,0:T(8,128)}, f32[128,1024]{1,0:T(8,128)}) custom-call(s32[1]{0:T(128)S(6)} %sub.3.side, bf16[4,4,4,56,128]{4,3,2,1,0:T(8,128)(2,1)S(1)} %bitcast.24, f32[768,1024]{1,0:T(8,128)} %get-tuple-element.50.rest_0_, f32[128,1024]{1,0:T(8,128)} %get-tuple-element.51.rest_1_), custom_call_target="tpu_custom_call", output_to_operand_aliasing={{0}: (2, {}), {1}: (3, {})} | custom-call | flops 786432 | bytes 2359296 | tf_op jit(solution)/shard_map/weight_out/pallas_call | solution.py:539
  (9 shorter events, 0.7 us)
Async XLA Ops:
  0.6 31.2 %copy-start.1 = (bf16[128,768]{1,0:T(8,128)(2,1)S(1)}, bf16[128,768]{1,0:T(8,128)(2,1)}, u32[]{:S(2)}) copy-start(bf16[128,768]{1,0:T(8,128)(2,1)} %feats.3) | copy-start | bytes 589828
  27.5 23.7 %all-to-all-start.1 = ((bf16[128,32,128]{2,1,0:T(8,128)(2,1)}), bf16[128,32,128]{2,1,0:T(8,128)(2,1)S(1)}, u32[]{:S(2)}, u32[]{:S(2)}) async-start(bf16[128,32,128]{2,1,0:T(8,128)(2,1)} %bitcast.30), calls=%async_computation.1 | async-start | bytes 2097152 | tf_op jit(solution)/shard_map/all_to_all | solution.py:665
  31.9 6.1 %collective-permute-start = (bf16[128,768]{1,0:T(8,128)(2,1)S(1)}, bf16[128,768]{1,0:T(8,128)(2,1)S(1)}, u32[]{:S(2)}, u32[]{:S(2)}) collective-permute-start(bf16[128,768]{1,0:T(8,128)(2,1)S(1)} %copy-done.1), channel_id=1, source_target_pairs={{0,4},{4,0},{1,5},{5,1},{2,6},{6,2},{3,7},{7,3},{8,12},{12,8},{9,1... | collective-permute-start | bytes 589832 | tf_op jit(solution)/shard_map/ppermute | solution.py:668
  52.2 1.7 %collective-permute-start.1 = (bf16[128,640]{1,0:T(8,128)(2,1)S(1)}, bf16[128,640]{1,0:T(8,128)(2,1)S(1)}, u32[]{:S(2)}, u32[]{:S(2)}) collective-permute-start(bf16[128,640]{1,0:T(8,128)(2,1)S(1)} %get-tuple-element.42), channel_id=1, source_target_pairs={{0,4},{4,0},{1,5},{5,1},{2,6},{6,2},{3,7},{7,3},{8,12},{12,8},{9,1... | collective-permute-start | bytes 491528 | tf_op jit(solution)/shard_map/ppermute | solution.py:668
  91.5 6.2 %copy-start = (bf16[128,72,128]{2,1,0:T(8,128)(2,1)}, bf16[128,72,128]{2,1,0:T(8,128)(2,1)S(1)}, u32[]{:S(2)}) copy-start(bf16[128,72,128]{2,1,0:T(8,128)(2,1)S(1)} %all_to_all.21.bundle) | copy-start | bytes 7077892
  92.8 21.0 %all-to-all-start.3 = ((bf16[64,56,128]{2,1,0:T(8,128)(2,1)}), bf16[64,56,128]{2,1,0:T(8,128)(2,1)S(1)}, u32[]{:S(2)}, u32[]{:S(2)}) async-start(bf16[64,56,128]{2,1,0:T(8,128)(2,1)} %sum_parts.1), calls=%async_computation.3 | async-start | bytes 1835008 | tf_op jit(solution)/shard_map/all_to_all | solution.py:665
  113.8 4.0 %collective-permute-start.2 = (bf16[64,56,128]{2,1,0:T(8,128)(2,1)S(1)}, bf16[64,56,128]{2,1,0:T(8,128)(2,1)S(1)}, u32[]{:S(2)}, u32[]{:S(2)}) collective-permute-start(bf16[64,56,128]{2,1,0:T(8,128)(2,1)S(1)} %after.1), channel_id=1, source_target_pairs={{0,4},{4,0},{1,5},{5,1},{2,6},{6,2},{3,7},{7,3},{8,12},{12,8},{9,1... | collective-permute-start | bytes 2752520 | tf_op jit(solution)/shard_map/ppermute | solution.py:668
